TPU v7x, 32 devices: a whole 2x2x4 slice. The times are simulated.
32 devices in a mesh: expert: 4 (over z), shard: 8 (over y, x, core).
Axes of the slice: x: 2, y: 2, z: 4, core: 2. Of those that a mesh axis runs over, the one named last changes fastest.
Arguments:
- tokens: bfloat16 [32768, 768], P(('expert', 'shard')), may hold values from -6 to 6
- cotangent: bfloat16 [32768, 768], P(('expert', 'shard')), may hold values from -6 to 6
- prev_logits: float32 [32768, 12], P(('expert', 'shard')), may hold values from -3 to 3
- routes: int32 [32768, 2], P(('expert', 'shard')), may hold values from 0 to 11, all different within a row
- priority: int32 [32, 2048], P(('expert', 'shard')), may hold values from 0 to 2047, each once within a row
- gain_mix: bfloat16 [768], P('shard'), may hold values from 0.5 to 1.5
- mix_qkv: bfloat16 [768, 2304], P('shard'), may hold values from -0.21875 to 0.21875
- mix_out: bfloat16 [768, 768], P('shard'), may hold values from -3.59375 to 3.59375
- gain_moe: bfloat16 [768], P('shard'), may hold values from 0.5 to 1.5
- router: bfloat16 [768, 12], P('shard'), may hold values from -0.109375 to 0.109375
- constants: bfloat16 [768, 2], P('shard'), may hold values from -6 to 6
- w_gate: bfloat16 [8, 768, 2048], P('expert', None, 'shard'), may hold values from -0.21875 to 0.21875
- w_up: bfloat16 [8, 768, 2048], P('expert', None, 'shard'), may hold values from -0.21875 to 0.21875
- w_down: bfloat16 [8, 768, 2048], P('expert', None, 'shard'), may hold values from -0.125 to 0.125
Outputs:
- block_out: bfloat16 [32768, 768], P(('expert', 'shard'))
- token_grad: float32 [32768, 768], P(('expert', 'shard'))
- logit_grad: float32 [32768, 12], P(('expert', 'shard'))
- grad_gain_mix: float32 [768], P('shard')
- grad_qkv: float32 [768, 2304], P('shard')
- grad_out: float32 [768, 768], P('shard')
- grad_gain_moe: float32 [768], P('shard')
- grad_router: float32 [768, 12], P('shard')
- grad_constants: float32 [768, 2], P('shard')
- grad_gate: float32 [8, 768, 2048], P('expert', None, 'shard')
- grad_up: float32 [8, 768, 2048], P('expert', None, 'shard')
- grad_down: float32 [8, 768, 2048], P('expert', None, 'shard')
Inputs may be any that keep to these rules, and one draw needn't show every extreme that they name: `routes`: each row names two different experts, and every expert is named by some row. `priority`: each row is a permutation: the claim order of the 2048 pairs of one sequence, pair 2 t + j being the sequence's token t with its j-th route.
All inputs are finite; a program needn't handle non-finite values.
Results may differ from a plain program's by a relative error of at most 0.03.
Values may be sent and summed in bfloat16 or wider, within the bound.
No kernel may reach another device: no remote copies, remote signals or barrier semaphores. Data moves between devices by JAX's collectives and lax.ppermute only.
A program may use at most 256 MiB of HBM per device.

v0:
```python
import jax
import jax.numpy as jnp
from jax import lax
from jax.sharding import PartitionSpec as P

HEADS = 12
HEAD = 64
EXPERTS = 8
ZEROS = 4
BLOCK = 256
CAP = 216


epsilon = 1e-06
highest = lax.Precision.HIGHEST


def rope_tables(length, head_size):
    half_size = head_size // 2
    frequencies = 10000.0 ** (-(jnp.arange(half_size).astype(jnp.float32) * 2.0 / head_size))
    angles = jnp.arange(length).astype(jnp.float32)[:, None] * frequencies[None, :]
    return (jnp.cos(angles), jnp.sin(angles))


def rotate(values, cosine, sine_table):
    half_size = values.shape[-1] // 2
    first_half = values[..., :half_size]
    second = values[..., half_size:]
    cos_b = cosine[:, None, :]
    sin_b = sine_table[:, None, :]
    return jnp.concatenate(
        [first_half * cos_b - second * sin_b, second * cos_b + first_half * sin_b], axis=-1
    )


def unrotate(grad_rot, cosine, sine_table):
    half_size = grad_rot.shape[-1] // 2
    first_grad = grad_rot[..., :half_size]
    second_grad = grad_rot[..., half_size:]
    cos_b = cosine[:, None, :]
    sin_b = sine_table[:, None, :]
    return jnp.concatenate(
        [first_grad * cos_b + second_grad * sin_b, second_grad * cos_b - first_grad * sin_b],
        axis=-1,
    )


def norm_forward(values, norm_gain):
    inverse = lax.rsqrt(jnp.mean(values * values, axis=-1, keepdims=True) + epsilon)
    return (inverse, (values * inverse * norm_gain).astype(jnp.bfloat16))


def norm_backward(values, inverse, norm_gain, grad_normed):
    scaled = grad_normed * norm_gain
    grad_values = inverse * scaled - values * inverse**3 * jnp.mean(
        scaled * values, axis=-1, keepdims=True
    )
    grad_gain = jnp.sum(grad_normed * values * inverse, axis=0)
    return (grad_values, grad_gain)


def placement(route_pairs, pair_order):
    pair_count = route_pairs.shape[0]
    counting = jnp.arange(pair_count)
    ordered = jnp.zeros((pair_count,), jnp.int32).at[pair_order].set(counting)
    sorted_ids = route_pairs[ordered]
    onehot_ids = (sorted_ids[:, None] == jnp.arange(EXPERTS + ZEROS)[None, :]).astype(jnp.int32)
    earlier = jnp.cumsum(onehot_ids, axis=0) - onehot_ids
    rank_sorted = jnp.sum(earlier * onehot_ids, axis=1)
    slot_index = rank_sorted[pair_order]
    kept_pair = (route_pairs < EXPERTS) & (slot_index < CAP)
    target = jnp.where(kept_pair, route_pairs * CAP + slot_index, EXPERTS * CAP)
    source = jnp.full((EXPERTS * CAP + 1,), pair_count, jnp.int32).at[target].set(counting)
    return (target, source[: EXPERTS * CAP])


def block_scores(query_block, keys_rot, block_start):
    rows_block = query_block.shape[0]
    score_scale = query_block.shape[-1] ** (-0.5)
    scores = (
        jnp.einsum("qhd,khd->hqk", query_block, keys_rot, preferred_element_type=jnp.float32)
        * score_scale
    )
    query_pos = (block_start + jnp.arange(rows_block)) // BLOCK
    key_pos = jnp.arange(keys_rot.shape[0]) // BLOCK
    allowed = key_pos[None, :] <= query_pos[:, None]
    return jnp.where(allowed[None], scores, -1e30)


def attention_forward(queries, keys_rot, values):
    length = queries.shape[0]
    block_rows = min(512, length)
    count_blocks = length // block_rows
    query_blocks = queries.reshape(count_blocks, block_rows, queries.shape[1], queries.shape[2])
    starts = jnp.arange(count_blocks) * block_rows

    def one_block(operands):
        query_block, block_start = operands
        scores = block_scores(query_block, keys_rot, block_start)
        top_score = jnp.max(scores, axis=-1, keepdims=True)
        exp_scores = jnp.exp(scores - top_score)
        row_total = jnp.sum(exp_scores, axis=-1, keepdims=True)
        probabilities = (exp_scores / row_total).astype(jnp.bfloat16)
        result = jnp.einsum(
            "hqk,khd->qhd", probabilities, values, preferred_element_type=jnp.float32
        )
        return (result, (top_score + jnp.log(row_total))[..., 0])

    attended, log_totals = lax.map(one_block, (query_blocks, starts))
    return (attended.reshape(queries.shape), log_totals)


def attention_backward(queries, keys_rot, values, log_totals, grad_attended):
    length = queries.shape[0]
    block_rows = min(512, length)
    count_blocks = length // block_rows
    score_scale = queries.shape[-1] ** (-0.5)
    query_blocks = queries.reshape(count_blocks, block_rows, queries.shape[1], queries.shape[2])
    grad_blocks = grad_attended.reshape(
        count_blocks, block_rows, queries.shape[1], queries.shape[2]
    )
    starts = jnp.arange(count_blocks) * block_rows

    def one_block(carried, operands):
        grad_keys, grad_values = carried
        query_block, grad_block, log_block, block_start = operands
        scores = block_scores(query_block, keys_rot, block_start)
        probabilities = jnp.exp(scores - log_block[..., None])
        grad_probs = jnp.einsum(
            "qhd,khd->hqk", grad_block, values, preferred_element_type=jnp.float32
        )
        inner_sum = jnp.sum(probabilities * grad_probs, axis=-1, keepdims=True)
        grad_scores = (probabilities * (grad_probs - inner_sum)).astype(jnp.bfloat16)
        grad_query = (
            jnp.einsum("hqk,khd->qhd", grad_scores, keys_rot, preferred_element_type=jnp.float32)
            * score_scale
        )
        grad_keys = (
            grad_keys
            + jnp.einsum(
                "hqk,qhd->khd", grad_scores, query_block, preferred_element_type=jnp.float32
            )
            * score_scale
        )
        grad_values = grad_values + jnp.einsum(
            "hqk,qhd->khd",
            probabilities.astype(jnp.bfloat16),
            grad_block,
            preferred_element_type=jnp.float32,
        )
        return ((grad_keys, grad_values), grad_query)

    zero_keys = jnp.zeros(keys_rot.shape, jnp.float32)
    carried, grad_query_blocks = lax.scan(
        one_block, (zero_keys, zero_keys), (query_blocks, grad_blocks, log_totals, starts)
    )
    return (grad_query_blocks.reshape(queries.shape), carried[0], carried[1])


def expert_forward(incoming, weights_full):
    gate_w, up_w, down_w = weights_full
    gate_pre = jnp.einsum("erd,edf->erf", incoming, gate_w, preferred_element_type=jnp.float32)
    up_pre = jnp.einsum("erd,edf->erf", incoming, up_w, preferred_element_type=jnp.float32)
    hidden = (gate_pre * jax.nn.sigmoid(gate_pre) * up_pre).astype(jnp.bfloat16)
    return (gate_pre, up_pre, hidden)


def local(
    tokens,
    cotangent,
    prev_logits,
    routes,
    priority,
    gain_mix,
    mix_qkv,
    mix_out,
    gain_moe,
    router,
    constants,
    w_gate,
    w_up,
    w_down,
):
    length = tokens.shape[0]
    model_width = tokens.shape[1]
    gathered = (
        lax.all_gather(gain_mix, "shard", axis=0, tiled=True),
        lax.all_gather(mix_qkv, "shard", axis=0, tiled=True),
        lax.all_gather(mix_out, "shard", axis=0, tiled=True),
        lax.all_gather(gain_moe, "shard", axis=0, tiled=True),
        lax.all_gather(router, "shard", axis=0, tiled=True),
        lax.all_gather(constants, "shard", axis=0, tiled=True),
    )
    gain_one = gathered[0].astype(jnp.float32)
    qkv_full = gathered[1]
    out_full = gathered[2]
    gain_two = gathered[3].astype(jnp.float32)
    router_wide = gathered[4].astype(jnp.float32)
    const_wide = gathered[5].astype(jnp.float32)
    cosine, sine_table = rope_tables(length, HEAD)
    inputs = tokens.astype(jnp.float32)
    inverse_one, normed_one = norm_forward(inputs, gain_one)
    projected = jnp.dot(normed_one, qkv_full, preferred_element_type=jnp.float32).astype(
        jnp.bfloat16
    )
    projected = projected.reshape(length, 3, HEADS, HEAD)
    queries = rotate(projected[:, 0].astype(jnp.float32), cosine, sine_table).astype(jnp.bfloat16)
    keys_rot = rotate(projected[:, 1].astype(jnp.float32), cosine, sine_table).astype(jnp.bfloat16)
    values = projected[:, 2]
    attended, log_totals = attention_forward(queries, keys_rot, values)
    attended_low = attended.reshape(length, model_width).astype(jnp.bfloat16)
    residual = inputs + jnp.dot(attended_low, out_full, preferred_element_type=jnp.float32)
    inverse_two, normed_two = norm_forward(residual, gain_two)
    normed_wide = normed_two.astype(jnp.float32)
    logits = jnp.dot(normed_wide, router_wide, precision=highest) + prev_logits
    chosen = jnp.take_along_axis(logits, routes, axis=1)
    gate_probs = jax.nn.softmax(chosen, axis=1)
    targets, sources = placement(routes.reshape(-1), priority[0])
    token_index = jnp.where(sources < 2 * length, sources // 2, length)
    padded_normed = jnp.concatenate([normed_two, jnp.zeros((1, model_width), jnp.bfloat16)], axis=0)
    outgoing = padded_normed[token_index].reshape(EXPERTS, CAP, model_width)
    incoming = lax.all_to_all(outgoing, "expert", split_axis=0, concat_axis=1, tiled=True)
    expert_full = (
        lax.all_gather(w_gate, "shard", axis=2, tiled=True),
        lax.all_gather(w_up, "shard", axis=2, tiled=True),
        lax.all_gather(w_down, "shard", axis=2, tiled=True),
    )
    gate_pre, up_pre, hidden = expert_forward(incoming, expert_full)
    produced = jnp.einsum(
        "erf,edf->erd", hidden, expert_full[2], preferred_element_type=jnp.float32
    ).astype(jnp.bfloat16)
    returned = lax.all_to_all(produced, "expert", split_axis=1, concat_axis=0, tiled=True)
    padded_returned = jnp.concatenate(
        [returned.reshape(EXPERTS * CAP, model_width), jnp.zeros((1, model_width), jnp.bfloat16)],
        axis=0,
    )
    ffn_values = padded_returned[targets].astype(jnp.float32).reshape(length, 2, model_width)
    id_cube = routes[:, :, None]
    branch = ffn_values + jnp.where(id_cube == EXPERTS + 1, normed_wide[:, None, :], 0.0)
    branch = branch + jnp.where(id_cube == EXPERTS + 2, const_wide[:, 0][None, None, :], 0.0)
    branch = branch + jnp.where(id_cube == EXPERTS + 3, const_wide[:, 1][None, None, :], 0.0)
    block_out = residual + jnp.sum(gate_probs[:, :, None] * branch, axis=1)
    back_mix = (
        lax.all_gather(gain_mix, "shard", axis=0, tiled=True),
        lax.all_gather(mix_qkv, "shard", axis=0, tiled=True),
        lax.all_gather(mix_out, "shard", axis=0, tiled=True),
        lax.all_gather(gain_moe, "shard", axis=0, tiled=True),
        lax.all_gather(router, "shard", axis=0, tiled=True),
        lax.all_gather(constants, "shard", axis=0, tiled=True),
    )
    back_expert = (
        lax.all_gather(w_gate, "shard", axis=2, tiled=True),
        lax.all_gather(w_up, "shard", axis=2, tiled=True),
        lax.all_gather(w_down, "shard", axis=2, tiled=True),
    )
    gate_back, up_back, hidden_back = expert_forward(incoming, back_expert)
    gain_one_back = back_mix[0].astype(jnp.float32)
    qkv_back = back_mix[1]
    out_back = back_mix[2]
    gain_two_back = back_mix[3].astype(jnp.float32)
    router_back = back_mix[4].astype(jnp.float32)
    grad_rows_out = cotangent.astype(jnp.float32)
    grad_gates = jnp.sum(grad_rows_out[:, None, :] * branch, axis=2)
    mean_grad = jnp.sum(gate_probs * grad_gates, axis=1, keepdims=True)
    grad_chosen = gate_probs * (grad_gates - mean_grad)
    expert_ids = jnp.arange(EXPERTS + ZEROS)
    grad_logits = jnp.sum(
        jnp.where(routes[:, :, None] == expert_ids[None, None, :], grad_chosen[:, :, None], 0.0),
        axis=1,
    )
    grad_router = jnp.dot(normed_wide.T, grad_logits, precision=highest)
    grad_normed = jnp.dot(grad_logits, router_back.T, precision=highest)
    weighted = gate_probs[:, :, None] * grad_rows_out[:, None, :]
    grad_normed = grad_normed + jnp.sum(jnp.where(id_cube == EXPERTS + 1, weighted, 0.0), axis=1)
    const_weights = jnp.stack(
        [
            jnp.sum(jnp.where(routes == EXPERTS + 2, gate_probs, 0.0), axis=1),
            jnp.sum(jnp.where(routes == EXPERTS + 3, gate_probs, 0.0), axis=1),
        ],
        axis=1,
    )
    grad_const = jnp.dot(grad_rows_out.T, const_weights, precision=highest)
    pair_grads = weighted.reshape(2 * length, model_width).astype(jnp.bfloat16)
    padded_pairs = jnp.concatenate([pair_grads, jnp.zeros((1, model_width), jnp.bfloat16)], axis=0)
    pair_index = jnp.where(sources < 2 * length, sources, 2 * length)
    grad_outgoing = padded_pairs[pair_index].reshape(EXPERTS, CAP, model_width)
    grad_incoming = lax.all_to_all(grad_outgoing, "expert", split_axis=0, concat_axis=1, tiled=True)
    gate_w, up_w, down_w = back_expert
    grad_hidden = jnp.einsum(
        "erd,edf->erf", grad_incoming, down_w, preferred_element_type=jnp.float32
    )
    sigmoid_gate = jax.nn.sigmoid(gate_back)
    grad_gate_pre = (
        grad_hidden * up_back * sigmoid_gate * (1.0 + gate_back * (1.0 - sigmoid_gate))
    ).astype(jnp.bfloat16)
    grad_up_pre = (grad_hidden * gate_back * sigmoid_gate).astype(jnp.bfloat16)
    grad_rows = jnp.einsum(
        "erf,edf->erd", grad_gate_pre, gate_w, preferred_element_type=jnp.float32
    )
    grad_rows = (
        grad_rows
        + jnp.einsum("erf,edf->erd", grad_up_pre, up_w, preferred_element_type=jnp.float32)
    ).astype(jnp.bfloat16)
    grad_back = lax.all_to_all(grad_rows, "expert", split_axis=1, concat_axis=0, tiled=True)
    ff_here = w_gate.shape[2]
    experts_here = w_gate.shape[0]
    term_gate = jnp.einsum(
        "erf,erd->fed", grad_gate_pre, incoming, preferred_element_type=jnp.float32
    )
    term_up = jnp.einsum("erf,erd->fed", grad_up_pre, incoming, preferred_element_type=jnp.float32)
    term_down = jnp.einsum(
        "erf,erd->fed", hidden_back, grad_incoming, preferred_element_type=jnp.float32
    )
    summed = lax.psum_scatter(
        jnp.stack([term_gate, term_up, term_down], axis=2)
        .reshape(ff_here * lax.axis_size("shard"), -1)
        .astype(jnp.bfloat16),
        "shard",
        scatter_dimension=0,
        tiled=True,
    ).astype(jnp.float32)
    summed = summed.reshape(ff_here, experts_here, 3, model_width)
    grad_gate = summed[:, :, 0, :].transpose(1, 2, 0)
    grad_up = summed[:, :, 1, :].transpose(1, 2, 0)
    grad_down = summed[:, :, 2, :].transpose(1, 2, 0)
    padded_back = jnp.concatenate(
        [grad_back.reshape(EXPERTS * CAP, model_width), jnp.zeros((1, model_width), jnp.bfloat16)],
        axis=0,
    )
    grad_normed = grad_normed + jnp.sum(
        padded_back[targets].astype(jnp.float32).reshape(length, 2, model_width), axis=1
    )
    grad_residual_norm, grad_gain_two = norm_backward(
        residual, inverse_two, gain_two_back, grad_normed
    )
    grad_residual = grad_rows_out + grad_residual_norm
    grad_attn_low = grad_residual.astype(jnp.bfloat16)
    grad_out_w = jnp.dot(attended_low.T, grad_attn_low, preferred_element_type=jnp.float32)
    grad_attended = jnp.dot(grad_attn_low, out_back.T, preferred_element_type=jnp.float32).astype(
        jnp.bfloat16
    )
    grad_attended = grad_attended.reshape(length, HEADS, HEAD)
    grad_queries, grad_keys, grad_values = attention_backward(
        queries, keys_rot, values, log_totals, grad_attended
    )
    grad_proj = jnp.stack(
        [
            unrotate(grad_queries.astype(jnp.bfloat16), cosine, sine_table),
            unrotate(grad_keys.astype(jnp.bfloat16), cosine, sine_table),
            grad_values.astype(jnp.bfloat16).astype(jnp.float32),
        ],
        axis=1,
    )
    grad_proj = grad_proj.reshape(length, 3 * model_width).astype(jnp.bfloat16)
    grad_qkv_w = jnp.dot(normed_one.T, grad_proj, preferred_element_type=jnp.float32)
    grad_normed_one = jnp.dot(grad_proj, qkv_back.T, preferred_element_type=jnp.float32)
    grad_inputs_norm, grad_gain_one = norm_backward(
        inputs, inverse_one, gain_one_back, grad_normed_one
    )
    token_grad = grad_residual + grad_inputs_norm
    shard_sums = (
        lax.psum_scatter(
            grad_gain_one.astype(jnp.bfloat16), "shard", scatter_dimension=0, tiled=True
        ).astype(jnp.float32),
        lax.psum_scatter(
            grad_qkv_w.astype(jnp.bfloat16), "shard", scatter_dimension=0, tiled=True
        ).astype(jnp.float32),
        lax.psum_scatter(
            grad_out_w.astype(jnp.bfloat16), "shard", scatter_dimension=0, tiled=True
        ).astype(jnp.float32),
        lax.psum_scatter(
            grad_gain_two.astype(jnp.bfloat16), "shard", scatter_dimension=0, tiled=True
        ).astype(jnp.float32),
        lax.psum_scatter(
            grad_router.astype(jnp.bfloat16), "shard", scatter_dimension=0, tiled=True
        ).astype(jnp.float32),
        lax.psum_scatter(
            grad_const.astype(jnp.bfloat16), "shard", scatter_dimension=0, tiled=True
        ).astype(jnp.float32),
    )
    totals = (
        lax.psum(shard_sums[0].astype(jnp.bfloat16), "expert").astype(jnp.float32),
        lax.psum(shard_sums[1].astype(jnp.bfloat16), "expert").astype(jnp.float32),
        lax.psum(shard_sums[2].astype(jnp.bfloat16), "expert").astype(jnp.float32),
        lax.psum(shard_sums[3].astype(jnp.bfloat16), "expert").astype(jnp.float32),
        lax.psum(shard_sums[4].astype(jnp.bfloat16), "expert").astype(jnp.float32),
        lax.psum(shard_sums[5].astype(jnp.bfloat16), "expert").astype(jnp.float32),
    )
    return (
        block_out.astype(jnp.bfloat16),
        token_grad,
        grad_logits,
        totals[0],
        totals[1],
        totals[2],
        totals[3],
        totals[4],
        totals[5],
        grad_gate,
        grad_up,
        grad_down,
    )


def solution(mesh):
    in_specs = (
        P(("expert", "shard"), None),
        P(("expert", "shard"), None),
        P(("expert", "shard"), None),
        P(("expert", "shard"), None),
        P(("expert", "shard"), None),
        P("shard"),
        P("shard", None),
        P("shard", None),
        P("shard"),
        P("shard", None),
        P("shard", None),
        P("expert", None, "shard"),
        P("expert", None, "shard"),
        P("expert", None, "shard"),
    )
    out_specs = (
        P(("expert", "shard"), None),
        P(("expert", "shard"), None),
        P(("expert", "shard"), None),
        P("shard"),
        P("shard", None),
        P("shard", None),
        P("shard"),
        P("shard", None),
        P("shard", None),
        P("expert", None, "shard"),
        P("expert", None, "shard"),
        P("expert", None, "shard"),
    )
    return jax.shard_map(local, mesh=mesh, in_specs=in_specs, out_specs=out_specs, check_vma=False)
```

profile of v0, /device:TPU:1, one launch (start us, length us, event | category | flops | bytes accessed | tf_op | source)
XLA Modules:
  0.0 1137.9 jit_solution(9035368770253987012)
XLA Ops:
  15.5 12.8 %all-reduce.9 = (bf16[768]{0:T(1024)(128)(2,1)S(1)}, bf16[768]{0:T(1024)(128)(2,1)S(1)}) all-reduce(bf16[768]{0:T(1024)(128)(2,1)S(1)} %dynamic-update-slice, bf16[768]{0:T(1024)(128)(2,1)S(1)} %dynamic-update-slice.1), channel_id=1, replica_groups=mesh['expert'=4,'shard'=8] {'shard'}, use_global_device_ids=true, to_apply=%add.4 | all-reduce | flops 1536 | bytes 6144
  65.3 11.8 %gather_fusion = s32[2048]{0:T(1024)S(1)} fusion(s32[2048]{0:T(1024)S(1)} %reshape.559, s32[2048]{0:T(1024)S(1)} %fusion.72), kind=kCustom, calls=%fused_computation | custom fusion | bytes 24576 | tf_op jit(solution)/shard_map/gather | solution.py:66
  82.5 11.8 %gather_fusion.1 = s32[2048]{0:T(1024)S(1)} fusion(s32[2048]{0:T(1024)S(1)} %fusion.68, s32[2048]{0:T(1024)S(1)} %broadcast_clamp_fusion.1), kind=kCustom, calls=%fused_computation.1 | custom fusion | bytes 24576 | tf_op jit(solution)/shard_map/gather | solution.py:70
  126.4 77.0 %while.33 = (s32[]{:T(128)}, bf16[2,512,12,64]{1,3,2,0:T(8,128)(2,1)}, f32[2,12,512]{2,1,0:T(8,128)S(1)}, s32[2]{0:T(128)S(1)}, bf16[2,512,12,64]{1,3,2,0:T(8,12...) while((s32[]{:T(128)}, bf16[2,512,12,64]{1,3,2,0:T(8,128)(2,1)}, ...), condition=%wide.region_4.5_spmd, body=%wide.region_1.4_spmd.sunk | while | flops 1686644736 | bytes 183997584 | solution.py:109
  128.1 12.0 %fusion.146 = (f32[12,512]{1,0:T(8,128)S(1)}, f32[12,512,1024]{2,1,0:T(8,128)}) fusion(pred[512,1024]{1,0:T(8,128)(4,1)S(1)} %broadcast_compare_fusion.8, bf16[1024,12,64]{0,2,1:T(8,128)(2,1)S(1)} %get-tuple-element.619, bf16[2,512,12,64]{1,3,2,0:T(8,128)(2,1)} %get-tuple-element.618, s32[]{:T(128)} %get-tuple-element.606), kind=kOutput, calls=%fused_computation.12.clone.1 | convolution fusion | flops 824174592 | bytes 28074496 | tf_op jit(solution)/shard_map/while/body/eval_jaxpr/qhd,khd->hqk/dot_general | solution.py:81
  140.0 13.1 %fusion.147 = f32[12,512]{1,0:T(8,128)S(1)} fusion(f32[12,512,1024]{2,1,0:T(8,128)} %get-tuple-element.584, f32[12,512]{1,0:T(8,128)S(1)} %get-tuple-element.585, pred[512,1024]{1,0:T(8,128)(4,1)S(1)} %broadcast_compare_fusion.8), kind=kLoop, calls=%fused_computation.13.clone.1 | loop fusion | flops 25159680 | bytes 25739264 | tf_op jit(solution)/shard_map/while/body/eval_jaxpr/reduce_sum | solution.py:102
  166.6 12.6 %fusion.146 = (f32[12,512]{1,0:T(8,128)S(1)}, f32[12,512,1024]{2,1,0:T(8,128)}) fusion(pred[512,1024]{1,0:T(8,128)(4,1)S(1)} %broadcast_compare_fusion.8, bf16[1024,12,64]{0,2,1:T(8,128)(2,1)S(1)} %get-tuple-element.619, bf16[2,512,12,64]{1,3,2,0:T(8,128)(2,1)} %get-tuple-element.618, s32[]{:T(128)} %get-tuple-element.606), kind=kOutput, calls=%fused_computation.12.clone.1 | convolution fusion | flops 824174592 | bytes 28074496 | tf_op jit(solution)/shard_map/while/body/eval_jaxpr/qhd,khd->hqk/dot_general | solution.py:81
  179.2 12.5 %fusion.147 = f32[12,512]{1,0:T(8,128)S(1)} fusion(f32[12,512,1024]{2,1,0:T(8,128)} %get-tuple-element.584, f32[12,512]{1,0:T(8,128)S(1)} %get-tuple-element.585, pred[512,1024]{1,0:T(8,128)(4,1)S(1)} %broadcast_compare_fusion.8), kind=kLoop, calls=%fused_computation.13.clone.1 | loop fusion | flops 25159680 | bytes 25739264 | tf_op jit(solution)/shard_map/while/body/eval_jaxpr/reduce_sum | solution.py:102
  217.6 16.8 %gather_fusion.6 = f32[2048]{0:T(1024)S(1)} fusion(f32[1024,12]{0,1:T(8,128)S(1)} %convolution_add_fusion, s32[2048]{0:T(1024)S(1)} %copy-done.4), kind=kCustom, calls=%fused_computation.6 | custom fusion | bytes 32768 | tf_op jit(solution)/shard_map/jit(take_along_axis)/gather | solution.py:216
  258.7 53.3 %all-to-all-done.2 = bf16[8,216,768]{2,1,0:T(8,128)(2,1)} async-done(((bf16[8,216,768]{2,1,0:T(8,128)(2,1)}), bf16[8,216,768]{2,1,0:T(8,128)(2,1)}, u32[]{:S(2)}, u32[]{:S(2)}) %all-to-all-start.2) | async-done | bytes 2654240 | tf_op jit(solution)/shard_map/all_to_all | solution.py:287
  319.2 56.2 %all-to-all-done = bf16[8,216,768]{2,1,0:T(8,128)(2,1)S(1)} async-done(((bf16[8,216,768]{2,1,0:T(8,128)(2,1)}), bf16[8,216,768]{2,1,0:T(8,128)(2,1)S(1)}, u32[]{:S(2)}, u32[]{:S(2)}) %all-to-all-start) | async-done | bytes 2654240 | tf_op jit(solution)/shard_map/all_to_all | solution.py:222
  377.2 11.6 %fusion.87 = f32[2,864,2048]{2,1,0:T(8,128)} fusion(bf16[2,864,768]{2,1,0:T(8,128)(2,1)} %bitcast.245, bf16[2,768,2048]{2,1,0:T(8,128)(2,1)} %all-gather.12.cloned.1.call-done), kind=kOutput, calls=%fused_computation.236 | convolution fusion | flops 5435817984 | bytes 23101440 | tf_op jit(solution)/shard_map/erd,edf->erf/dot_general | solution.py:162
  388.8 11.7 %fusion.88 = f32[2,864,2048]{2,1,0:T(8,128)} fusion(bf16[2,864,768]{2,1,0:T(8,128)(2,1)S(1)} %bitcast.247, bf16[2,768,2048]{2,1,0:T(8,128)(2,1)} %all-gather.14.cloned.1.call-done), kind=kOutput, calls=%fused_computation.237 | convolution fusion | flops 5435817984 | bytes 23101440 | tf_op jit(solution)/shard_map/erd,edf->erf/dot_general | solution.py:163
  400.6 25.1 %multiply_convert_fusion.1 = (bf16[2,864,2048]{2,1,0:T(8,128)(2,1)}, bf16[2,864,2048]{2,1,0:T(8,128)(2,1)}, bf16[2,864,2048]{2,1,0:T(8,128)(2,1)}) fusion(f32[2,864,2048]{2,1,0:T(8,128)} %fusion.87, f32[2,864,2048]{2,1,0:T(8,128)} %fusion.88, bf16[2,864,768]{2,1,0:T(8,128)(2,1)} %bitcast.249, bf16[2,768,2048]{2,1,0:T(8,128)(2,1)} %all-gather.16.cloned.1.call-done), kind=kOutput, calls=%fused_computation.84 | convolution fusion | flops 5492441088 | bytes 58490880 | tf_op jit(solution)/shard_map/erd,edf->erf/dot_general | solution.py:289
  479.9 22.9 %all-to-all-done.1 = bf16[2,864,768]{2,0,1:T(2,128)(2,1)} async-done(((bf16[2,864,768]{2,0,1:T(2,128)(2,1)}), bf16[2,864,768]{2,0,1:T(2,128)(2,1)}, u32[]{:S(2)}, u32[]{:S(2)}) %all-to-all-start.1) | async-done | bytes 2654240 | tf_op jit(solution)/shard_map/all_to_all | solution.py:232
  528.0 33.5 %multiply_reduce_fusion.1 = (f32[1024,2]{1,0:T(8,128)}, f32[1024,768]{1,0:T(8,128)}, f32[1024,768]{1,0:T(8,128)}) fusion(f32[1024,768]{1,0:T(8,128)} %convert_element_type.312, f32[1024,2]{1,0:T(8,128)} %copy-done.21, pred[1024,2]{1,0:T(8,128)(4,1)S(1)} %copy.174, f32[768]{0:T(1024)} %get-tuple-element.390, pred[1024,2]{1,0:T(8,128)(4,1)S(1)} %copy.177, ...), kind=kLoop, calls=%fused_computation.99 | loop fusion | flops 18872320 | bytes 18903040 | tf_op jit(solution)/shard_map/reduce_sum | solution.py:263
  587.1 12.1 %reduce_sum.179 = f32[1024,768]{1,0:T(8,128)} reduce(f32[1024,2,768]{2,1,0:T(2,128)} %reshape.570, f32[]{:T(128)} %constant.232.clone.1), dimensions={1}, to_apply=%region_18.19 | reduce | flops 786432 | bytes 9437188 | tf_op jit(solution)/shard_map/reduce_sum | solution.py:330
  619.3 170.7 %while.34 = (s32[]{:T(128)}, f32[1024,12,64]{0,2,1:T(8,128)}, f32[1024,12,64]{0,2,1:T(8,128)}, bf16[2,512,12,64]{1,3,2,0:T(8,128)(2,1)}, bf16[2,512,12,64]{1,3,2...) while((s32[]{:T(128)}, f32[1024,12,64]{0,2,1:T(8,128)}, ...), condition=%wide.region_22.23_spmd.clone, body=%wide.region_20.22_spmd.clone.sunk | while | flops 4125763584 | bytes 213047968 | solution.py:154
  632.6 18.1 %multiply_reduce_fusion.8 = (f32[12,512]{1,0:T(8,128)S(1)}, f32[12,512,1024]{2,1,0:T(8,128)}) fusion(f32[12,512,1024]{2,1,0:T(8,128)} %fusion.157, f32[12,512]{1,0:T(8,128)S(1)} %dynamic-slice_bitcast_fusion.2, pred[512,1024]{1,0:T(8,128)(4,1)S(1)} %broadcast_compare_fusion.9, bf16[1024,12,64]{0,2,1:T(8,128)(2,1)} %get-tuple-element.655, ...), kind=kOutput, calls=%fused_computation.41.clone.1 | convolution fusion | flops 836757504 | bytes 53264896 | tf_op jit(solution)/shard_map/while/body/eval_jaxpr/qhd,khd->hqk/dot_general | solution.py:129
  650.8 21.2 %multiply_convert_fusion.8 = bf16[12,512,1024]{2,1,0:T(8,128)(2,1)} fusion(f32[12,512,1024]{2,1,0:T(8,128)} %get-tuple-element.596, f32[12,512,1024]{2,1,0:T(8,128)} %fusion.157, f32[12,512]{1,0:T(8,128)S(1)} %get-tuple-element.597, f32[12,512]{1,0:T(8,128)S(1)} %dynamic-slice_bitcast_fusion.2, pred[512,1024]{1,0:T(8,128)(4,1)S(1)} %broadcast_compare_fusion.9), kind=kLoop, calls=%fused_computation.40.clone.1 | loop fusion | flops 37748736 | bytes 63488000 | tf_op jit(solution)/shard_map/while/body/eval_jaxpr/convert_element_type | solution.py:133
  690.1 13.7 %bitcast_add_fusion.5 = f32[1024,12,64]{0,2,1:T(8,128)} fusion(f32[1024,12,64]{0,2,1:T(8,128)} %get-tuple-element.636, f32[12,512,1024]{2,1,0:T(8,128)} %fusion.157, f32[12,512]{1,0:T(8,128)S(1)} %dynamic-slice_bitcast_fusion.2, pred[512,1024]{1,0:T(8,128)(4,1)S(1)} %broadcast_compare_fusion.9, pred[]{:T(512)S(6)} %compare.41, ...), kind=kOutput, calls=%fused_computation.46.clone.1 | convolution fusion | flops 832045056 | bytes 32793088 | tf_op jit(solution)/shard_map/while/body/eval_jaxpr/hqk,qhd->khd/dot_general | solution.py:145
  716.7 18.1 %multiply_reduce_fusion.8 = (f32[12,512]{1,0:T(8,128)S(1)}, f32[12,512,1024]{2,1,0:T(8,128)}) fusion(f32[12,512,1024]{2,1,0:T(8,128)} %fusion.157, f32[12,512]{1,0:T(8,128)S(1)} %dynamic-slice_bitcast_fusion.2, pred[512,1024]{1,0:T(8,128)(4,1)S(1)} %broadcast_compare_fusion.9, bf16[1024,12,64]{0,2,1:T(8,128)(2,1)} %get-tuple-element.655, ...), kind=kOutput, calls=%fused_computation.41.clone.1 | convolution fusion | flops 836757504 | bytes 53264896 | tf_op jit(solution)/shard_map/while/body/eval_jaxpr/qhd,khd->hqk/dot_general | solution.py:129
  734.9 21.2 %multiply_convert_fusion.8 = bf16[12,512,1024]{2,1,0:T(8,128)(2,1)} fusion(f32[12,512,1024]{2,1,0:T(8,128)} %get-tuple-element.596, f32[12,512,1024]{2,1,0:T(8,128)} %fusion.157, f32[12,512]{1,0:T(8,128)S(1)} %get-tuple-element.597, f32[12,512]{1,0:T(8,128)S(1)} %dynamic-slice_bitcast_fusion.2, pred[512,1024]{1,0:T(8,128)(4,1)S(1)} %broadcast_compare_fusion.9), kind=kLoop, calls=%fused_computation.40.clone.1 | loop fusion | flops 37748736 | bytes 63488000 | tf_op jit(solution)/shard_map/while/body/eval_jaxpr/convert_element_type | solution.py:133
  775.1 14.6 %bitcast_add_fusion.5 = f32[1024,12,64]{0,2,1:T(8,128)} fusion(f32[1024,12,64]{0,2,1:T(8,128)} %get-tuple-element.636, f32[12,512,1024]{2,1,0:T(8,128)} %fusion.157, f32[12,512]{1,0:T(8,128)S(1)} %dynamic-slice_bitcast_fusion.2, pred[512,1024]{1,0:T(8,128)(4,1)S(1)} %broadcast_compare_fusion.9, pred[]{:T(512)S(6)} %compare.41, ...), kind=kOutput, calls=%fused_computation.46.clone.1 | convolution fusion | flops 832045056 | bytes 32793088 | tf_op jit(solution)/shard_map/while/body/eval_jaxpr/hqk,qhd->khd/dot_general | solution.py:145
  806.3 11.9 %convert_bitcast_fusion = bf16[2048,2,1,768]{0,3,1,2:T(8,128)(2,1)} fusion(bf16[2,864,768]{2,1,0:T(8,128)(2,1)S(1)} %bitcast.250, bf16[2,864,2048]{2,1,0:T(8,128)(2,1)} %get-tuple-element.445), kind=kOutput, calls=%fused_computation.94 | convolution fusion | flops 5438963712 | bytes 16023552 | tf_op jit(solution)/shard_map/erf,erd->fed/dot_general | solution.py:311
  818.3 11.9 %convert_bitcast_fusion.1 = bf16[2048,2,1,768]{0,3,1,2:T(8,128)(2,1)} fusion(bf16[2,864,768]{2,1,0:T(8,128)(2,1)S(1)} %bitcast.248, bf16[2,864,2048]{2,1,0:T(8,128)(2,1)} %get-tuple-element.443), kind=kOutput, calls=%fused_computation.95 | convolution fusion | flops 5438963712 | bytes 16023552 | tf_op jit(solution)/shard_map/erf,erd->fed/dot_general | solution.py:310
  833.7 12.0 %convert_bitcast_fusion.2 = bf16[2048,2,1,768]{0,3,1,2:T(8,128)(2,1)} fusion(bf16[2,864,768]{2,1,0:T(8,128)(2,1)} %bitcast.246, bf16[2,864,2048]{2,1,0:T(8,128)(2,1)} %get-tuple-element.444), kind=kOutput, calls=%fused_computation.96 | convolution fusion | flops 5438963712 | bytes 16023552 | tf_op jit(solution)/shard_map/erf,erd->fed/dot_general | solution.py:307
  845.8 34.9 %reduce-scatter.10.cloned.1.call-done = bf16[96,2304]{1,0:T(8,128)(2,1)} async-done(((bf16[768,2304]{1,0:T(8,128)(2,1)}), bf16[96,2304]{1,0:T(8,128)(2,1)}) %reduce-scatter.10.cloned.1.call-update) | async-done | bytes 442384 | tf_op jit(solution)/shard_map/reduce_scatter | solution.py:365
  907.6 11.8 %all-reduce.8 = (bf16[768]{0:T(1024)(128)(2,1)S(1)}, bf16[768]{0:T(1024)(128)(2,1)S(1)}) all-reduce(bf16[768]{0:T(1024)(128)(2,1)S(1)} %get-tuple-element.383, bf16[768]{0:T(1024)(128)(2,1)S(1)} %copy-done.68), channel_id=2, replica_groups=mesh['expert'=4,'shard'=8] {'shard'}, use_global_device_ids=true, to_apply=%region_25.26.clone | all-reduce | flops 1536 | bytes 6144
  924.4 30.3 %reduce-scatter.16.cloned.1.call-done = bf16[96,12]{1,0:T(8,128)(2,1)} async-done(((bf16[768,12]{1,0:T(8,128)(2,1)}), bf16[96,12]{1,0:T(8,128)(2,1)}) %reduce-scatter.16.cloned.1.call-update) | async-done | bytes 2320
  967.7 29.0 %all-reduce.14.cloned.1.call-done = (bf16[96,2304]{1,0:T(8,128)(2,1)}, bf16[96,768]{1,0:T(8,128)(2,1)}) async-done(((bf16[96,2304]{1,0:T(8,128)(2,1)}, bf16[96,768]{1,0:T(8,128)(2,1)}), (bf16[96,2304]{1,0:T(8,128)(2,1)}, bf16[96,768]{1,0:T(8,128)(2,1)})) %all-reduce.14.cloned.1.call-update) | async-done | bytes 589840 | tf_op jit(solution)/shard_map/psum | solution.py:383
  1000.4 126.4 %reduce-scatter.14.cloned.1.call-done = bf16[256,4608]{0,1:T(8,128)(2,1)} async-done(((bf16[2048,4608]{0,1:T(8,128)(2,1)}), bf16[256,4608]{0,1:T(8,128)(2,1)}) %reduce-scatter.14.cloned.1.call-update) | async-done | bytes 2359312 | tf_op jit(solution)/shard_map/reduce_scatter | solution.py:314
  (365 shorter events, 415.7 us)
Async XLA Ops:
  7.2 21.1 %copy-start.19 = (bf16[1024,768]{1,0:T(8,128)(2,1)S(1)}, bf16[1024,768]{1,0:T(8,128)(2,1)}, u32[]{:S(2)}) copy-start(bf16[1024,768]{1,0:T(8,128)(2,1)} %param.18) | copy-start | bytes 4718596
  7.2 22.6 %copy-start.70 = (bf16[96,12]{0,1:T(8,128)(2,1)S(1)}, bf16[96,12]{0,1:T(8,128)(2,1)}, u32[]{:S(2)}) copy-start(bf16[96,12]{0,1:T(8,128)(2,1)} %param.27) | copy-start | bytes 6916
  7.2 36.8 %copy-start.8 = (bf16[1024,768]{1,0:T(8,128)(2,1)S(1)}, bf16[1024,768]{1,0:T(8,128)(2,1)}, u32[]{:S(2)}) copy-start(bf16[1024,768]{1,0:T(8,128)(2,1)} %param.19) | copy-start | bytes 4718596
  7.3 96.8 %all-gather.8.cloned.1.call-start = ((), (), s32[]{:S(2)}) async-start(), calls=%async_computation.9 | async-start | bytes 3981312 | tf_op jit(solution)/shard_map/all_gather | solution.py:188
  8.0 201.3 %all-gather.10.cloned.1.call-start = ((), (), s32[]{:S(2)}) async-start(), calls=%async_computation.10 | async-start | bytes 1327104 | tf_op jit(solution)/shard_map/all_gather | solution.py:189
  8.7 368.5 %all-gather.12.cloned.1.call-start = ((), (), s32[]{:S(2)}) async-start(), calls=%async_computation.11 | async-start | bytes 7077888 | tf_op jit(solution)/shard_map/all_gather | solution.py:224
  9.5 379.4 %all-gather.14.cloned.1.call-start = ((), (), s32[]{:S(2)}) async-start(), calls=%async_computation.12 | async-start | bytes 7077888 | tf_op jit(solution)/shard_map/all_gather | solution.py:225
  10.1 390.5 %all-gather.16.cloned.1.call-start = ((), (), s32[]{:S(2)}) async-start(), calls=%async_computation.13 | async-start | bytes 7077888 | tf_op jit(solution)/shard_map/all_gather | solution.py:226
  28.3 75.8 %copy-start.63 = (f32[768]{0:T(1024)}, f32[768]{0:T(1024)S(1)}, u32[]{:S(2)}) copy-start(f32[768]{0:T(1024)S(1)} %convert_element_type.290) | copy-start | bytes 9220
  29.3 74.8 %copy-start.60 = (f32[1024]{0:T(1024)}, f32[1024]{0:T(1024)S(1)}, u32[]{:S(2)}) copy-start(f32[1024]{0:T(1024)S(1)} %get-tuple-element.475) | copy-start | bytes 12292
  48.3 16.7 %copy-start.27 = (s32[1024,2]{1,0:T(8,128)S(1)}, s32[1024,2]{1,0:T(8,128)}, u32[]{:S(2)}) copy-start(s32[1024,2]{1,0:T(8,128)} %copy.169) | copy-start | bytes 24580
  103.4 18.5 %copy-start.29 = (f32[1024,32]{0,1:T(8,128)}, f32[1024,32]{0,1:T(8,128)S(1)}, u32[]{:S(2)}) copy-start(f32[1024,32]{0,1:T(8,128)S(1)} %get-tuple-element.472) | copy-start | bytes 393220
  103.4 18.5 %copy-start.31 = (f32[1024,32]{0,1:T(8,128)}, f32[1024,32]{0,1:T(8,128)S(1)}, u32[]{:S(2)}) copy-start(f32[1024,32]{0,1:T(8,128)S(1)} %get-tuple-element.473) | copy-start | bytes 393220
  140.0 16.4 %copy-start = (f32[12,512,1024]{2,1,0:T(8,128)S(1)}, f32[12,512,1024]{2,1,0:T(8,128)}, u32[]{:S(2)}) copy-start(f32[12,512,1024]{2,1,0:T(8,128)} %get-tuple-element.584) | copy-start | bytes 75497472 | tf_op jit(solution)/shard_map/while
  217.6 17.5 %copy-start.38 = (s32[1024,2]{0,1:T(2,128)S(1)}, s32[1024,2]{0,1:T(2,128)}, u32[]{:S(2)}) copy-start(s32[1024,2]{0,1:T(2,128)} %param.21) | copy-start | bytes 24580
  247.5 64.4 %all-to-all-start.2 = ((bf16[8,216,768]{2,1,0:T(8,128)(2,1)}), bf16[8,216,768]{2,1,0:T(8,128)(2,1)}, u32[]{:S(2)}, u32[]{:S(2)}) async-start(bf16[8,216,768]{2,1,0:T(8,128)(2,1)} %bitcast.237), calls=%async_computation.2 | async-start | bytes 5308416 | tf_op jit(solution)/shard_map/all_to_all | solution.py:287
  312.0 63.5 %all-to-all-start = ((bf16[8,216,768]{2,1,0:T(8,128)(2,1)}), bf16[8,216,768]{2,1,0:T(8,128)(2,1)S(1)}, u32[]{:S(2)}, u32[]{:S(2)}) async-start(bf16[8,216,768]{2,1,0:T(8,128)(2,1)} %bitcast.236), calls=%async_computation | async-start | bytes 5308416 | tf_op jit(solution)/shard_map/all_to_all | solution.py:222
  400.6 25.1 %copy-start.73 = (bf16[2,768,2048]{2,1,0:T(8,128)(2,1)S(1)}, bf16[2,768,2048]{2,1,0:T(8,128)(2,1)}, u32[]{:S(2)}) copy-start(bf16[2,768,2048]{2,1,0:T(8,128)(2,1)} %all-gather.16.cloned.1.call-done) | copy-start | bytes 18874372
  438.4 64.4 %all-to-all-start.1 = ((bf16[2,864,768]{2,0,1:T(2,128)(2,1)}), bf16[2,864,768]{2,0,1:T(2,128)(2,1)}, u32[]{:S(2)}, u32[]{:S(2)}) async-start(bf16[2,864,768]{2,0,1:T(2,128)(2,1)} %copy.172), calls=%async_computation.1 | async-start | bytes 5308416 | tf_op jit(solution)/shard_map/all_to_all | solution.py:232
  479.9 28.2 %copy-start.58 = (s32[2048,1]{0,1:T(1,128)S(1)}, s32[2048,1]{0,1:T(1,128)}, u32[]{:S(2)}) copy-start(s32[2048,1]{0,1:T(1,128)} %copy-done.57) | copy-start | bytes 24580
  502.8 64.3 %all-to-all-start.3 = ((bf16[2,864,768]{2,0,1:T(2,128)(2,1)}), bf16[2,864,768]{2,0,1:T(2,128)(2,1)}, u32[]{:S(2)}, u32[]{:S(2)}) async-start(bf16[2,864,768]{2,0,1:T(2,128)(2,1)} %copy.182), calls=%async_computation.3 | async-start | bytes 5308416 | tf_op jit(solution)/shard_map/all_to_all | solution.py:304
  507.4 338.4 %reduce-scatter.12.cloned.1.call-start = ((), (), s32[]{:S(2)}) async-start(), calls=%async_computation.15 | async-start | bytes 1327104 | tf_op jit(solution)/shard_map/reduce_scatter | solution.py:368
  528.0 34.7 %copy-start.43 = (f32[1024,2]{0,1:T(2,128)S(1)}, f32[1024,2]{0,1:T(2,128)}, u32[]{:S(2)}) copy-start(f32[1024,2]{0,1:T(2,128)} %copy-done.42) | copy-start | bytes 24580
  528.0 36.8 %copy-start.39 = (s32[1024,2]{0,1:T(2,128)S(1)}, s32[1024,2]{0,1:T(2,128)}, u32[]{:S(2)}) copy-start(s32[1024,2]{0,1:T(2,128)} %param.21) | copy-start | bytes 24580
  564.9 34.3 %copy-start.33 = (f32[1024,12]{0,1:T(8,128)}, f32[1024,12]{0,1:T(8,128)S(1)}, u32[]{:S(2)}) copy-start(f32[1024,12]{0,1:T(8,128)S(1)} %fusion.69) | copy-start | bytes 147460
  792.6 88.1 %reduce-scatter.10.cloned.1.call-start = ((), (), s32[]{:S(2)}) async-start(), calls=%async_computation.14 | async-start | bytes 3981312 | tf_op jit(solution)/shard_map/reduce_scatter | solution.py:365
  804.6 119.0 %reduce-scatter.18.cloned.1.call-start = ((), (), s32[]{:S(2)}) async-start(), calls=%async_computation.18 | async-start | bytes 221184
  831.8 123.0 %reduce-scatter.16.cloned.1.call-start = ((), (), s32[]{:S(2)}) async-start(), calls=%async_computation.17 | async-start | bytes 221184
  833.7 163.1 %all-reduce.14.cloned.1.call-start = ((), (), s32[]{:S(2)}) async-start(), calls=%async_computation.19 | async-start | bytes 1179648 | tf_op jit(solution)/shard_map/psum | solution.py:383
  880.7 246.0 %reduce-scatter.14.cloned.1.call-start = ((), (), s32[]{:S(2)}) async-start(), calls=%async_computation.16 | async-start | bytes 21233664 | tf_op jit(solution)/shard_map/reduce_scatter | solution.py:314
  897.7 22.0 %copy-start.18 = (f32[1024,768]{1,0:T(8,128)S(1)}, f32[1024,768]{1,0:T(8,128)}, u32[]{:S(2)}) copy-start(f32[1024,768]{1,0:T(8,128)} %copy-done.17) | copy-start | bytes 9437188
  897.7 22.0 %copy-start.59 = (f32[1024]{0:T(1024)S(1)}, f32[1024]{0:T(1024)}, u32[]{:S(2)}) copy-start(f32[1024]{0:T(1024)} %get-tuple-element.474) | copy-start | bytes 12292
  (63 other events, 340.2 us)
Sparse Core Ops, SparseCore 0:
  10.0 36.6 all-gather.7
  48.5 24.0 all-gather.9
  74.5 46.6 all-gather.11
  122.9 46.6 all-gather.13
  171.3 46.6 all-gather.15
  792.7 35.8 reduce-scatter.11
  832.4 48.1 reduce-scatter.9
  884.6 32.9 reduce-scatter.17
  921.2 33.5 reduce-scatter.15
  957.2 39.5 all-reduce.13
  1000.8 125.9 reduce-scatter.13
where the time goes:
time: 1150 us; the launch traced here: 1140 us
  waiting for transfers between devices  358 us (31%)
  matrix products  319 us (28%)
  local copies, waits for them, and re-layouts  203 us (18%)
  other arithmetic  166 us (14%)
  blocking collectives  55 us (5%)
  starting transfers between devices  18.5 us (2%)
  between operations  16.6 us (1%)
    reduce_scatter x1, waiting for transfers between devices, local(): lax.psum_scatter(jnp.stack([term_gate, term_up, term_down], axis=2).resha...  126 us
    all_to_all x1, waiting for transfers between devices, local(): lax.all_to_all(outgoing, 'expert', split_axis=0, concat_axis=1, tiled=True)  56.2 us
    all_to_all x1, waiting for transfers between devices, local(): lax.all_to_all(grad_outgoing, 'expert', split_axis=0, concat_axis=1, tile...  53.3 us
    dot_general x4, matrix products, block_scores(): jnp.einsum('qhd,khd->hqk', query_block, keys_rot, preferred_element_type=...  47.2 us
    convert_element_type x2, other arithmetic, one_block(): (probabilities * (grad_probs - inner_sum)).astype(jnp.bfloat16)  42.4 us
    dot_general x2, matrix products, one_block(): jnp.einsum('qhd,khd->hqk', grad_block, values, preferred_element_type=jnp...  36.2 us
    reduce_scatter x1, waiting for transfers between devices, local(): lax.psum_scatter(grad_qkv_w.astype(jnp.bfloat16), 'shard', scatter_dimens...  34.9 us
    unnamed x13, waiting for transfers between devices  33.5 us
  transfers between devices with their start and end apart: 15, of which 8 were waited for; matrix products, arithmetic and copies ran while one was open for 36% of the time, Pallas kernels for 0%

commit v1 on v0

v1 whole, which is shorter than its diff:
```python
import functools

import jax
import jax.numpy as jnp
import numpy as np
from jax import lax
from jax.experimental import pallas as pl
from jax.experimental.pallas import tpu as pltpu
from jax.sharding import Mesh
from jax.sharding import PartitionSpec as P

HEADS = 12
HEAD = 64
EXPERTS = 8
ZEROS = 4
BLOCK = 256
CAP = 216
PAIRS = HEADS // 2
SLOTS = 224
GROUP = EXPERTS * SLOTS
SCALAR_ROWS = SLOTS - 16
GROUPS = ((0, 1, 2, 3), (4, 5), (6, 7))
TILE = 256
MIB = 1 << 20
LIMIT = 60
WEIGHT = 10
LIGHT = 3
LATE = 0.01
FILL = 0.01

epsilon = 1e-06
bf16 = jnp.bfloat16
f32 = jnp.float32


def dot_nn(a, b):
    return lax.dot_general(a, b, (((1,), (0,)), ((), ())), preferred_element_type=f32)


def dot_nt(a, b):
    return lax.dot_general(a, b, (((1,), (1,)), ((), ())), preferred_element_type=f32)


def dot_tn(a, b):
    return lax.dot_general(a, b, (((0,), (0,)), ((), ())), preferred_element_type=f32)


def iota(shape, axis):
    return lax.broadcasted_iota(jnp.int32, shape, axis)


def mark(condition):
    return jnp.where(condition, 1.0, 0.0).astype(bf16)


def split(value):
    high = value.astype(bf16)
    return high, (value - high.astype(f32)).astype(bf16)


def full(shape):
    return pl.BlockSpec(shape, lambda *_: (0,) * len(shape))


def rows(tile, width, steps=None):
    if steps is None:
        return pl.BlockSpec((tile, width), lambda i: (i, 0))
    return pl.BlockSpec((tile, width), lambda i: (jnp.minimum(i, steps - 1), 0))


def columns(height, tile):
    return pl.BlockSpec((height, tile), lambda i: (0, i))


SCALAR = pl.BlockSpec(memory_space=pltpu.SMEM)
WHOLE = pl.BlockSpec(memory_space=pl.ANY)


def shape(dims, dtype):
    return jax.ShapeDtypeStruct(dims, dtype)


def cost(flops, moved, weight=WEIGHT):
    return pl.CostEstimate(
        flops=int(flops * weight), bytes_accessed=int(moved * weight), transcendentals=0
    )


def params():
    return pltpu.CompilerParams(vmem_limit_bytes=LIMIT * MIB)


def nothing(*refs):
    pass


def after(value, *others):
    if not others:
        return value
    return pl.pallas_call(
        nothing,
        in_specs=[WHOLE] * (1 + len(others)),
        out_specs=WHOLE,
        out_shape=shape(value.shape, value.dtype),
        input_output_aliases={0: 0},
        name="after",
    )(value, *others)


def all_after(values, *others):
    count = len(values)
    return pl.pallas_call(
        nothing,
        in_specs=[WHOLE] * (count + len(others)),
        out_specs=[WHOLE] * count,
        out_shape=[shape(value.shape, value.dtype) for value in values],
        input_output_aliases={index: index for index in range(count)},
        name="all_after",
    )(*values, *others)


def one_hot(targets, base, count, width, axis):
    dims = (count, width) if axis == 0 else (width, count)
    slots = iota(dims, axis) + base
    first, second = targets
    return mark((slots == first) | (slots == second))


def place_body(routes_ref, order_ref, cot_ref, trow_ref, tcol_ref, piece_ref):
    length = routes_ref.shape[1]
    ids = jnp.concatenate([routes_ref[0:1, :], routes_ref[1:2, :]], axis=1)
    order = jnp.concatenate([order_ref[0:1, :], order_ref[1:2, :]], axis=1)
    high = order >> 7
    low = order & 127
    place = iota((128, 2 * length), 0)
    by_group = mark(place == ids * 16 + high)
    by_low = mark(place == low)
    table = dot_nt(by_group, by_low).astype(bf16)
    line = iota((128, 128), 0)
    lane = iota((128, 128), 1)
    before = mark(line < lane)
    groups = mark(((line >> 4) == (lane >> 4)) & ((lane & 15) < (line & 15)))
    earlier = dot_nn(groups, table).astype(bf16)
    ahead = dot_nn(table, before) + dot_nn(earlier, jnp.ones((128, 128), bf16))
    ahead = jnp.minimum(ahead, 255.0).astype(bf16)
    picked = dot_tn(ahead, by_group)
    slot = jnp.sum(jnp.where(place == low, picked, 0.0), axis=0, keepdims=True)
    slot = slot.astype(jnp.int32)
    kept = (ids < EXPERTS) & (slot < CAP)
    target = jnp.where(kept, ids * SLOTS + slot, -1)
    first = target[:, :length]
    second = target[:, length:]
    line8 = iota((8, length), 0)
    both = jnp.where(line8 == 0, first, jnp.where(line8 == 1, second, -1))
    trow_ref[...] = both
    tcol_ref[...] = jnp.transpose(both.astype(f32)).astype(jnp.int32)
    chosen = one_hot((first, second), 0, GROUP, length, 0)
    rows_out = dot_nn(chosen, cot_ref[...]).astype(bf16)
    piece_ref[...] = rows_out.reshape(EXPERTS, SLOTS, rows_out.shape[1])


def place(routes_row, order_row, cot):
    length, width = cot.shape
    dims = (EXPERTS, SLOTS, width)
    return pl.pallas_call(
        place_body,
        grid=(1,),
        in_specs=[full((2, length)), full((2, length)), full((length, width))],
        out_specs=[full((8, length)), full((length, 8)), full(dims)],
        out_shape=[
            shape((8, length), jnp.int32),
            shape((length, 8), jnp.int32),
            shape(dims, bf16),
        ],
        compiler_params=params(),
        cost_estimate=cost(2 * GROUP * length * width, 3 * length * width * 2, LIGHT),
        name="place",
    )(routes_row, order_row, cot)


def rotary(length):
    half = HEAD // 2
    frequencies = 10000.0 ** (-(np.arange(half).astype(np.float32) * 2.0 / HEAD))
    angles = np.arange(length).astype(np.float32)[:, None] * frequencies[None, :].astype(np.float32)
    cosine = np.cos(angles).astype(np.float32)
    sine = np.sin(angles).astype(np.float32)
    return (
        np.concatenate([cosine, cosine, cosine, cosine], axis=1),
        np.concatenate([-sine, sine, -sine, sine], axis=1),
    )


def turn(value, cosine, sine):
    lane = iota(value.shape, 1)
    first = (lane & (HEAD - 1)) < HEAD // 2
    other = jnp.where(
        first, pltpu.roll(value, 128 - HEAD // 2, 1), pltpu.roll(value, HEAD // 2, 1)
    )
    return value * cosine + other * sine


def project_body(starts, where_ref, tokens_ref, cos_ref, sin_ref, *rest):
    count = len(starts)
    pieces = rest[:count]
    (
        q_ref,
        k_ref,
        v_ref,
        normed_ref,
        small_ref,
        weight_out,
        out_w_out,
        weight_ref,
        out_w_ref,
        sems,
        out_sems,
    ) = rest[count:]
    back = (
        pltpu.make_async_copy(weight_ref, weight_out, out_sems.at[0]),
        pltpu.make_async_copy(out_w_ref, out_w_out, out_sems.at[1]),
    )
    width = tokens_ref.shape[1]
    wide = weight_ref.shape[1]
    step = pl.program_id(0)

    @pl.when(step == 0)
    def _():
        copies = []
        for index, piece in enumerate(pieces):
            deep = piece.shape[0]
            where = pl.ds(pl.multiple_of(where_ref[index], 16), deep)
            copies.append(
                pltpu.make_async_copy(
                    piece.at[:, :wide], weight_ref.at[where, :], sems.at[0, index]
                )
            )
            copies.append(
                pltpu.make_async_copy(
                    piece.at[:, wide:], out_w_ref.at[where, :], sems.at[1, index]
                )
            )
        for copy in copies:
            copy.start()
        for copy in copies:
            copy.wait()
        for copy in back:
            copy.start()
        extra = weight_ref[:, 3 * width :].astype(f32)
        small_ref[...] = jnp.transpose(extra)[0:16, :]

    @pl.when(step == pl.num_programs(0) - 1)
    def _():
        for copy in back:
            copy.wait()

    gain = small_ref[14:15, :]
    value = tokens_ref[...].astype(f32)
    inverse = lax.rsqrt(jnp.mean(value * value, axis=1, keepdims=True) + epsilon)
    normed = (value * inverse * gain).astype(bf16)
    normed_ref[...] = normed
    cosine = cos_ref[...]
    sine = sin_ref[...]
    for part in range(3):
        for pair in range(0, PAIRS, 2):
            start = pair * 128
            projected = dot_nn(
                normed, weight_ref[:, part * width + start : part * width + start + 256]
            )
            for half in range(2):
                cut = slice(start + half * 128, start + half * 128 + 128)
                piece = projected[:, half * 128 : half * 128 + 128]
                if part == 0:
                    q_ref[:, cut] = (turn(piece, cosine, sine).astype(bf16) * 0.125).astype(bf16)
                elif part == 1:
                    k_ref[:, cut] = turn(piece, cosine, sine).astype(bf16)
                else:
                    v_ref[:, cut] = piece.astype(bf16)


def project(tokens, pieces, where, cosine, sine):
    length, width = tokens.shape
    count = len(pieces)
    wide = pieces[0].shape[1] - width
    return pl.pallas_call(
        functools.partial(project_body, tuple(range(count))),
        grid=(length // TILE,),
        in_specs=[SCALAR, rows(TILE, width), rows(TILE, 128), rows(TILE, 128)]
        + [WHOLE] * count,
        out_specs=[rows(TILE, width)] * 4 + [full((16, width)), WHOLE, WHOLE],
        out_shape=[shape((length, width), bf16)] * 4
        + [
            shape((16, width), f32),
            shape((width, wide), bf16),
            shape((width, width), bf16),
        ],
        scratch_shapes=[
            pltpu.VMEM((width, wide), bf16),
            pltpu.VMEM((width, width), bf16),
            pltpu.SemaphoreType.DMA((2, count)),
            pltpu.SemaphoreType.DMA((2,)),
        ],
        compiler_params=params(),
        cost_estimate=cost(6 * length * width * width, 16 * length * width, LIGHT),
        name="project",
    )(where, tokens, cosine, sine, *pieces)


def attend_body(q_ref, k_ref, v_ref, out_ref, total_ref, wide_ref):
    length = q_ref.shape[0]
    wide_ref[:, :128] = v_ref[...]
    wide_ref[:, 128:] = jnp.ones((length, 128), bf16)
    lane = iota((BLOCK, 128), 1)
    for block in range(length // BLOCK):
        cut = slice(block * BLOCK, (block + 1) * BLOCK)
        seen = (block + 1) * BLOCK
        query = q_ref[cut, :]
        zero = jnp.zeros_like(query)
        result = None
        total = None
        for head in range(2):
            mine = (lane < HEAD) if head == 0 else (lane >= HEAD)
            scores = dot_nt(jnp.where(mine, query, zero), k_ref[:seen, :])
            top = jnp.max(scores, axis=1, keepdims=True)
            weights = jnp.exp(scores - top).astype(bf16)
            both = dot_nn(weights, wide_ref[:seen, :])
            summed = both[:, 128:]
            out = both[:, :128] / summed
            log_total = top + jnp.log(summed)
            if head == 0:
                result, total = out, log_total
            else:
                result = jnp.where(mine, out, result)
                total = jnp.where(mine, log_total, total)
        out_ref[cut, :] = result.astype(bf16)
        turned = jnp.transpose(total)
        total_ref[0, 0:1, cut] = turned[0:1, :]
        total_ref[0, 1:2, cut] = turned[HEAD : HEAD + 1, :]


def attend(queries, keys, values):
    length, width = queries.shape
    pair = pl.BlockSpec((length, 128), lambda i: (0, i))
    return pl.pallas_call(
        attend_body,
        grid=(PAIRS,),
        in_specs=[pair] * 3,
        out_specs=[pair, pl.BlockSpec((1, 2, length), lambda i: (i, 0, 0))],
        out_shape=[shape((length, width), bf16), shape((PAIRS, 2, length), f32)],
        scratch_shapes=[pltpu.VMEM((length, 256), bf16)],
        compiler_params=params(),
        cost_estimate=cost(8 * length * length * width, 8 * length * width, LIGHT),
        name="attend",
    )(queries, keys, values)


def mix_body(
    mine_ref,
    attended_ref,
    weight_ref,
    tokens_ref,
    cot_ref,
    small_ref,
    prev_ref,
    routes_ref,
    trow_ref,
    residual_ref,
    normed_ref,
    gates_ref,
    zero_ref,
    *rest,
):
    pieces = rest[:EXPERTS]
    kept, logits_ref, rows_all, sems = rest[EXPERTS:]
    length = kept.shape[0]
    steps = length // TILE
    step = pl.program_id(0)

    @pl.when(step < steps)
    def _():
        residual = tokens_ref[...].astype(f32) + dot_nn(attended_ref[...], weight_ref[...])
        residual_ref[...] = residual
        inverse = lax.rsqrt(jnp.mean(residual * residual, axis=1, keepdims=True) + epsilon)
        normed = (residual * inverse * small_ref[15:16, :]).astype(bf16)
        normed_ref[...] = normed
        kept[pl.ds(pl.multiple_of(step * TILE, TILE), TILE), :] = normed
        small = small_ref[...].astype(bf16)
        cot = cot_ref[...]
        high, low = split(cot.astype(f32) * normed.astype(f32))
        ones = jnp.ones((16, high.shape[1]), bf16)
        along = dot_nt(ones, high) + dot_nt(ones, low)
        constant = dot_nt(small, cot)
        line = iota((16, TILE), 0)
        where = pl.ds(pl.multiple_of(step * TILE, TILE), TILE)
        zero_ref[:, where] = jnp.where(
            line == EXPERTS + 1,
            along,
            jnp.where(
                line == EXPERTS + 2,
                constant[12:13, :],
                jnp.where(line == EXPERTS + 3, constant[13:14, :], 0.0),
            ),
        )
        logits_ref[:, where] = dot_nt(small, normed)

    @pl.when(step == steps)
    def _():
        all_ids = EXPERTS + ZEROS
        logits = logits_ref[0:all_ids, :] + prev_ref[...]
        line = iota((all_ids, length), 0)
        id0 = routes_ref[0:1, :]
        id1 = routes_ref[1:2, :]
        one = jnp.sum(jnp.where(line == id0, logits, 0.0), axis=0, keepdims=True)
        two = jnp.sum(jnp.where(line == id1, logits, 0.0), axis=0, keepdims=True)
        top = jnp.maximum(one, two)
        one = jnp.exp(one - top)
        two = jnp.exp(two - top)
        scale = 1.0 / (one + two)
        gate0 = one * scale
        gate1 = two * scale

        def gate_of(expert):
            return jnp.where(id0 == expert, gate0, jnp.where(id1 == expert, gate1, 0.0))

        line8 = iota((8, length), 0)
        gates = jnp.where(line8 == 0, gate0, jnp.where(line8 == 1, gate1, 0.0))
        for offset in range(1, ZEROS):
            expert = EXPERTS + offset
            own = jnp.where(id0 == expert, gate0, jnp.where(id1 == expert, gate1, 0.0))
            gates = jnp.where(line8 == 1 + offset, own, gates)
        gates_ref[...] = gates
        targets = (trow_ref[0:1, :], trow_ref[1:2, :])
        chosen = one_hot(targets, 0, GROUP, length, 0)
        picked = dot_nn(chosen, kept[...]).astype(bf16)
        rows_all[...] = picked.reshape(EXPERTS, SLOTS, picked.shape[1])
        line16 = iota((16, length), 0)
        expert_of = line16 & (EXPERTS - 1)
        own = jnp.where(id0 == expert_of, gate0, jnp.where(id1 == expert_of, gate1, 0.0))
        high = own.astype(bf16).astype(f32)
        both = jnp.where(line16 < EXPERTS, high, own - high)
        scalars = dot_nt(both.astype(bf16), chosen)
        for expert in range(EXPERTS):
            shift = expert * SLOTS
            turned = pltpu.roll(scalars, GROUP - shift, 1) if shift else scalars
            put_scalars(
                rows_all,
                expert,
                turned[expert : expert + 1, :TILE],
                turned[EXPERTS + expert : EXPERTS + expert + 1, :TILE],
            )
        copies = [
            pltpu.make_async_copy(rows_all.at[mine_ref[0] ^ index], piece, sems.at[index])
            for index, piece in enumerate(pieces)
        ]
        for copy in copies:
            copy.start()
        for copy in copies:
            copy.wait()


def put_scalars(target, index, high, low):
    line = iota((16, TILE), 0)
    lane = iota((16, TILE), 1)
    extra = jnp.where(line == 8, high, jnp.where(line == 9, low, 0.0))
    extra = jnp.where(lane < SLOTS, extra, 0.0)
    last = target[index, SCALAR_ROWS:, :TILE].astype(f32)
    target[index, SCALAR_ROWS:, :TILE] = (last + extra).astype(bf16)


def take_scalars(tile):
    turned = jnp.transpose(tile.astype(f32))[:SLOTS]
    return turned[:, 8:9], turned[:, 9:10]


def mix(mine, attended, weight, tokens, cot, small, prev_row, routes_row, trow):
    length, width = tokens.shape
    steps = length // TILE
    tile = rows(TILE, width, steps)
    return pl.pallas_call(
        mix_body,
        grid=(steps + 1,),
        in_specs=[
            SCALAR,
            tile,
            full(weight.shape),
            tile,
            tile,
            full(small.shape),
            full(prev_row.shape),
            full((2, length)),
            full((8, length)),
        ],
        out_specs=[tile, tile, full((8, length)), full((16, length))]
        + [WHOLE] * EXPERTS,
        out_shape=[
            shape((length, width), f32),
            shape((length, width), bf16),
            shape((8, length), f32),
            shape((16, length), f32),
        ]
        + [shape((SLOTS, width), bf16)] * EXPERTS,
        scratch_shapes=[
            pltpu.VMEM((length, width), bf16),
            pltpu.VMEM((16, length), f32),
            pltpu.VMEM((EXPERTS, SLOTS, width), bf16),
            pltpu.SemaphoreType.DMA((EXPERTS,)),
        ],
        compiler_params=params(),
        cost_estimate=cost(
            2 * length * width * width + 2 * GROUP * length * width, 18 * length * width, LIGHT),
        name="mix",
    )(mine, attended, weight, tokens, cot, small, prev_row, routes_row, trow)


def expert_body(group, chained, mine_ref, *refs):
    count = len(group)
    incoming = refs[:count]
    cot_all, weight_ref = refs[count : count + 2]
    refs = refs[count + 2 + chained :]
    hidden_ref, gate_ref, up_ref, scaled_ref, sent_ref = refs[:5]
    back = refs[5 : 5 + count]
    (
        rows_all,
        cot,
        sent,
        hidden_all,
        grads_all,
        down_all,
        in_all,
        gate_col,
        sems,
    ) = refs[5 + count :]
    step = pl.program_id(0)
    last = pl.num_programs(0) - 1
    width = rows_all.shape[1]
    part = hidden_ref.shape[1]
    inner = hidden_all.shape[1]
    deep = count * SLOTS

    @pl.when(step == 0)
    def _():
        copies = [
            pltpu.make_async_copy(cot_all.at[mine_ref[0] ^ index], cot.at[place_in], sems.at[place_in])
            for place_in, index in enumerate(group)
        ]
        for copy in copies:
            copy.start()
        for index in range(count):
            cut = slice(index * SLOTS, (index + 1) * SLOTS)
            rows_all[cut, :] = incoming[index][...]
            high, low = take_scalars(incoming[index][SCALAR_ROWS:, :TILE])
            gate_col[cut, :] = jnp.broadcast_to(high + low, (SLOTS, 128))
        for copy in copies:
            copy.wait()
        for index in range(count):
            cut = slice(index * SLOTS, (index + 1) * SLOTS)
            scaled_ref[cut, :] = (gate_col[cut, 0:1] * cot[index].astype(f32)).astype(bf16)

    value = rows_all[...]
    gate = dot_nn(value, weight_ref[0, 0])
    up = dot_nn(value, weight_ref[0, 1])
    grad_hidden = dot_nn(scaled_ref[...], weight_ref[0, 2])
    sigmoid = 1.0 / (1.0 + jnp.exp(-gate))
    active = gate * sigmoid
    hidden = (active * up).astype(bf16)
    grad_up = (grad_hidden * active).astype(bf16)
    grad_gate = (grad_hidden * up * (sigmoid + active * (1.0 - sigmoid))).astype(bf16)
    where = pl.ds(pl.multiple_of(step * part, part), part)
    behind = pl.ds(pl.multiple_of(inner + step * part, part), part)
    hidden_ref[...] = hidden
    gate_ref[...] = grad_gate
    up_ref[...] = grad_up
    hidden_all[:, where] = hidden
    grads_all[:, where] = grad_gate
    grads_all[:, behind] = grad_up
    in_all[:, where] = weight_ref[0, 0]
    in_all[:, behind] = weight_ref[0, 1]
    down_all[:, where] = weight_ref[0, 2]

    @pl.when(step == last)
    def _():
        column = gate_col[:, 0:1]
        along = None
        for start in range(0, width, TILE):
            cut = slice(start, start + TILE)
            produced = dot_nt(hidden_all[...], down_all[cut, :]).astype(bf16).astype(f32)
            sent[:, :, cut] = (produced * column).astype(bf16).reshape(count, SLOTS, TILE)
            term = jnp.sum(
                produced * cot[:, :, cut].reshape(deep, TILE).astype(f32), axis=1, keepdims=True
            )
            along = term if along is None else along + term
        copies = [
            pltpu.make_async_copy(
                sent.at[place_in], sent_ref.at[mine_ref[0] ^ index], sems.at[place_in]
            )
            for place_in, index in enumerate(group)
        ]
        for copy in copies:
            copy.start()
        for start in range(0, width, TILE):
            cut = slice(start, start + TILE)
            grads = dot_nt(grads_all[...], in_all[cut, :]).astype(bf16)
            for index in range(count):
                own = grads[index * SLOTS : (index + 1) * SLOTS]
                if start == 0:
                    scalar = along[index * SLOTS : (index + 1) * SLOTS]
                    scalar = jnp.broadcast_to(scalar, (SLOTS, 128))
                    spare = jnp.zeros((TILE - SLOTS, 128), f32)
                    scalar = jnp.transpose(jnp.concatenate([scalar, spare], axis=0))[0:16]
                    high = scalar.astype(bf16).astype(f32)
                    line = iota((16, TILE), 0)
                    extra = jnp.where(line == 8, high, jnp.where(line == 9, scalar - high, 0.0))
                    back[index][:SCALAR_ROWS, cut] = own[:SCALAR_ROWS]
                    last_rows = own[SCALAR_ROWS:].astype(f32) + extra
                    back[index][SCALAR_ROWS:, cut] = last_rows.astype(bf16)
                else:
                    back[index][:, cut] = own
        for copy in copies:
            copy.wait()


def expert_rows(group, mine, incoming, cotangents, weight, sent):
    count = len(group)
    width = incoming[0].shape[1]
    blocks, _, _, part = weight.shape
    inner = blocks * part
    deep = count * SLOTS
    chained = len(sent)
    block = pl.BlockSpec((deep, part), lambda i: (0, i))
    wide = shape((deep, inner), bf16)
    piece = full((SLOTS, width))
    return pl.pallas_call(
        functools.partial(expert_body, group, chained),
        grid=(blocks,),
        in_specs=[SCALAR]
        + [piece] * count
        + [WHOLE, pl.BlockSpec((1, 3, width, part), lambda i: (i, 0, 0, 0))]
        + [WHOLE] * chained,
        out_specs=[block, block, block, full((deep, width)), WHOLE] + [piece] * count,
        out_shape=[wide, wide, wide, shape((deep, width), bf16)]
        + [shape((EXPERTS, SLOTS, width), bf16)]
        + [shape((SLOTS, width), bf16)] * count,
        input_output_aliases={count + 3: 4} if chained else {},
        scratch_shapes=[
            pltpu.VMEM((deep, width), bf16),
            pltpu.VMEM((count, SLOTS, width), bf16),
            pltpu.VMEM((count, SLOTS, width), bf16),
            pltpu.VMEM((deep, inner), bf16),
            pltpu.VMEM((deep, 2 * inner), bf16),
            pltpu.VMEM((width, inner), bf16),
            pltpu.VMEM((width, 2 * inner), bf16),
            pltpu.VMEM((deep, 128), f32),
            pltpu.SemaphoreType.DMA((count,)),
        ],
        compiler_params=params(),
        cost_estimate=cost(12 * deep * width * inner, 6 * width * inner + 6 * deep * inner),
        name="expert_rows",
    )(mine, *incoming, cotangents, weight, *sent)


def weights_body(counts, chained, *refs):
    total = sum(counts)
    groups = len(counts)
    incoming = refs[:total]
    scaled = refs[total : total + groups]
    wide = refs[total + groups : total + 4 * groups]
    refs = refs[total + 4 * groups + chained :]
    out_ref = refs[0]
    turned = refs[1:]
    step = pl.program_id(0)

    @pl.when(step == 0)
    def _():
        start = 0
        for group, count in enumerate(counts):
            value = jnp.concatenate(
                [incoming[start + index][...] for index in range(count)], axis=0
            )
            turned[2 * group][...] = jnp.transpose(value)
            turned[2 * group + 1][...] = jnp.transpose(scaled[group][...])
            start += count

    for which in range(3):
        result = None
        for group in range(groups):
            hidden, grad_gate, grad_up = wide[3 * group : 3 * group + 3]
            left = turned[2 * group + (1 if which == 2 else 0)]
            term = dot_nn(left[...], (grad_gate, grad_up, hidden)[which][...])
            result = term if result is None else result + term
        out_ref[0, which] = result.astype(bf16)


def expert_weights(start, count, incoming, scaled, wide, blocks, made):
    width = incoming[0].shape[1]
    part = wide[0].shape[1] // blocks
    inner = count * part
    depths = [block.shape[0] for block in scaled]
    in_specs = [full((SLOTS, width))] * len(incoming)
    in_specs += [full((deep, width)) for deep in depths]
    scratch = []
    for deep in depths:
        in_specs += [pl.BlockSpec((deep, part), lambda i: (0, i + start))] * 3
        scratch += [pltpu.VMEM((width, deep), bf16)] * 2
    given = (*incoming, *scaled, *wide)
    return pl.pallas_call(
        functools.partial(weights_body, tuple(deep // SLOTS for deep in depths), len(made)),
        grid=(count,),
        in_specs=in_specs + [WHOLE] * len(made),
        out_specs=pl.BlockSpec((1, 3, width, part), lambda i: (i + start, 0, 0, 0)),
        out_shape=shape((blocks, 3, width, part), bf16),
        input_output_aliases={len(given): 0} if made else {},
        scratch_shapes=scratch,
        compiler_params=params(),
        cost_estimate=cost(
            6 * GROUP * width * inner, 6 * width * inner + 6 * GROUP * inner, FILL
        ),
        name="expert_weights",
    )(*given, *made)


def dealt(height, parts, width, split_of):
    chips, subs = split_of
    return (chips, parts, height // (chips * subs), width)


def deal(place_ref, source, keep_ref, give_ref):
    chips, parts, deep, width = keep_ref.shape
    subs = source.shape[0] // (chips * deep)
    for chip in range(chips):
        for other, target in enumerate((keep_ref, give_ref)[:subs]):
            start = ((place_ref[0] ^ chip) * subs + (place_ref[1] ^ other)) * deep
            block = source[pl.ds(pl.multiple_of(start, 16), deep), :]
            for part in range(parts):
                target[chip, part] = block[:, part * width : (part + 1) * width]


def return_body(
    place_ref,
    tcol_ref,
    routes_ref,
    gates_ref,
    zero_ref,
    small_ref,
    weight_ref,
    residual_ref,
    normed_ref,
    cot_ref,
    attended_ref,
    *rest,
):
    pieces = rest[:EXPERTS]
    logit_ref, grad_res_ref, grad_att_ref, delta_ref, keep_ref, give_ref = rest[
        EXPERTS : EXPERTS + 6
    ]
    out_sum, extra_sum, grads_all, scalars_all, back_all, sems = rest[EXPERTS + 6 :]
    step = pl.program_id(0)
    width = residual_ref.shape[1]
    id0 = routes_ref[0:1, :]
    id1 = routes_ref[1:2, :]
    line = iota((16, TILE), 0)

    @pl.when(step == 0)
    def _():
        copies = [
            pltpu.make_async_copy(piece, back_all.at[place_ref[2] ^ index], sems.at[index])
            for index, piece in enumerate(pieces)
        ]
        for copy in copies:
            copy.start()
        for copy in copies:
            copy.wait()
        lane = iota((SLOTS, 128), 1)
        for expert in range(EXPERTS):
            high, low = take_scalars(back_all[expert, SCALAR_ROWS:, :TILE])
            spot = jnp.where(lane == expert, high, jnp.where(lane == EXPERTS + expert, low, 0.0))
            scalars_all[expert * SLOTS : (expert + 1) * SLOTS, :] = spot.astype(bf16)

    chosen = one_hot((tcol_ref[:, 0:1], tcol_ref[:, 1:2]), 0, GROUP, TILE, 1)
    from_rows = dot_nn(chosen, back_all[...].reshape(GROUP, width))
    scalars = jnp.transpose(dot_nn(chosen, scalars_all[...]))
    through = jnp.concatenate(
        [scalars[:EXPERTS] + scalars[EXPERTS : 2 * EXPERTS], zero_ref[EXPERTS:]], axis=0
    )
    gate0 = gates_ref[0:1, :]
    gate1 = gates_ref[1:2, :]
    grad0 = jnp.sum(jnp.where(line == id0, through, 0.0), axis=0, keepdims=True)
    grad1 = jnp.sum(jnp.where(line == id1, through, 0.0), axis=0, keepdims=True)
    mean = gate0 * grad0 + gate1 * grad1
    chosen0 = gate0 * (grad0 - mean)
    chosen1 = gate1 * (grad1 - mean)
    logit = jnp.where(line == id0, chosen0, jnp.where(line == id1, chosen1, 0.0))
    logit_ref[...] = logit[: EXPERTS + ZEROS]
    logit_high, logit_low = split(logit)
    small = small_ref[...].astype(bf16)
    both = jnp.concatenate([logit_high.astype(f32), logit_low.astype(f32)], axis=0).astype(bf16)
    twice = jnp.concatenate([small_ref[...], small_ref[...]], axis=0).astype(bf16)
    grad_normed = dot_tn(both, twice)
    grad_normed += from_rows
    cot = cot_ref[...]
    cot_wide = cot.astype(f32)
    gate_cols = jnp.transpose(gates_ref[...])
    grad_normed += gate_cols[:, 2:3] * cot_wide
    residual = residual_ref[...]
    gain = small_ref[15:16, :]
    inverse = lax.rsqrt(jnp.mean(residual * residual, axis=1, keepdims=True) + epsilon)
    scaled = grad_normed * gain
    spread = jnp.mean(scaled * residual, axis=1, keepdims=True)
    grad_residual = cot_wide + inverse * scaled - residual * (inverse * inverse * inverse * spread)
    grad_res_ref[...] = grad_residual
    grad_low = grad_residual.astype(bf16)
    grad_att = dot_nt(grad_low, weight_ref[...]).astype(bf16)
    grad_att_ref[...] = grad_att
    attended = attended_ref[...]
    product = (grad_att.astype(f32) * attended.astype(f32)).astype(bf16)
    head_of = (iota((16, width), 1) >> 6) == iota((16, width), 0)
    delta = dot_nt(mark(head_of), product)
    for pair in range(PAIRS):
        delta_ref[pair] = delta[2 * pair : 2 * pair + 2, :]
    out_term = dot_tn(attended, grad_low)
    grad_gain = jnp.sum(grad_normed * residual * inverse, axis=0, keepdims=True)
    normed = normed_ref[...]
    router_term = dot_nn(logit_high, normed) + dot_nn(logit_low, normed)
    const0 = gates_ref[3:4, :]
    const1 = gates_ref[4:5, :]
    weights = jnp.where(line == 12, const0, jnp.where(line == 13, const1, 0.0))
    const_high, const_low = split(weights)
    const_term = dot_nn(const_high, cot) + dot_nn(const_low, cot)
    extra = router_term + const_term
    extra = jnp.where(iota((16, width), 0) == 15, grad_gain, extra)

    @pl.when(step == 0)
    def _():
        out_sum[...] = out_term
        extra_sum[...] = jnp.zeros_like(extra_sum)
        extra_sum[0:16, :] = extra

    @pl.when(step > 0)
    def _():
        out_sum[...] += out_term
        extra_sum[0:16, :] += extra

    @pl.when(step == pl.num_programs(0) - 1)
    def _():
        small_grads = jnp.transpose(extra_sum[...]).astype(bf16)
        grads_all[:, :width] = out_sum[...].astype(bf16)
        grads_all[:, width:] = small_grads
        deal(place_ref, grads_all, keep_ref, give_ref)


def come_back(
    place_of,
    tcol,
    routes_row,
    gates,
    zero,
    small,
    weight,
    residual,
    normed,
    cot,
    attended,
    pieces,
    split_of,
):
    length, width = cot.shape
    steps = length // TILE
    tile = rows(TILE, width)
    dims = dealt(width, 1, width + 128, split_of)
    all_ids = EXPERTS + ZEROS
    return pl.pallas_call(
        return_body,
        grid=(steps,),
        in_specs=[
            SCALAR,
            rows(TILE, 8),
            columns(2, TILE),
            columns(8, TILE),
            columns(16, TILE),
            full(small.shape),
            full(weight.shape),
            tile,
            tile,
            tile,
            tile,
        ]
        + [WHOLE] * EXPERTS,
        out_specs=[
            columns(all_ids, TILE),
            tile,
            tile,
            pl.BlockSpec((PAIRS, 2, TILE), lambda i: (0, 0, i)),
            full(dims),
            full(dims),
        ],
        out_shape=[
            shape((all_ids, length), f32),
            shape((length, width), f32),
            shape((length, width), bf16),
            shape((PAIRS, 2, length), f32),
            shape(dims, bf16),
            shape(dims, bf16),
        ],
        scratch_shapes=[
            pltpu.VMEM((width, width), f32),
            pltpu.VMEM((128, width), f32),
            pltpu.VMEM((width, width + 128), bf16),
            pltpu.VMEM((GROUP, 128), bf16),
            pltpu.VMEM((EXPERTS, SLOTS, width), bf16),
            pltpu.SemaphoreType.DMA((EXPERTS,)),
        ],
        compiler_params=params(),
        cost_estimate=cost(
            4 * length * width * width + 2 * GROUP * length * width, 18 * length * width, 30),
        name="come_back",
    )(
        place_of,
        tcol,
        routes_row,
        gates,
        zero,
        small,
        weight,
        residual,
        normed,
        cot,
        attended,
        *pieces,
    )


def attend_back_body(
    place_ref,
    q_ref,
    k_ref,
    v_ref,
    grad_ref,
    total_ref,
    delta_ref,
    cos_ref,
    sin_ref,
    normed_ref,
    grads_ref,
    keep_ref,
    give_ref,
    turned,
    normed_turned,
    weight_grads,
):
    @pl.when(pl.program_id(0) == 0)
    def _():
        normed_turned[...] = jnp.transpose(normed_ref[...])

    length = q_ref.shape[0]
    cosine = cos_ref[...]
    sine = sin_ref[...]
    lane = iota((BLOCK, 128), 1)
    keys_turned = jnp.transpose(k_ref[...])
    line = iota((128, BLOCK), 0)
    for block in range(length // BLOCK):
        start = block * BLOCK
        cut = slice(start, start + BLOCK)
        key = k_ref[cut, :]
        value = v_ref[cut, :]
        zero = jnp.zeros_like(key)
        query = q_ref[start:, :]
        grad = grad_ref[start:, :]
        grad_key = None
        grad_value = None
        for head in range(2):
            mine = (lane < HEAD) if head == 0 else (lane >= HEAD)
            scores = dot_nt(jnp.where(mine, key, zero), query)
            weights = jnp.exp(scores - total_ref[0, head : head + 1, start:])
            grad_weights = dot_nt(jnp.where(mine, value, zero), grad)
            grad_scores = weights * (grad_weights - delta_ref[0, head : head + 1, start:])
            grad_scores = grad_scores.astype(bf16)
            value_term = dot_nn(weights.astype(bf16), grad)
            key_term = dot_nn(grad_scores, query)
            key_mine = (line < HEAD) if head == 0 else (line >= HEAD)
            key_line = keys_turned[:, cut]
            query_term = dot_nn(jnp.where(key_mine, key_line, jnp.zeros_like(key_line)), grad_scores)
            if block == 0 and head == 0:
                turned[...] = query_term
            else:
                turned[:, start:] += query_term
            if head == 0:
                grad_key, grad_value = key_term, value_term
            else:
                grad_key = jnp.where(mine, key_term, grad_key)
                grad_value = jnp.where(mine, value_term, grad_value)
        grad_key = grad_key.astype(bf16).astype(f32)
        grads_ref[cut, 128:256] = turn(grad_key, cosine[cut], -sine[cut]).astype(bf16)
        grads_ref[cut, 256:] = grad_value.astype(bf16)
    grad_query = (jnp.transpose(turned[...]) * 0.125).astype(bf16).astype(f32)
    grads_ref[:, :128] = turn(grad_query, cosine, -sine).astype(bf16)
    weight_grads[...] = dot_nn(normed_turned[...], grads_ref[...]).astype(bf16)
    deal(place_ref, weight_grads, keep_ref, give_ref)


def attend_back(
    first, count, place_of, queries, keys, values, grad, total, delta, cosine, sine, normed, split_of
):
    length, width = queries.shape
    pair = pl.BlockSpec((length, 128), lambda i: (0, i + first))
    line = pl.BlockSpec((1, 2, length), lambda i: (i + first, 0, 0))
    chips, parts, deep, across = dealt(width, 3, 128 * count, split_of)
    block = pl.BlockSpec((chips, parts, deep, 128), lambda i: (0, 0, 0, i))
    dims = shape((chips, parts, deep, across), bf16)
    return pl.pallas_call(
        attend_back_body,
        grid=(count,),
        in_specs=[SCALAR]
        + [pair] * 4
        + [line, line, full((length, 128)), full((length, 128)), full((length, width))],
        out_specs=[columns(length, 384), block, block],
        out_shape=[shape((length, 384 * count), bf16), dims, dims],
        scratch_shapes=[
            pltpu.VMEM((128, length), f32),
            pltpu.VMEM((width, length), bf16),
            pltpu.VMEM((width, 384), bf16),
        ],
        compiler_params=params(),
        cost_estimate=cost(
            26 * length * length * 128 * count, 14 * length * 128 * count, LATE),
        name="attend_back",
    )(place_of, queries, keys, values, grad, total, delta, cosine, sine, normed)


def tokens_grad_body(first_ref, second_ref, weight_ref, tokens_ref, grad_res_ref, small_ref, out_ref):
    width = tokens_ref.shape[1]
    grad_normed = None
    for group, ref in enumerate((first_ref, second_ref)):
        pairs = ref.shape[1] // 384
        for part in range(3):
            start = part * width + group * pairs * 128
            grads = jnp.concatenate(
                [
                    ref[:, pair * 384 + part * 128 : pair * 384 + part * 128 + 128]
                    for pair in range(pairs)
                ],
                axis=1,
            )
            term = dot_nt(grads, weight_ref[:, start : start + pairs * 128])
            grad_normed = term if grad_normed is None else grad_normed + term
    value = tokens_ref[...].astype(f32)
    inverse = lax.rsqrt(jnp.mean(value * value, axis=1, keepdims=True) + epsilon)
    scaled = grad_normed * small_ref[14:15, :]
    spread_of = jnp.mean(scaled * value, axis=1, keepdims=True)
    grad = inverse * scaled - value * (inverse * inverse * inverse * spread_of)
    out_ref[...] = grad_res_ref[...] + grad


def tokens_grad(grads, weight, tokens, grad_res, small):
    length, width = tokens.shape
    tile = rows(TILE, width)
    wide = grads[0].shape[1]
    return pl.pallas_call(
        tokens_grad_body,
        grid=(length // TILE,),
        in_specs=[rows(TILE, wide)] * 2
        + [full(weight.shape), tile, tile, full(small.shape)],
        out_specs=tile,
        out_shape=shape((length, width), f32),
        compiler_params=params(),
        cost_estimate=cost(6 * length * width * width, 16 * length * width, LATE),
        name="tokens_grad",
    )(*grads, weight, tokens, grad_res, small)


def output_body(
    tcol_ref, gates_ref, small_ref, residual_ref, normed_ref, block_ref, out_ref
):
    gates = gates_ref[...]
    line = iota(gates.shape, 0)
    gate_cols = jnp.transpose(gates)
    consts = jnp.where((line == 3) | (line == 4), gates, 0.0)
    high, low = split(consts)
    vectors = jnp.where(iota((8, small_ref.shape[1]), 0) == 3, small_ref[12:13, :], 0.0)
    vectors = jnp.where(
        iota((8, small_ref.shape[1]), 0) == 4, small_ref[13:14, :], vectors
    )
    both = jnp.concatenate([high.astype(f32), low.astype(f32)], axis=0).astype(bf16)
    twice = jnp.concatenate([vectors, vectors], axis=0).astype(bf16)
    total = residual_ref[...] + dot_tn(both, twice)
    total += gate_cols[:, 2:3] * normed_ref[...].astype(f32)
    chosen = one_hot((tcol_ref[:, 0:1], tcol_ref[:, 1:2]), 0, GROUP, TILE, 1)
    total += dot_nn(chosen, block_ref[...].reshape(GROUP, block_ref.shape[2]))
    out_ref[...] = total.astype(bf16)


def output(tcol, gates, small, residual, normed, block):
    length, width = residual.shape
    tile = rows(TILE, width)
    return pl.pallas_call(
        output_body,
        grid=(length // TILE,),
        in_specs=[rows(TILE, 8), columns(8, TILE), full(small.shape), tile, tile]
        + [full((EXPERTS, SLOTS, width))],
        out_specs=tile,
        out_shape=shape((length, width), bf16),
        compiler_params=params(),
        cost_estimate=cost(2 * GROUP * length * width, 12 * length * width, LATE),
        name="output",
    )(tcol, gates, small, residual, normed, block)


def local(
    tokens,
    cotangent,
    prev_logits,
    routes,
    priority,
    gain_mix,
    mix_qkv,
    mix_out,
    gain_moe,
    router,
    constants,
    w_gate,
    w_up,
    w_down,
):
    length, width = tokens.shape
    here, _, part = w_gate.shape
    depth = lax.axis_size("expert")
    chips = lax.axis_size("chip")
    z = lax.axis_index("expert").astype(jnp.int32)
    chip = lax.axis_index("chip").astype(jnp.int32)
    sub = lax.axis_index("sub").astype(jnp.int32)
    pairwise = chips == 4 and here == 2
    split_of = (chips, here) if pairwise else (1, 1)
    own = (z * here + sub).astype(jnp.int32)
    mine_of = own.reshape(1)
    spot = (chip, sub) if pairwise else (jnp.int32(0), jnp.int32(0))
    place_of = jnp.stack([*spot, own])
    members = [(a, b) for a in range(depth) for b in range(here)]

    def partner(index, value):
        if index == 0:
            return value
        moves = []
        for source, (a, b) in enumerate(members):
            c, d = members[source ^ index]
            moves += [
                ((a * chips + i) * here + b, (c * chips + i) * here + d) for i in range(chips)
            ]
        return lax.ppermute(value, ("expert", "chip", "sub"), moves)

    def trade(value, axis, size, index):
        return lax.ppermute(value, axis, [(i, i ^ index) for i in range(size)])

    def exchange(value):
        return lax.all_to_all(value, ("expert", "sub"), split_axis=0, concat_axis=0, tiled=True)

    features = mix_qkv.shape[0]
    extra = jnp.concatenate(
        [router, constants, gain_mix[:, None], gain_moe[:, None]], axis=1
    )
    extra = jnp.pad(extra, ((0, 0), (0, 128 - extra.shape[1])))
    packed = jnp.concatenate([mix_qkv, extra, mix_out], axis=1)
    routes_row = routes.T
    order_row = priority.reshape(length, 2).T
    trow, tcol, grads_out = place(routes_row, order_row, cotangent)
    cot_in = exchange(grads_out)

    if pairwise:
        near = [trade(packed, "chip", chips, index) for index in (1, 2)]
    else:
        near = [packed]

    def of_expert(index):
        return jnp.stack(
            [lax.dynamic_index_in_dim(w, index, 0, keepdims=False) for w in (w_gate, w_up, w_down)]
        )

    keep = of_expert(sub)
    if here == 1:
        mine = keep[None]
    else:
        give = of_expert(1 - sub)
        mine = jnp.stack([keep, trade(give, "sub", here, 1)], axis=0)
    weight = lax.all_gather(mine, "chip", axis=0, tiled=True)
    count = weight.shape[0]
    if part < 256:
        join = 256 // part
        weight = weight.reshape(count // join, join, 3, width, part)
        weight = weight.transpose(0, 2, 3, 1, 4).reshape(count // join, 3, width, 256)

    if pairwise:
        near = [after(piece, trow, mine) for piece in near]
        half = features // 2
        far = [
            trade(near[1][:half], "chip", chips, 1),
            trade(near[0][half:], "chip", chips, 2),
        ]
        pieces = [packed, *near, *far]
        spots = [chip, chip ^ 1, chip ^ 2, chip ^ 3, chip ^ 3]
        lower = [0, 0, 0, 0, half]
        pieces += [trade(piece, "sub", here, 1) for piece in pieces]
        where = jnp.stack(
            [(spot * here + sub) * features + low for spot, low in zip(spots, lower)]
            + [(spot * here + (sub ^ 1)) * features + low for spot, low in zip(spots, lower)]
        )
    else:
        pieces = [lax.all_gather(packed, ("chip", "sub"), axis=0, tiled=True)]
        where = jnp.zeros((1,), jnp.int32)

    cosine, sine = rotary(length)
    outs = project(tokens, pieces, where, cosine, sine)
    queries, keys, values, normed_one, small, qkv, out_w = outs
    attended, log_total = attend(queries, keys, values)
    outs = mix(mine_of, attended, out_w, tokens, cotangent, small, prev_logits.T, routes_row, trow)
    residual, normed_two, gates, zero = outs[:4]
    leaving = outs[4:]
    rows_in = [None] * EXPERTS
    returned = [None] * EXPERTS
    near = GROUPS[0][1:]
    far = [index for group in GROUPS[1:] for index in group]
    for index in GROUPS[0]:
        rows_in[index] = partner(index, leaving[index])
    crossing = all_after([leaving[index] for index in far], *[rows_in[index] for index in near])
    for index, block in zip(far, crossing):
        rows_in[index] = partner(index, block)

    sent, scaled, wide, ordered = [], [], [], []
    blocks = weight.shape[0]
    for group in GROUPS[:2]:
        incoming = [rows_in[index] for index in group]
        outs = expert_rows(group, mine_of, incoming, cot_in, weight, sent)
        wide += outs[:3]
        scaled.append(outs[3])
        sent = [outs[4]]
        ordered += incoming
        for index, block in zip(group, outs[5:]):
            returned[index] = partner(index, block)
    group = GROUPS[2]
    incoming = [rows_in[index] for index in group]
    sent[0] = after(sent[0], *[returned[index] for index in near])
    outs = expert_rows(group, mine_of, incoming, cot_in, weight, sent)
    wide += outs[:3]
    scaled.append(outs[3])
    sent = outs[4]
    ordered += incoming
    early = 3 * blocks // 8
    grads_w = [expert_weights(0, early, ordered, scaled, wide, blocks, [])]
    before = [returned[index] for index in GROUPS[1]] + grads_w
    for index, block in zip(group, all_after(outs[5:], *before)):
        returned[index] = partner(index, block)
    grads_w = expert_weights(
        early, blocks - early, ordered, scaled, wide, blocks, grads_w
    )
    residual_late = after(residual, grads_w)
    produced = exchange(sent)

    if part < 256:
        grads_w = grads_w.reshape(count // join, 3, width, join, part)
        grads_w = grads_w.transpose(0, 3, 1, 2, 4).reshape(count, 3, width, part)
    grads_w = lax.psum_scatter(grads_w, "chip", scatter_dimension=0, tiled=True)
    outs = come_back(
        place_of,
        tcol,
        routes_row,
        gates,
        zero,
        small,
        out_w,
        residual_late,
        normed_two,
        cotangent,
        attended,
        returned,
        split_of,
    )
    logit_grad, grad_res, grad_att, delta = outs[:4]
    dealt_out = outs[4:]

    def flat(block):
        return block.transpose(1, 0, 2).reshape(block.shape[1], -1)

    def over_cores(dealt_parts):
        if not pairwise:
            return [jnp.concatenate([flat(keep[0]) for keep, _ in dealt_parts], axis=1)]
        got = [trade(give, "sub", here, 1) for _, give in dealt_parts]
        sums = []
        for index in range(chips):
            both = [
                flat(keep[index]).astype(f32) + flat(other[index]).astype(f32)
                for (keep, _), other in zip(dealt_parts, got)
            ]
            sums.append(jnp.concatenate(both, axis=1).astype(bf16 if index else f32))
        return sums

    def over_chips(sums):
        if not pairwise:
            axes = ("chip", "sub")
            return lax.psum_scatter(sums[0], axes, scatter_dimension=0, tiled=True).astype(f32)
        total = sums[0]
        for index in range(1, chips):
            total += trade(sums[index], "chip", chips, index).astype(f32)
        return total

    def over_planes(total, index):
        low = total.astype(bf16)
        return low.astype(f32) + trade(low, "expert", depth, index).astype(f32)

    def back_through(first, normed):
        return attend_back(
            first,
            count,
            place_of,
            queries,
            keys,
            values,
            grad_att,
            log_total,
            delta,
            cosine,
            sine,
            normed,
            split_of,
        )

    count = PAIRS // 2
    grads_a, *dealt_a = back_through(0, normed_one)
    sums_a = over_cores([dealt_a, dealt_out])
    grads_b, *dealt_b = back_through(count, after(normed_one, sums_a[-1]))
    total_a = over_chips([after(sums_a[0], grads_b), *sums_a[1:]])
    dealt_b[0] = after(dealt_b[0], produced)
    sums_b = over_cores([dealt_b])
    total_a = after(over_planes(total_a, 1), sums_b[-1])
    token_grad = tokens_grad([grads_a, grads_b], qkv, tokens, after(grad_res, total_a), small)
    total_b = over_chips([after(sums_b[0], token_grad), *sums_b[1:]])
    block_out = output(tcol, gates, small, after(residual, total_b), normed_two, produced)
    index = 2
    while index < depth:
        total_a = over_planes(total_a, index)
        index *= 2
    index = 1
    while index < depth:
        total_b = over_planes(total_b, index)
        index *= 2
    summed = [total_a, total_b]

    if here == 1:
        grads_w = grads_w[0][:, None].astype(f32)
    else:
        own = grads_w[0]
        theirs = trade(after(grads_w[1], block_out), "sub", here, 1)
        pair = jnp.stack([own, theirs], axis=1).astype(f32)
        swapped = jnp.stack([theirs, own], axis=1).astype(f32)
        grads_w = jnp.where(sub == 0, pair, swapped)

    across = 128 * count
    mixed = summed[0][:, 3 * across :]
    grad_qkv = jnp.concatenate(
        [
            part[:, index * across : (index + 1) * across]
            for index in range(3)
            for part in summed
        ],
        axis=1,
    )
    grad_gain = jnp.sum(grad_qkv * mix_qkv.astype(f32), axis=1) / gain_mix.astype(f32)
    all_ids = EXPERTS + ZEROS
    return (
        block_out,
        token_grad,
        logit_grad.T,
        grad_gain,
        grad_qkv,
        mixed[:, :width],
        mixed[:, width + 15],
        mixed[:, width : width + all_ids],
        mixed[:, width + 12 : width + 14],
        grads_w[0],
        grads_w[1],
        grads_w[2],
    )


def solution(mesh):
    depth = mesh.shape["expert"]
    here = EXPERTS // depth
    chips = mesh.shape["shard"] // here
    fine = Mesh(mesh.devices.reshape(depth, chips, here), ("expert", "chip", "sub"))
    shard = ("chip", "sub")
    by_token = P(("expert", "chip", "sub"), None)
    weights = P("expert", None, shard)
    mixer = (P(shard), P(shard, None), P(shard, None), P(shard), P(shard, None), P(shard, None))
    in_specs = (by_token,) * 5 + mixer + (weights,) * 3
    out_specs = (by_token,) * 3 + mixer + (weights,) * 3
    return jax.shard_map(
        local, mesh=fine, in_specs=in_specs, out_specs=out_specs, check_vma=False
    )
```

time: 1150 us -> 414 us (0.36)
  matrix products: 319 us -> 0 us
  waiting for transfers between devices: 358 us -> 69.5 us
  Pallas kernels: 0 us -> 221 us
  local copies, waits for them, and re-layouts: 203 us -> 27.3 us
  other arithmetic: 166 us -> 15.5 us
  blocking collectives: 55 us -> 0 us
  starting transfers between devices: 18.5 us -> 57.3 us
    dot_general x33 -> x0, matrix products: 319 us -> none  [the longest x4 47.2 us: block_scores(): jnp.einsum('qhd,khd->hqk', query_block, keys_rot, preferred_element_type=...]
    pallas_call x0 -> x28, Pallas kernels: none -> 221 us  [the longest x3 64 us: expert_rows(): pl.pallas_call(functools.partial(expert_body, group, chained), grid=(bloc...]
    reduce_scatter x3 -> x1, waiting for transfers between devices: 161 us -> 0.01 us  [local(): grads_w = lax.psum_scatter(grads_w, 'chip', scatter_dimension=0, tiled=True)]
    all_to_all x4 -> x2, waiting for transfers between devices: 135 us -> 0.01 us  [exchange(): lax.all_to_all(value, ('expert', 'sub'), split_axis=0, concat_axis=0, til...]
    gather x11 -> x0, local copies, waits for them, and re-layouts: 75.7 us -> none  [the longest x5 20.4 us: local(): chosen = jnp.take_along_axis(logits, routes, axis=1)]
    reduce_sum x9 -> x1, other arithmetic: 73.1 us -> 1.35 us  [local(): jnp.sum(grad_qkv * mix_qkv.astype(f32), axis=1) / gain_mix.astype(f32)]
    ppermute x0 -> x38, waiting for transfers between devices: none -> 69.5 us  [the longest x14 36.2 us: partner(): return lax.ppermute(value, ('expert', 'chip', 'sub'), moves)]
    convert_element_type x17 -> x4, other arithmetic: 56.2 us -> 4.5 us  [over_planes(): low = total.astype(bf16)]
  transfers between devices with their start and end apart: 15 -> 42, of which waited for: 8 -> 12; matrix products, arithmetic and copies ran while one was open for 36% -> 6% of each run, Pallas kernels for 0% -> 55%
where the time goes in v1:
time: 414 us; the launch traced here: 406 us
  Pallas kernels  221 us (53%)
  waiting for transfers between devices  69.5 us (17%)
  starting transfers between devices  57.3 us (14%)
  local copies, waits for them, and re-layouts  27.3 us (7%)
  other arithmetic  15.5 us (4%)
  between operations  14.8 us (4%)
    pallas_call x3, Pallas kernels, expert_rows(): pl.pallas_call(functools.partial(expert_body, group, chained), grid=(bloc...  64 us
    ppermute x14, waiting for transfers between devices, partner(): return lax.ppermute(value, ('expert', 'chip', 'sub'), moves)  36.2 us
    pallas_call x2, Pallas kernels, attend_back(): pl.pallas_call(attend_back_body, grid=(count,), in_specs=[SCALAR] + [pair...  34.6 us
    pallas_call x2, Pallas kernels, expert_weights(): pl.pallas_call(functools.partial(weights_body, tuple((deep // SLOTS for d...  34.5 us
    ppermute x24, waiting for transfers between devices, trade(): return lax.ppermute(value, axis, [(i, i ^ index) for i in range(size)])  33.3 us
    ppermute x24, starting transfers between devices, trade(): return lax.ppermute(value, axis, [(i, i ^ index) for i in range(size)])  30.6 us
    pallas_call x1, Pallas kernels, come_back(): pl.pallas_call(return_body, grid=(steps,), in_specs=[SCALAR, rows(TILE, 8...  19.4 us
    pallas_call x1, Pallas kernels, attend(): pl.pallas_call(attend_body, grid=(PAIRS,), in_specs=[pair] * 3, out_specs...  18.2 us
  transfers between devices with their start and end apart: 42, of which 12 were waited for; matrix products, arithmetic and copies ran while one was open for 6% of the time, Pallas kernels for 55%

profile of v1, /device:TPU:1, one launch (start us, length us, event | category | flops | bytes accessed | tf_op | source)
XLA Modules:
  0.0 405.7 jit_solution(13080395553659945779)
XLA Ops:
  9.3 2.7 collective-permute-done.1
  14.7 2.4 collective-permute-start.2
  21.8 7.7 %place.1 = (s32[8,1024]{1,0:T(8,128)}, s32[1024,8]{1,0:T(8,128)}, bf16[8,224,768]{2,1,0:T(8,128)(2,1)}) custom-call(s32[2,1024]{1,0:T(2,128)} %bitcast.104, s32[2,1024]{1,0:T(2,128)} %bitcast.100, bf16[1024,768]{1,0:T(8,128)(2,1)} %cot_ref.5), custom_call_target="tpu_custom_call" | custom-call | flops 8455716864 | bytes 14155776 | tf_op jit(solution)/shard_map/place/pallas_call | solution.py:165
  29.5 4.0 collective-permute-done.2.refs_0_
  40.5 3.3 collective-permute-start.7
  43.8 5.6 %all-to-all-start = ((bf16[8,224,768]{2,1,0:T(8,128)(2,1)}), bf16[8,224,768]{2,1,0:T(8,128)(2,1)}, u32[]{:S(2)}, u32[]{:S(2)}) async-start(bf16[8,224,768]{2,1,0:T(8,128)(2,1)} %get-tuple-element.100), calls=%async_computation | async-start | bytes 5505024 | tf_op jit(solution)/shard_map/all_to_all | solution.py:1151
  50.6 3.2 collective-permute-start.8
  53.9 3.8 collective-permute-start.9
  59.6 10.2 %project.1 = (bf16[1024,768]{1,0:T(8,128)(2,1)}, bf16[1024,768]{1,0:T(8,128)(2,1)}, bf16[1024,768]{1,0:T(8,128)(2,1)}, bf16[1024,768]{1,0:T(8,128)(2,1)}, f32[16...) custom-call(s32[10]{0:T(128)} %stack.84.where_ref, bf16[1024,768]{1,0:T(8,128)(2,1)} %tokens_ref.5, ...), custom_call_target="tpu_custom_call" | custom-call | flops 10871635968 | bytes 37748736 | tf_op jit(solution)/shard_map/project/pallas_call | solution.py:284
  69.8 18.2 %attend.1 = (bf16[1024,768]{1,0:T(8,128)(2,1)}, f32[6,2,1024]{2,1,0:T(2,128)}) custom-call(bf16[1024,768]{1,0:T(8,128)(2,1)} %get-tuple-element.79.q_ref, bf16[1024,768]{1,0:T(8,128)(2,1)} %get-tuple-element.80.k_ref, bf16[1024,768]{1,0:T(8,128)(2,1)} %get-tuple-element.81.v_ref), custom_call_target="tpu_custom_call" | custom-call | flops 19327352832 | bytes 18874368 | tf_op jit(solution)/shard_map/attend/pallas_call | solution.py:343
  87.9 13.6 %mix.1 = (f32[1024,768]{1,0:T(8,128)}, bf16[1024,768]{1,0:T(8,128)(2,1)}, f32[8,1024]{1,0:T(8,128)}, f32[16,1024]{1,0:T(8,128)}, bf16[224,768]{1,0:T(8,128)(2,1)...) custom-call(s32[1]{0:T(128)} %bitcast.2.mine_ref, ...), custom_call_target="tpu_custom_call" | custom-call | flops 12079595520 | bytes 42467328 | tf_op jit(solution)/shard_map/mix/pallas_call | solution.py:478
  103.8 15.8 %collective-permute-done.11.refs_5_.refs_2_ = bf16[224,768]{1,0:T(8,128)(2,1)S(1)} collective-permute-done((bf16[224,768]{1,0:T(8,128)(2,1)}, bf16[224,768]{1,0:T(8,128)(2,1)S(1)}, u32[]{:S(2)}, u32[]{:S(2)}) %collective-permute-start.11) | collective-permute-done | bytes 344096 | tf_op jit(solution)/shard_map/ppermute | solution.py:1145
  119.6 7.3 %collective-permute-done.12.refs_6_.refs_3_ = bf16[224,768]{1,0:T(8,128)(2,1)S(1)} collective-permute-done((bf16[224,768]{1,0:T(8,128)(2,1)}, bf16[224,768]{1,0:T(8,128)(2,1)S(1)}, u32[]{:S(2)}, u32[]{:S(2)}) %collective-permute-start.12) | collective-permute-done | bytes 344096 | tf_op jit(solution)/shard_map/ppermute | solution.py:1145
  127.6 2.9 collective-permute-start.14
  133.8 27.5 %expert_rows.3 = (bf16[896,2048]{1,0:T(8,128)(2,1)}, bf16[896,2048]{1,0:T(8,128)(2,1)}, bf16[896,2048]{1,0:T(8,128)(2,1)}, bf16[896,768]{1,0:T(8,128)(2,1)}, bf1...) custom-call(s32[1]{0:T(128)} %bitcast.2.mine_ref, ...), custom_call_target="tpu_custom_call" | custom-call | flops 169114337280 | bytes 204472320 | tf_op jit(solution)/shard_map/expert_rows/pallas_call | solution.py:631
  161.8 5.6 %collective-permute-done.13.refs_0_.refs_4_ = bf16[224,768]{1,0:T(8,128)(2,1)} collective-permute-done((bf16[224,768]{1,0:T(8,128)(2,1)}, bf16[224,768]{1,0:T(8,128)(2,1)}, u32[]{:S(2)}, u32[]{:S(2)}) %collective-permute-start.13) | collective-permute-done | bytes 344096 | tf_op jit(solution)/shard_map/ppermute | solution.py:1145
  167.4 7.4 %collective-permute-done.14.refs_1_.refs_5_ = bf16[224,768]{1,0:T(8,128)(2,1)} collective-permute-done((bf16[224,768]{1,0:T(8,128)(2,1)}, bf16[224,768]{1,0:T(8,128)(2,1)}, u32[]{:S(2)}, u32[]{:S(2)}) %collective-permute-start.14) | collective-permute-done | bytes 344096 | tf_op jit(solution)/shard_map/ppermute | solution.py:1145
  174.8 18.3 %expert_rows.4 = (bf16[448,2048]{1,0:T(8,128)(2,1)}, bf16[448,2048]{1,0:T(8,128)(2,1)}, bf16[448,2048]{1,0:T(8,128)(2,1)}, bf16[448,768]{1,0:T(8,128)(2,1)}, bf1...) custom-call(s32[1]{0:T(128)} %bitcast.2.mine_ref, ...), custom_call_target="tpu_custom_call", output_to_operand_aliasing={{4}: (5, {})} | custom-call | flops 84557168640 | bytes 149422080 | tf_op jit(solution)/shard_map/expert_rows/pallas_call | solution.py:631
  193.2 2.5 collective-permute-start.20
  196.9 18.2 %expert_rows.5 = (bf16[448,2048]{1,0:T(8,128)(2,1)}, bf16[448,2048]{1,0:T(8,128)(2,1)}, bf16[448,2048]{1,0:T(8,128)(2,1)}, bf16[448,768]{1,0:T(8,128)(2,1)}, bf1...) custom-call(s32[1]{0:T(128)} %bitcast.2.mine_ref, ...), custom_call_target="tpu_custom_call", output_to_operand_aliasing={{4}: (5, {})} | custom-call | flops 84557168640 | bytes 149422080 | tf_op jit(solution)/shard_map/expert_rows/pallas_call | solution.py:631
  215.2 14.7 %expert_weights.2.refs_20_.refs_4_ = bf16[8,3,768,256]{3,2,1,0:T(8,128)(2,1)} custom-call(bf16[224,768]{1,0:T(8,128)(2,1)} %get-tuple-element.88.refs_0_, bf16[224,768]{1,0:T(8,128)(2,1)} %copy-done.2, bf16[224,768]{1,0:T(8,128)(2,1)} %copy-done.3, bf16[224,768]{1,0:T(8,128)(2,1)} %copy-done.4, bf16[224,768]{1,0:T(8,128)(2,1)} %collective-permute-done.13.refs_0_.refs_4_, ...), custom_call_target="tpu_custom_call" | custom-call | flops 63417876 | bytes 117964 | tf_op jit(solution)/shard_map/expert_weights/pallas_call | solution.py:704
  236.3 19.9 %expert_weights.3.refs_1_ = bf16[8,3,768,256]{3,2,1,0:T(8,128)(2,1)} custom-call(bf16[224,768]{1,0:T(8,128)(2,1)} %get-tuple-element.88.refs_0_, bf16[224,768]{1,0:T(8,128)(2,1)} %copy-done.2, bf16[224,768]{1,0:T(8,128)(2,1)} %copy-done.3, bf16[224,768]{1,0:T(8,128)(2,1)} %copy-done.4, ...), custom_call_target="tpu_custom_call", output_to_operand_aliasing={{}: (20, {})} | custom-call | flops 105696464 | bytes 196608 | tf_op jit(solution)/shard_map/expert_weights/pallas_call | solution.py:704
  256.2 5.1 %all-to-all-start.1 = ((bf16[8,224,768]{2,1,0:T(8,128)(2,1)}), bf16[8,224,768]{2,1,0:T(8,128)(2,1)}, u32[]{:S(2)}, u32[]{:S(2)}) async-start(bf16[8,224,768]{2,1,0:T(8,128)(2,1)} %get-tuple-element.135), calls=%async_computation.1 | async-start | bytes 5505024 | tf_op jit(solution)/shard_map/all_to_all | solution.py:1151
  262.1 19.4 %come_back.1 = (f32[12,1024]{1,0:T(8,128)}, f32[1024,768]{1,0:T(8,128)}, bf16[1024,768]{1,0:T(8,128)(2,1)}, f32[6,2,1024]{2,1,0:T(2,128)}, bf16[4,1,96,896]{3,2,...) custom-call(s32[3]{0:T(128)} %pad_add_fusion.place_ref, s32[1024,8]{1,0:T(8,128)} %get-tuple-element.77.tcol_ref, ...), custom_call_target="tpu_custom_call" | custom-call | flops 157034741760 | bytes 424673280 | tf_op jit(solution)/shard_map/come_back/pallas_call | solution.py:869
  281.8 17.2 %attend_back.2 = (bf16[1024,1152]{1,0:T(8,128)(2,1)}, bf16[4,3,96,384]{3,2,1,0:T(8,128)(2,1)}, bf16[4,3,96,384]{3,2,1,0:T(8,128)(2,1)}) custom-call(s32[3]{0:T(128)} %pad_add_fusion.place_ref, bf16[1024,768]{1,0:T(8,128)(2,1)} %get-tuple-element.79.q_ref, bf16[1024,768]{1,0:T(8,128)(2,1)} %get-tuple-element.80.k_ref, ...), custom_call_target="tpu_custom_call" | custom-call | flops 104689824 | bytes 55050 | tf_op jit(solution)/shard_map/attend_back/pallas_call | solution.py:1007
  307.2 17.4 %attend_back.3 = (bf16[1024,1152]{1,0:T(8,128)(2,1)}, bf16[4,3,96,384]{3,2,1,0:T(8,128)(2,1)}, bf16[4,3,96,384]{3,2,1,0:T(8,128)(2,1)}) custom-call(s32[3]{0:T(128)} %pad_add_fusion.place_ref, bf16[1024,768]{1,0:T(8,128)(2,1)} %get-tuple-element.79.q_ref, bf16[1024,768]{1,0:T(8,128)(2,1)} %get-tuple-element.80.k_ref, ...), custom_call_target="tpu_custom_call" | custom-call | flops 104689824 | bytes 55050 | tf_op jit(solution)/shard_map/attend_back/pallas_call | solution.py:1007
  326.3 6.0 %collective-permute-done.29 = bf16[96,2048]{1,0:T(8,128)(2,1)S(1)} collective-permute-done((bf16[96,2048]{1,0:T(8,128)(2,1)S(1)}, bf16[96,2048]{1,0:T(8,128)(2,1)S(1)}, u32[]{:S(2)}, u32[]{:S(2)}) %collective-permute-start.29) | collective-permute-done | bytes 393248 | tf_op jit(solution)/shard_map/ppermute | solution.py:1148
  339.2 4.8 %collective-permute-done.30 = bf16[96,2048]{1,0:T(8,128)(2,1)S(1)} collective-permute-done((bf16[96,2048]{1,0:T(8,128)(2,1)S(1)}, bf16[96,2048]{1,0:T(8,128)(2,1)S(1)}, u32[]{:S(2)}, u32[]{:S(2)}) %collective-permute-start.30) | collective-permute-done | bytes 393248 | tf_op jit(solution)/shard_map/ppermute | solution.py:1148
  349.0 10.7 %tokens_grad.1.refs_1_ = f32[1024,768]{1,0:T(8,128)} custom-call(bf16[1024,1152]{1,0:T(8,128)(2,1)} %get-tuple-element.137.first_ref, bf16[1024,1152]{1,0:T(8,128)(2,1)} %get-tuple-element.138.refs_1_.second_ref, bf16[768,2432]{1,0:T(8,128)(2,1)} %get-tuple-element.139.weight_ref, bf16[1024,768]{1,0:T(8,128)(2,1)} %tokens_ref.5, ...), custom_call_target="tpu_custom_call" | custom-call | flops 36238784 | bytes 125829 | tf_op jit(solution)/shard_map/tokens_grad/pallas_call | solution.py:1055
  362.7 8.3 %output.1.refs_1_ = bf16[1024,768]{1,0:T(8,128)(2,1)} custom-call(s32[1024,8]{1,0:T(8,128)} %get-tuple-element.77.tcol_ref, f32[8,1024]{1,0:T(8,128)} %get-tuple-element.85.gates_ref, f32[16,768]{1,0:T(8,128)} %get-tuple-element.84.small_ref, f32[1024,768]{1,0:T(8,128)} %after.22.residual_ref, bf16[1024,768]{1,0:T(8,128)(2,1)} %get-tuple-element.118.normed_ref, ...), custom_call_target="tpu_custom_call" | custom-call | flops 28185722 | bytes 94371 | tf_op jit(solution)/shard_map/output/pallas_call | solution.py:1092
  374.5 12.5 %collective-permute-done.36 = bf16[96,1152]{1,0:T(8,128)(2,1)S(1)} collective-permute-done((bf16[96,1152]{1,0:T(8,128)(2,1)S(1)}, bf16[96,1152]{1,0:T(8,128)(2,1)S(1)}, u32[]{:S(2)}, u32[]{:S(2)}) %collective-permute-start.36) | collective-permute-done | bytes 221216 | tf_op jit(solution)/shard_map/ppermute | solution.py:1148
  388.0 2.8 slice_bitcast_fusion.4
  (210 shorter events, 71.9 us)
Async XLA Ops:
  7.2 126.6 %all-gather.2.cloned.1.call-start = ((), (), s32[]{:S(2)}) async-start(), calls=%async_computation.3 | async-start | bytes 11796480 | tf_op jit(solution)/shard_map/all_gather | solution.py:1180
  14.7 18.8 %collective-permute-start.2 = (bf16[96,3200]{1,0:T(8,128)(2,1)S(1)}, bf16[96,3200]{1,0:T(8,128)(2,1)S(1)}, u32[]{:S(2)}, u32[]{:S(2)}) collective-permute-start(bf16[96,3200]{1,0:T(8,128)(2,1)S(1)} %fusion.3.rest_0_), channel_id=1, source_target_pairs={{0,4},{2,6},{4,0},{6,2},{1,5},{3,7},{5,1},{7,3},{8,12},{10,14},{12... | collective-permute-start | bytes 1843208 | tf_op jit(solution)/shard_map/ppermute | solution.py:1148
  17.2 19.3 %collective-permute-start = (bf16[96,3200]{1,0:T(8,128)(2,1)S(1)}, bf16[96,3200]{1,0:T(8,128)(2,1)S(1)}, u32[]{:S(2)}, u32[]{:S(2)}) collective-permute-start(bf16[96,3200]{1,0:T(8,128)(2,1)S(1)} %fusion.3.rest_0_), channel_id=1, source_target_pairs={{0,2},{2,0},{4,6},{6,4},{1,3},{3,1},{5,7},{7,5},{8,10},{10,8},{12,... | collective-permute-start | bytes 1843208 | tf_op jit(solution)/shard_map/ppermute | solution.py:1148
  18.4 39.9 %collective-permute-start.5 = (bf16[96,3200]{1,0:T(8,128)(2,1)S(1)}, bf16[96,3200]{1,0:T(8,128)(2,1)S(1)}, u32[]{:S(2)}, u32[]{:S(2)}) collective-permute-start(bf16[96,3200]{1,0:T(8,128)(2,1)S(1)} %fusion.3.rest_0_), channel_id=1, source_target_pairs={{0,1},{1,0},{2,3},{3,2},{4,5},{5,4},{6,7},{7,6},{8,9},{9,8},{10,11... | collective-permute-start | bytes 1843208 | tf_op jit(solution)/shard_map/ppermute | solution.py:1148
  35.3 15.3 %collective-permute-start.3 = (bf16[48,3200]{1,0:T(8,128)(2,1)S(1)}, bf16[48,3200]{1,0:T(8,128)(2,1)S(1)}, u32[]{:S(2)}, u32[]{:S(2)}) collective-permute-start(bf16[48,3200]{1,0:T(8,128)(2,1)S(1)} %slice.169), channel_id=1, source_target_pairs={{0,2},{2,0},{4,6},{6,4},{1,3},{3,1},{5,7},{7,5},{8,10},{10,8},{12,... | collective-permute-start | bytes 921608 | tf_op jit(solution)/shard_map/ppermute | solution.py:1148
  38.3 15.6 %collective-permute-start.4 = (bf16[48,3200]{1,0:T(8,128)(2,1)S(1)}, bf16[48,3200]{1,0:T(8,128)(2,1)S(1)}, u32[]{:S(2)}, u32[]{:S(2)}) collective-permute-start(bf16[48,3200]{1,0:T(8,128)(2,1)S(1)} %slice.170), channel_id=1, source_target_pairs={{0,4},{2,6},{4,0},{6,2},{1,5},{3,7},{5,1},{7,3},{8,12},{10,14},{12... | collective-permute-start | bytes 921608 | tf_op jit(solution)/shard_map/ppermute | solution.py:1148
  40.5 17.8 %collective-permute-start.7 = (bf16[96,3200]{1,0:T(8,128)(2,1)S(1)}, bf16[96,3200]{1,0:T(8,128)(2,1)}, u32[]{:S(2)}, u32[]{:S(2)}) collective-permute-start(bf16[96,3200]{1,0:T(8,128)(2,1)S(1)} %copy-done.10), channel_id=1, source_target_pairs={{0,1},{1,0},{2,3},{3,2},{4,5},{5,4},{6,7},{7,6},{8,9},{9,8},{10,11... | collective-permute-start | bytes 1843208 | tf_op jit(solution)/shard_map/ppermute | solution.py:1148
  43.8 15.1 %collective-permute-start.6 = (bf16[96,3200]{1,0:T(8,128)(2,1)}, bf16[96,3200]{1,0:T(8,128)(2,1)}, u32[]{:S(2)}, u32[]{:S(2)}) collective-permute-start(bf16[96,3200]{1,0:T(8,128)(2,1)} %after.12.rest_1_), channel_id=1, source_target_pairs={{0,1},{1,0},{2,3},{3,2},{4,5},{5,4},{6,7},{7,6},{8,9},{9,8},{10,11... | collective-permute-start | bytes 1843208 | tf_op jit(solution)/shard_map/ppermute | solution.py:1148
  43.8 90.0 %all-to-all-start = ((bf16[8,224,768]{2,1,0:T(8,128)(2,1)}), bf16[8,224,768]{2,1,0:T(8,128)(2,1)}, u32[]{:S(2)}, u32[]{:S(2)}) async-start(bf16[8,224,768]{2,1,0:T(8,128)(2,1)} %get-tuple-element.100), calls=%async_computation | async-start | bytes 5505024 | tf_op jit(solution)/shard_map/all_to_all | solution.py:1151
  49.5 338.6 %reduce-scatter.2.cloned.1.call-start = ((), (), s32[]{:S(2)}) async-start(), calls=%async_computation.4 | async-start | bytes 11796480 | tf_op jit(solution)/shard_map/reduce_scatter | solution.py:1256
  102.0 17.6 %collective-permute-start.11 = (bf16[224,768]{1,0:T(8,128)(2,1)}, bf16[224,768]{1,0:T(8,128)(2,1)S(1)}, u32[]{:S(2)}, u32[]{:S(2)}) collective-permute-start(bf16[224,768]{1,0:T(8,128)(2,1)} %get-tuple-element.90), channel_id=1, source_target_pairs={{0,8},{2,10},{4,12},{6,14},{1,9},{3,11},{5,13},{7,15},{8,0},{10,2}... | collective-permute-start | bytes 1032200 | tf_op jit(solution)/shard_map/ppermute | solution.py:1145
  103.1 23.7 %collective-permute-start.12 = (bf16[224,768]{1,0:T(8,128)(2,1)}, bf16[224,768]{1,0:T(8,128)(2,1)S(1)}, u32[]{:S(2)}, u32[]{:S(2)}) collective-permute-start(bf16[224,768]{1,0:T(8,128)(2,1)} %get-tuple-element.91), channel_id=1, source_target_pairs={{0,9},{2,11},{4,13},{6,15},{1,8},{3,10},{5,12},{7,14},{8,1},{10,3}... | collective-permute-start | bytes 1032200 | tf_op jit(solution)/shard_map/ppermute | solution.py:1145
  127.6 39.8 %collective-permute-start.13 = (bf16[224,768]{1,0:T(8,128)(2,1)}, bf16[224,768]{1,0:T(8,128)(2,1)}, u32[]{:S(2)}, u32[]{:S(2)}) collective-permute-start(bf16[224,768]{1,0:T(8,128)(2,1)} %get-tuple-element.96), channel_id=1, source_target_pairs={{0,16},{2,18},{4,20},{6,22},{1,17},{3,19},{5,21},{7,23},{8,24},{10... | collective-permute-start | bytes 1032200 | tf_op jit(solution)/shard_map/ppermute | solution.py:1145
  127.6 47.2 %collective-permute-start.14 = (bf16[224,768]{1,0:T(8,128)(2,1)}, bf16[224,768]{1,0:T(8,128)(2,1)}, u32[]{:S(2)}, u32[]{:S(2)}) collective-permute-start(bf16[224,768]{1,0:T(8,128)(2,1)} %get-tuple-element.97), channel_id=1, source_target_pairs={{0,17},{2,19},{4,21},{6,23},{1,16},{3,18},{5,20},{7,22},{8,25},{10... | collective-permute-start | bytes 1032200 | tf_op jit(solution)/shard_map/ppermute | solution.py:1145
  130.5 66.4 %collective-permute-start.15 = (bf16[224,768]{1,0:T(8,128)(2,1)}, bf16[224,768]{1,0:T(8,128)(2,1)}, u32[]{:S(2)}, u32[]{:S(2)}) collective-permute-start(bf16[224,768]{1,0:T(8,128)(2,1)} %get-tuple-element.98), channel_id=1, source_target_pairs={{0,24},{2,26},{4,28},{6,30},{1,25},{3,27},{5,29},{7,31},{8,16},{10... | collective-permute-start | bytes 1032200 | tf_op jit(solution)/shard_map/ppermute | solution.py:1145
  131.5 65.4 %collective-permute-start.16 = (bf16[224,768]{1,0:T(8,128)(2,1)}, bf16[224,768]{1,0:T(8,128)(2,1)}, u32[]{:S(2)}, u32[]{:S(2)}) collective-permute-start(bf16[224,768]{1,0:T(8,128)(2,1)} %get-tuple-element.99), channel_id=1, source_target_pairs={{0,25},{2,27},{4,29},{6,31},{1,24},{3,26},{5,28},{7,30},{8,17},{10... | collective-permute-start | bytes 1032200 | tf_op jit(solution)/shard_map/ppermute | solution.py:1145
  161.3 31.9 %collective-permute-start.17 = (bf16[224,768]{1,0:T(8,128)(2,1)}, bf16[224,768]{1,0:T(8,128)(2,1)S(1)}, u32[]{:S(2)}, u32[]{:S(2)}) collective-permute-start(bf16[224,768]{1,0:T(8,128)(2,1)} %get-tuple-element.105), channel_id=1, source_target_pairs={{0,1},{2,3},{4,5},{6,7},{1,0},{3,2},{5,4},{7,6},{8,9},{10,11},{12,... | collective-permute-start | bytes 1032200 | tf_op jit(solution)/shard_map/ppermute | solution.py:1145
  167.4 28.2 %collective-permute-start.18 = (bf16[224,768]{1,0:T(8,128)(2,1)}, bf16[224,768]{1,0:T(8,128)(2,1)S(1)}, u32[]{:S(2)}, u32[]{:S(2)}) collective-permute-start(bf16[224,768]{1,0:T(8,128)(2,1)} %get-tuple-element.106), channel_id=1, source_target_pairs={{0,8},{2,10},{4,12},{6,14},{1,9},{3,11},{5,13},{7,15},{8,0},{10,2}... | collective-permute-start | bytes 1032200 | tf_op jit(solution)/shard_map/ppermute | solution.py:1145
  174.8 21.4 %collective-permute-start.19 = (bf16[224,768]{1,0:T(8,128)(2,1)}, bf16[224,768]{1,0:T(8,128)(2,1)S(1)}, u32[]{:S(2)}, u32[]{:S(2)}) collective-permute-start(bf16[224,768]{1,0:T(8,128)(2,1)} %get-tuple-element.107), channel_id=1, source_target_pairs={{0,9},{2,11},{4,13},{6,15},{1,8},{3,10},{5,12},{7,14},{8,1},{10,3}... | collective-permute-start | bytes 1032200 | tf_op jit(solution)/shard_map/ppermute | solution.py:1145
  193.2 36.7 %collective-permute-start.20 = (bf16[224,768]{1,0:T(8,128)(2,1)}, bf16[224,768]{1,0:T(8,128)(2,1)S(1)}, u32[]{:S(2)}, u32[]{:S(2)}) collective-permute-start(bf16[224,768]{1,0:T(8,128)(2,1)} %get-tuple-element.120), channel_id=1, source_target_pairs={{0,16},{2,18},{4,20},{6,22},{1,17},{3,19},{5,21},{7,23},{8,24},{10... | collective-permute-start | bytes 1032200 | tf_op jit(solution)/shard_map/ppermute | solution.py:1145
  195.6 34.2 %collective-permute-start.21 = (bf16[224,768]{1,0:T(8,128)(2,1)}, bf16[224,768]{1,0:T(8,128)(2,1)S(1)}, u32[]{:S(2)}, u32[]{:S(2)}) collective-permute-start(bf16[224,768]{1,0:T(8,128)(2,1)} %get-tuple-element.121), channel_id=1, source_target_pairs={{0,17},{2,19},{4,21},{6,23},{1,16},{3,18},{5,20},{7,22},{8,25},{10... | collective-permute-start | bytes 1032200 | tf_op jit(solution)/shard_map/ppermute | solution.py:1145
  230.7 30.6 %collective-permute-start.22 = (bf16[224,768]{1,0:T(8,128)(2,1)}, bf16[224,768]{1,0:T(8,128)(2,1)S(1)}, u32[]{:S(2)}, u32[]{:S(2)}) collective-permute-start(bf16[224,768]{1,0:T(8,128)(2,1)} %get-tuple-element.124), channel_id=1, source_target_pairs={{0,24},{2,26},{4,28},{6,30},{1,25},{3,27},{5,29},{7,31},{8,16},{10... | collective-permute-start | bytes 1032200 | tf_op jit(solution)/shard_map/ppermute | solution.py:1145
  232.5 28.9 %collective-permute-start.23 = (bf16[224,768]{1,0:T(8,128)(2,1)}, bf16[224,768]{1,0:T(8,128)(2,1)}, u32[]{:S(2)}, u32[]{:S(2)}) collective-permute-start(bf16[224,768]{1,0:T(8,128)(2,1)} %get-tuple-element.125), channel_id=1, source_target_pairs={{0,25},{2,27},{4,29},{6,31},{1,24},{3,26},{5,28},{7,30},{8,17},{10... | collective-permute-start | bytes 1032200 | tf_op jit(solution)/shard_map/ppermute | solution.py:1145
  256.2 78.6 %all-to-all-start.1 = ((bf16[8,224,768]{2,1,0:T(8,128)(2,1)}), bf16[8,224,768]{2,1,0:T(8,128)(2,1)}, u32[]{:S(2)}, u32[]{:S(2)}) async-start(bf16[8,224,768]{2,1,0:T(8,128)(2,1)} %get-tuple-element.135), calls=%async_computation.1 | async-start | bytes 5505024 | tf_op jit(solution)/shard_map/all_to_all | solution.py:1151
  281.5 17.9 %collective-permute-start.25 = (bf16[4,1,96,896]{3,2,1,0:T(8,128)(2,1)}, bf16[4,1,96,896]{3,2,1,0:T(8,128)(2,1)S(1)}, u32[]{:S(2)}, u32[]{:S(2)}) collective-permute-start(bf16[4,1,96,896]{3,2,1,0:T(8,128)(2,1)} %get-tuple-element.133), channel_id=1, source_target_pairs={{0,1},{1,0},{2,3},{3,2},{4,5},{5,4},{6,7},{7,6},{8,9},{9,8},{10,11... | collective-permute-start | bytes 2064392 | tf_op jit(solution)/shard_map/ppermute | solution.py:1148
  302.8 23.5 %collective-permute-start.27 = (bf16[96,2048]{1,0:T(8,128)(2,1)}, bf16[96,2048]{1,0:T(8,128)(2,1)S(1)}, u32[]{:S(2)}, u32[]{:S(2)}) collective-permute-start(bf16[96,2048]{1,0:T(8,128)(2,1)} %pad_maximum_fusion.4), channel_id=1, source_target_pairs={{0,2},{2,0},{4,6},{6,4},{1,3},{3,1},{5,7},{7,5},{8,10},{10,8},{12,... | collective-permute-start | bytes 1179656 | tf_op jit(solution)/shard_map/ppermute | solution.py:1148
  304.6 21.7 %collective-permute-start.28 = (bf16[96,2048]{1,0:T(8,128)(2,1)}, bf16[96,2048]{1,0:T(8,128)(2,1)S(1)}, u32[]{:S(2)}, u32[]{:S(2)}) collective-permute-start(bf16[96,2048]{1,0:T(8,128)(2,1)} %pad_maximum_fusion.5), channel_id=1, source_target_pairs={{0,4},{2,6},{4,0},{6,2},{1,5},{3,7},{5,1},{7,3},{8,12},{10,14},{12... | collective-permute-start | bytes 1179656 | tf_op jit(solution)/shard_map/ppermute | solution.py:1148
  306.5 25.9 %collective-permute-start.29 = (bf16[96,2048]{1,0:T(8,128)(2,1)S(1)}, bf16[96,2048]{1,0:T(8,128)(2,1)S(1)}, u32[]{:S(2)}, u32[]{:S(2)}) collective-permute-start(bf16[96,2048]{1,0:T(8,128)(2,1)S(1)} %pad_maximum_fusion.3.refs_1_), channel_id=1, source_target_pairs={{0,6},{2,4},{4,2},{6,0},{1,7},{3,5},{5,3},{7,1},{8,14},{10,12},{12... | collective-permute-start | bytes 1179656 | tf_op jit(solution)/shard_map/ppermute | solution.py:1148
  336.4 23.3 %collective-permute-start.31 = (bf16[96,1152]{1,0:T(8,128)(2,1)S(1)}, bf16[96,1152]{1,0:T(8,128)(2,1)S(1)}, u32[]{:S(2)}, u32[]{:S(2)}) collective-permute-start(bf16[96,1152]{1,0:T(8,128)(2,1)S(1)} %bitcast.98), channel_id=1, source_target_pairs={{0,2},{2,0},{4,6},{6,4},{1,3},{3,1},{5,7},{7,5},{8,10},{10,8},{12,... | collective-permute-start | bytes 663560 | tf_op jit(solution)/shard_map/ppermute | solution.py:1148
  336.7 23.0 %collective-permute-start.32 = (bf16[96,1152]{1,0:T(8,128)(2,1)S(1)}, bf16[96,1152]{1,0:T(8,128)(2,1)S(1)}, u32[]{:S(2)}, u32[]{:S(2)}) collective-permute-start(bf16[96,1152]{1,0:T(8,128)(2,1)S(1)} %bitcast.99), channel_id=1, source_target_pairs={{0,4},{2,6},{4,0},{6,2},{1,5},{3,7},{5,1},{7,3},{8,12},{10,14},{12... | collective-permute-start | bytes 663560 | tf_op jit(solution)/shard_map/ppermute | solution.py:1148
  337.3 22.4 %collective-permute-start.33 = (bf16[96,1152]{1,0:T(8,128)(2,1)S(1)}, bf16[96,1152]{1,0:T(8,128)(2,1)S(1)}, u32[]{:S(2)}, u32[]{:S(2)}) collective-permute-start(bf16[96,1152]{1,0:T(8,128)(2,1)S(1)} %bitcast.93), channel_id=1, source_target_pairs={{0,6},{2,4},{4,2},{6,0},{1,7},{3,5},{5,3},{7,1},{8,14},{10,12},{12... | collective-permute-start | bytes 663560 | tf_op jit(solution)/shard_map/ppermute | solution.py:1148
  347.0 24.0 %collective-permute-start.34 = (bf16[96,2048]{1,0:T(8,128)(2,1)S(1)}, bf16[96,2048]{1,0:T(8,128)(2,1)S(1)}, u32[]{:S(2)}, u32[]{:S(2)}) collective-permute-start(bf16[96,2048]{1,0:T(8,128)(2,1)S(1)} %convert_element_type.257), channel_id=1, source_target_pairs={{0,16},{8,24},{16,0},{24,8},{1,17},{9,25},{17,1},{25,9},{2,18},{10... | collective-permute-start | bytes 1179656 | tf_op jit(solution)/shard_map/ppermute | solution.py:1148
  (46 other events, 212.9 us)
Sparse Core Ops, SparseCore 0:
  13.8 109.7 all-gather.1
  256.4 112.1 reduce-scatter.1

commit v2 on v1

--- a/solution.py
+++ b/solution.py
@@ -21,10 +21,11 @@
 SCALAR_ROWS = SLOTS - 16
 GROUPS = ((0, 1, 2, 3), (4, 5), (6, 7))
 TILE = 256
+ROWS = 512
 MIB = 1 << 20
 LIMIT = 60
 WEIGHT = 10
-LIGHT = 3
+LIGHT = 2.6
 LATE = 0.01
 FILL = 0.01
 
@@ -283,10 +284,10 @@
     wide = pieces[0].shape[1] - width
     return pl.pallas_call(
         functools.partial(project_body, tuple(range(count))),
-        grid=(length // TILE,),
-        in_specs=[SCALAR, rows(TILE, width), rows(TILE, 128), rows(TILE, 128)]
+        grid=(length // ROWS,),
+        in_specs=[SCALAR, rows(ROWS, width), rows(ROWS, 128), rows(ROWS, 128)]
         + [WHOLE] * count,
-        out_specs=[rows(TILE, width)] * 4 + [full((16, width)), WHOLE, WHOLE],
+        out_specs=[rows(ROWS, width)] * 4 + [full((16, width)), WHOLE, WHOLE],
         out_shape=[shape((length, width), bf16)] * 4
         + [
             shape((16, width), f32),
@@ -310,27 +311,34 @@
     wide_ref[:, :128] = v_ref[...]
     wide_ref[:, 128:] = jnp.ones((length, 128), bf16)
     lane = iota((BLOCK, 128), 1)
-    for block in range(length // BLOCK):
+
+    def score(block, head):
+        mine = (lane < HEAD) if head == 0 else (lane >= HEAD)
+        query = q_ref[block * BLOCK : (block + 1) * BLOCK, :]
+        query = jnp.where(mine, query, jnp.zeros_like(query))
+        return dot_nt(query, k_ref[: (block + 1) * BLOCK, :])
+
+    items = [(block, head) for block in range(length // BLOCK) for head in range(2)]
+    ahead = score(*items[0])
+    result = None
+    total = None
+    for spot, (block, head) in enumerate(items):
         cut = slice(block * BLOCK, (block + 1) * BLOCK)
         seen = (block + 1) * BLOCK
-        query = q_ref[cut, :]
-        zero = jnp.zeros_like(query)
-        result = None
-        total = None
-        for head in range(2):
-            mine = (lane < HEAD) if head == 0 else (lane >= HEAD)
-            scores = dot_nt(jnp.where(mine, query, zero), k_ref[:seen, :])
-            top = jnp.max(scores, axis=1, keepdims=True)
-            weights = jnp.exp(scores - top).astype(bf16)
-            both = dot_nn(weights, wide_ref[:seen, :])
-            summed = both[:, 128:]
-            out = both[:, :128] / summed
-            log_total = top + jnp.log(summed)
-            if head == 0:
-                result, total = out, log_total
-            else:
-                result = jnp.where(mine, out, result)
-                total = jnp.where(mine, log_total, total)
+        scores = ahead
+        if spot + 1 < len(items):
+            ahead = score(*items[spot + 1])
+        top = jnp.max(scores, axis=1, keepdims=True)
+        weights = jnp.exp(scores - top).astype(bf16)
+        both = dot_nn(weights, wide_ref[:seen, :])
+        summed = both[:, 128:]
+        out = both[:, :128] / summed
+        log_total = top + jnp.log(summed)
+        if head == 0:
+            result, total = out, log_total
+            continue
+        result = jnp.where(lane < HEAD, result, out)
+        total = jnp.where(lane < HEAD, total, log_total)
         out_ref[cut, :] = result.astype(bf16)
         turned = jnp.transpose(total)
         total_ref[0, 0:1, cut] = turned[0:1, :]
@@ -372,25 +380,24 @@
     pieces = rest[:EXPERTS]
     kept, logits_ref, rows_all, sems = rest[EXPERTS:]
     length = kept.shape[0]
-    steps = length // TILE
+    steps = length // ROWS
     step = pl.program_id(0)
 
     @pl.when(step < steps)
     def _():
         residual = tokens_ref[...].astype(f32) + dot_nn(attended_ref[...], weight_ref[...])
-        residual_ref[...] = residual
+        residual_ref[...] = residual.astype(bf16)
         inverse = lax.rsqrt(jnp.mean(residual * residual, axis=1, keepdims=True) + epsilon)
         normed = (residual * inverse * small_ref[15:16, :]).astype(bf16)
         normed_ref[...] = normed
-        kept[pl.ds(pl.multiple_of(step * TILE, TILE), TILE), :] = normed
+        kept[pl.ds(pl.multiple_of(step * ROWS, ROWS), ROWS), :] = normed
         small = small_ref[...].astype(bf16)
         cot = cot_ref[...]
-        high, low = split(cot.astype(f32) * normed.astype(f32))
-        ones = jnp.ones((16, high.shape[1]), bf16)
-        along = dot_nt(ones, high) + dot_nt(ones, low)
+        along = jnp.sum(cot.astype(f32) * normed.astype(f32), axis=1, keepdims=True)
+        along = jnp.transpose(jnp.broadcast_to(along, (ROWS, 128)))[0:16]
         constant = dot_nt(small, cot)
-        line = iota((16, TILE), 0)
-        where = pl.ds(pl.multiple_of(step * TILE, TILE), TILE)
+        line = iota((16, ROWS), 0)
+        where = pl.ds(pl.multiple_of(step * ROWS, ROWS), ROWS)
         zero_ref[:, where] = jnp.where(
             line == EXPERTS + 1,
             along,
@@ -473,8 +480,8 @@
 
 def mix(mine, attended, weight, tokens, cot, small, prev_row, routes_row, trow):
     length, width = tokens.shape
-    steps = length // TILE
-    tile = rows(TILE, width, steps)
+    steps = length // ROWS
+    tile = rows(ROWS, width, steps)
     return pl.pallas_call(
         mix_body,
         grid=(steps + 1,),
@@ -492,7 +499,7 @@
         out_specs=[tile, tile, full((8, length)), full((16, length))]
         + [WHOLE] * EXPERTS,
         out_shape=[
-            shape((length, width), f32),
+            shape((length, width), bf16),
             shape((length, width), bf16),
             shape((8, length), f32),
             shape((16, length), f32),
@@ -556,25 +563,36 @@
             scaled_ref[cut, :] = (gate_col[cut, 0:1] * cot[index].astype(f32)).astype(bf16)
 
     value = rows_all[...]
-    gate = dot_nn(value, weight_ref[0, 0])
-    up = dot_nn(value, weight_ref[0, 1])
-    grad_hidden = dot_nn(scaled_ref[...], weight_ref[0, 2])
-    sigmoid = 1.0 / (1.0 + jnp.exp(-gate))
-    active = gate * sigmoid
-    hidden = (active * up).astype(bf16)
-    grad_up = (grad_hidden * active).astype(bf16)
-    grad_gate = (grad_hidden * up * (sigmoid + active * (1.0 - sigmoid))).astype(bf16)
-    where = pl.ds(pl.multiple_of(step * part, part), part)
-    behind = pl.ds(pl.multiple_of(inner + step * part, part), part)
-    hidden_ref[...] = hidden
-    gate_ref[...] = grad_gate
-    up_ref[...] = grad_up
-    hidden_all[:, where] = hidden
-    grads_all[:, where] = grad_gate
-    grads_all[:, behind] = grad_up
-    in_all[:, where] = weight_ref[0, 0]
-    in_all[:, behind] = weight_ref[0, 1]
-    down_all[:, where] = weight_ref[0, 2]
+    scaled = scaled_ref[...]
+    several = weight_ref.shape[0]
+    part = part // several
+    products = [
+        (
+            dot_nn(value, weight_ref[index, 0]),
+            dot_nn(value, weight_ref[index, 1]),
+            dot_nn(scaled, weight_ref[index, 2]),
+        )
+        for index in range(several)
+    ]
+    for index, (gate, up, grad_hidden) in enumerate(products):
+        sigmoid = 1.0 / (1.0 + jnp.exp(-gate))
+        active = gate * sigmoid
+        hidden = (active * up).astype(bf16)
+        grad_up = (grad_hidden * active).astype(bf16)
+        grad_gate = (grad_hidden * up * (sigmoid + active * (1.0 - sigmoid))).astype(bf16)
+        own = slice(index * part, (index + 1) * part)
+        first = (step * several + index) * part
+        where = pl.ds(pl.multiple_of(first, part), part)
+        behind = pl.ds(pl.multiple_of(inner + first, part), part)
+        hidden_ref[:, own] = hidden
+        gate_ref[:, own] = grad_gate
+        up_ref[:, own] = grad_up
+        hidden_all[:, where] = hidden
+        grads_all[:, where] = grad_gate
+        grads_all[:, behind] = grad_up
+        in_all[:, where] = weight_ref[index, 0]
+        in_all[:, behind] = weight_ref[index, 1]
+        down_all[:, where] = weight_ref[index, 2]
 
     @pl.when(step == last)
     def _():
@@ -625,15 +643,16 @@
     inner = blocks * part
     deep = count * SLOTS
     chained = len(sent)
-    block = pl.BlockSpec((deep, part), lambda i: (0, i))
+    several = 2 if blocks % 2 == 0 else 1
+    block = pl.BlockSpec((deep, several * part), lambda i: (0, i))
     wide = shape((deep, inner), bf16)
     piece = full((SLOTS, width))
     return pl.pallas_call(
         functools.partial(expert_body, group, chained),
-        grid=(blocks,),
+        grid=(blocks // several,),
         in_specs=[SCALAR]
         + [piece] * count
-        + [WHOLE, pl.BlockSpec((1, 3, width, part), lambda i: (i, 0, 0, 0))]
+        + [WHOLE, pl.BlockSpec((several, 3, width, part), lambda i: (i, 0, 0, 0))]
         + [WHOLE] * chained,
         out_specs=[block, block, block, full((deep, width)), WHOLE] + [piece] * count,
         out_shape=[wide, wide, wide, shape((deep, width), bf16)]
@@ -657,13 +676,13 @@
     )(mine, *incoming, cotangents, weight, *sent)
 
 
-def weights_body(counts, chained, *refs):
+def weights_body(counts, *refs):
     total = sum(counts)
     groups = len(counts)
     incoming = refs[:total]
     scaled = refs[total : total + groups]
     wide = refs[total + groups : total + 4 * groups]
-    refs = refs[total + 4 * groups + chained :]
+    refs = refs[total + 4 * groups :]
     out_ref = refs[0]
     turned = refs[1:]
     step = pl.program_id(0)
@@ -689,32 +708,30 @@
         out_ref[0, which] = result.astype(bf16)
 
 
-def expert_weights(start, count, incoming, scaled, wide, blocks, made):
+def expert_weights(incoming, scaled, wide, blocks):
     width = incoming[0].shape[1]
-    part = wide[0].shape[1] // blocks
-    inner = count * part
+    inner = wide[0].shape[1]
+    part = inner // blocks
     depths = [block.shape[0] for block in scaled]
     in_specs = [full((SLOTS, width))] * len(incoming)
     in_specs += [full((deep, width)) for deep in depths]
     scratch = []
     for deep in depths:
-        in_specs += [pl.BlockSpec((deep, part), lambda i: (0, i + start))] * 3
+        in_specs += [pl.BlockSpec((deep, part), lambda i: (0, i))] * 3
         scratch += [pltpu.VMEM((width, deep), bf16)] * 2
-    given = (*incoming, *scaled, *wide)
     return pl.pallas_call(
-        functools.partial(weights_body, tuple(deep // SLOTS for deep in depths), len(made)),
-        grid=(count,),
-        in_specs=in_specs + [WHOLE] * len(made),
-        out_specs=pl.BlockSpec((1, 3, width, part), lambda i: (i + start, 0, 0, 0)),
+        functools.partial(weights_body, tuple(deep // SLOTS for deep in depths)),
+        grid=(blocks,),
+        in_specs=in_specs,
+        out_specs=pl.BlockSpec((1, 3, width, part), lambda i: (i, 0, 0, 0)),
         out_shape=shape((blocks, 3, width, part), bf16),
-        input_output_aliases={len(given): 0} if made else {},
         scratch_shapes=scratch,
         compiler_params=params(),
         cost_estimate=cost(
             6 * GROUP * width * inner, 6 * width * inner + 6 * GROUP * inner, FILL
         ),
         name="expert_weights",
-    )(*given, *made)
+    )(*incoming, *scaled, *wide)
 
 
 def dealt(height, parts, width, split_of):
@@ -756,7 +773,7 @@
     width = residual_ref.shape[1]
     id0 = routes_ref[0:1, :]
     id1 = routes_ref[1:2, :]
-    line = iota((16, TILE), 0)
+    line = iota((16, ROWS), 0)
 
     @pl.when(step == 0)
     def _():
@@ -774,7 +791,7 @@
             spot = jnp.where(lane == expert, high, jnp.where(lane == EXPERTS + expert, low, 0.0))
             scalars_all[expert * SLOTS : (expert + 1) * SLOTS, :] = spot.astype(bf16)
 
-    chosen = one_hot((tcol_ref[:, 0:1], tcol_ref[:, 1:2]), 0, GROUP, TILE, 1)
+    chosen = one_hot((tcol_ref[:, 0:1], tcol_ref[:, 1:2]), 0, GROUP, ROWS, 1)
     from_rows = dot_nn(chosen, back_all[...].reshape(GROUP, width))
     scalars = jnp.transpose(dot_nn(chosen, scalars_all[...]))
     through = jnp.concatenate(
@@ -799,14 +816,14 @@
     cot_wide = cot.astype(f32)
     gate_cols = jnp.transpose(gates_ref[...])
     grad_normed += gate_cols[:, 2:3] * cot_wide
-    residual = residual_ref[...]
+    residual = residual_ref[...].astype(f32)
     gain = small_ref[15:16, :]
     inverse = lax.rsqrt(jnp.mean(residual * residual, axis=1, keepdims=True) + epsilon)
     scaled = grad_normed * gain
     spread = jnp.mean(scaled * residual, axis=1, keepdims=True)
     grad_residual = cot_wide + inverse * scaled - residual * (inverse * inverse * inverse * spread)
-    grad_res_ref[...] = grad_residual
     grad_low = grad_residual.astype(bf16)
+    grad_res_ref[...] = grad_low
     grad_att = dot_nt(grad_low, weight_ref[...]).astype(bf16)
     grad_att_ref[...] = grad_att
     attended = attended_ref[...]
@@ -862,8 +879,8 @@
     split_of,
 ):
     length, width = cot.shape
-    steps = length // TILE
-    tile = rows(TILE, width)
+    steps = length // ROWS
+    tile = rows(ROWS, width)
     dims = dealt(width, 1, width + 128, split_of)
     all_ids = EXPERTS + ZEROS
     return pl.pallas_call(
@@ -871,10 +888,10 @@
         grid=(steps,),
         in_specs=[
             SCALAR,
-            rows(TILE, 8),
-            columns(2, TILE),
-            columns(8, TILE),
-            columns(16, TILE),
+            rows(ROWS, 8),
+            columns(2, ROWS),
+            columns(8, ROWS),
+            columns(16, ROWS),
             full(small.shape),
             full(weight.shape),
             tile,
@@ -884,16 +901,16 @@
         ]
         + [WHOLE] * EXPERTS,
         out_specs=[
-            columns(all_ids, TILE),
+            columns(all_ids, ROWS),
             tile,
             tile,
-            pl.BlockSpec((PAIRS, 2, TILE), lambda i: (0, 0, i)),
+            pl.BlockSpec((PAIRS, 2, ROWS), lambda i: (0, 0, i)),
             full(dims),
             full(dims),
         ],
         out_shape=[
             shape((all_ids, length), f32),
-            shape((length, width), f32),
+            shape((length, width), bf16),
             shape((length, width), bf16),
             shape((PAIRS, 2, length), f32),
             shape(dims, bf16),
@@ -941,7 +958,11 @@
     grads_ref,
     keep_ref,
     give_ref,
-    turned,
+    query_turned,
+    grad_turned,
+    key_turned,
+    value_turned,
+    query_sum,
     normed_turned,
     weight_grads,
 ):
@@ -953,43 +974,45 @@
     cosine = cos_ref[...]
     sine = sin_ref[...]
     lane = iota((BLOCK, 128), 1)
-    keys_turned = jnp.transpose(k_ref[...])
-    line = iota((128, BLOCK), 0)
-    for block in range(length // BLOCK):
+    query_turned[...] = jnp.transpose(q_ref[...])
+    grad_turned[...] = jnp.transpose(grad_ref[...])
+    scalars = [total_ref[0], delta_ref[0], jnp.zeros((4, length), f32)]
+    scalars = jnp.transpose(jnp.concatenate(scalars, axis=0))
+
+    def products(block, head):
+        cut = slice(block * BLOCK, (block + 1) * BLOCK)
+        mine = (lane < HEAD) if head == 0 else (lane >= HEAD)
+        key = jnp.where(mine, k_ref[cut, :], jnp.zeros((BLOCK, 128), bf16))
+        value = jnp.where(mine, v_ref[cut, :], jnp.zeros((BLOCK, 128), bf16))
+        scores = dot_nt(q_ref[block * BLOCK :, :], key)
+        return key, scores, dot_nt(grad_ref[block * BLOCK :, :], value)
+
+    items = [(block, head) for block in range(length // BLOCK) for head in range(2)]
+    ahead = products(*items[0])
+    query_term = None
+    for spot, (block, head) in enumerate(items):
         start = block * BLOCK
         cut = slice(start, start + BLOCK)
-        key = k_ref[cut, :]
-        value = v_ref[cut, :]
-        zero = jnp.zeros_like(key)
-        query = q_ref[start:, :]
-        grad = grad_ref[start:, :]
-        grad_key = None
-        grad_value = None
-        for head in range(2):
-            mine = (lane < HEAD) if head == 0 else (lane >= HEAD)
-            scores = dot_nt(jnp.where(mine, key, zero), query)
-            weights = jnp.exp(scores - total_ref[0, head : head + 1, start:])
-            grad_weights = dot_nt(jnp.where(mine, value, zero), grad)
-            grad_scores = weights * (grad_weights - delta_ref[0, head : head + 1, start:])
-            grad_scores = grad_scores.astype(bf16)
-            value_term = dot_nn(weights.astype(bf16), grad)
-            key_term = dot_nn(grad_scores, query)
-            key_mine = (line < HEAD) if head == 0 else (line >= HEAD)
-            key_line = keys_turned[:, cut]
-            query_term = dot_nn(jnp.where(key_mine, key_line, jnp.zeros_like(key_line)), grad_scores)
-            if block == 0 and head == 0:
-                turned[...] = query_term
-            else:
-                turned[:, start:] += query_term
-            if head == 0:
-                grad_key, grad_value = key_term, value_term
-            else:
-                grad_key = jnp.where(mine, key_term, grad_key)
-                grad_value = jnp.where(mine, value_term, grad_value)
-        grad_key = grad_key.astype(bf16).astype(f32)
-        grads_ref[cut, 128:256] = turn(grad_key, cosine[cut], -sine[cut]).astype(bf16)
-        grads_ref[cut, 256:] = grad_value.astype(bf16)
-    grad_query = (jnp.transpose(turned[...]) * 0.125).astype(bf16).astype(f32)
+        line = slice(head * HEAD, (head + 1) * HEAD)
+        key, scores, grad_weights = ahead
+        if spot + 1 < len(items):
+            ahead = products(*items[spot + 1])
+        weights = jnp.exp(scores - scalars[start:, head : head + 1])
+        grad_scores = weights * (grad_weights - scalars[start:, head + 2 : head + 3])
+        grad_scores = grad_scores.astype(bf16)
+        term = dot_nn(grad_scores, key)
+        value_turned[line, cut] = dot_nn(grad_turned[line, start:], weights.astype(bf16))
+        key_turned[line, cut] = dot_nn(query_turned[line, start:], grad_scores)
+        if head == 0:
+            query_term = term
+        elif block == 0:
+            query_sum[...] = query_term + term
+        else:
+            query_sum[start:, :] += query_term + term
+    grad_key = jnp.transpose(key_turned[...]).astype(bf16).astype(f32)
+    grads_ref[:, 128:256] = turn(grad_key, cosine, -sine).astype(bf16)
+    grads_ref[:, 256:] = jnp.transpose(value_turned[...]).astype(bf16)
+    grad_query = (query_sum[...] * 0.125).astype(bf16).astype(f32)
     grads_ref[:, :128] = turn(grad_query, cosine, -sine).astype(bf16)
     weight_grads[...] = dot_nn(normed_turned[...], grads_ref[...]).astype(bf16)
     deal(place_ref, weight_grads, keep_ref, give_ref)
@@ -1013,7 +1036,11 @@
         out_specs=[columns(length, 384), block, block],
         out_shape=[shape((length, 384 * count), bf16), dims, dims],
         scratch_shapes=[
+            pltpu.VMEM((128, length), bf16),
+            pltpu.VMEM((128, length), bf16),
             pltpu.VMEM((128, length), f32),
+            pltpu.VMEM((128, length), f32),
+            pltpu.VMEM((length, 128), f32),
             pltpu.VMEM((width, length), bf16),
             pltpu.VMEM((width, 384), bf16),
         ],
@@ -1045,17 +1072,17 @@
     scaled = grad_normed * small_ref[14:15, :]
     spread_of = jnp.mean(scaled * value, axis=1, keepdims=True)
     grad = inverse * scaled - value * (inverse * inverse * inverse * spread_of)
-    out_ref[...] = grad_res_ref[...] + grad
+    out_ref[...] = grad_res_ref[...].astype(f32) + grad
 
 
 def tokens_grad(grads, weight, tokens, grad_res, small):
     length, width = tokens.shape
-    tile = rows(TILE, width)
+    tile = rows(ROWS, width)
     wide = grads[0].shape[1]
     return pl.pallas_call(
         tokens_grad_body,
-        grid=(length // TILE,),
-        in_specs=[rows(TILE, wide)] * 2
+        grid=(length // ROWS,),
+        in_specs=[rows(ROWS, wide)] * 2
         + [full(weight.shape), tile, tile, full(small.shape)],
         out_specs=tile,
         out_shape=shape((length, width), f32),
@@ -1079,20 +1106,20 @@
     )
     both = jnp.concatenate([high.astype(f32), low.astype(f32)], axis=0).astype(bf16)
     twice = jnp.concatenate([vectors, vectors], axis=0).astype(bf16)
-    total = residual_ref[...] + dot_tn(both, twice)
+    total = residual_ref[...].astype(f32) + dot_tn(both, twice)
     total += gate_cols[:, 2:3] * normed_ref[...].astype(f32)
-    chosen = one_hot((tcol_ref[:, 0:1], tcol_ref[:, 1:2]), 0, GROUP, TILE, 1)
+    chosen = one_hot((tcol_ref[:, 0:1], tcol_ref[:, 1:2]), 0, GROUP, ROWS, 1)
     total += dot_nn(chosen, block_ref[...].reshape(GROUP, block_ref.shape[2]))
     out_ref[...] = total.astype(bf16)
 
 
 def output(tcol, gates, small, residual, normed, block):
     length, width = residual.shape
-    tile = rows(TILE, width)
+    tile = rows(ROWS, width)
     return pl.pallas_call(
         output_body,
-        grid=(length // TILE,),
-        in_specs=[rows(TILE, 8), columns(8, TILE), full(small.shape), tile, tile]
+        grid=(length // ROWS,),
+        in_specs=[rows(ROWS, 8), columns(8, ROWS), full(small.shape), tile, tile]
         + [full((EXPERTS, SLOTS, width))],
         out_specs=tile,
         out_shape=shape((length, width), bf16),
@@ -1100,6 +1127,37 @@
         cost_estimate=cost(2 * GROUP * length * width, 12 * length * width, LATE),
         name="output",
     )(tcol, gates, small, residual, normed, block)
+
+
+def finish_body(low_ref, high_ref, first_ref, weight_ref, gain_ref, out_ref, gain_out):
+    across = low_ref.shape[1] // 3
+    weighted = None
+    for part in range(3):
+        cut = slice(part * across, (part + 1) * across)
+        for half in range(2):
+            if half:
+                grads = low_ref[:, cut].astype(f32) + high_ref[:, cut].astype(f32)
+            else:
+                grads = first_ref[:, cut]
+            place_of = slice((2 * part + half) * across, (2 * part + half + 1) * across)
+            out_ref[:, place_of] = grads
+            term = jnp.sum(grads * weight_ref[:, place_of].astype(f32), axis=1, keepdims=True)
+            weighted = term if weighted is None else weighted + term
+    gain_out[...] = weighted / gain_ref[...]
+
+
+def finish(low, high, first, weight, gain):
+    given = (low, high, first, weight, gain)
+    return pl.pallas_call(
+        finish_body,
+        grid=(1,),
+        in_specs=[full(value.shape) for value in given],
+        out_specs=[full(weight.shape), full(gain.shape)],
+        out_shape=[shape(weight.shape, f32), shape(gain.shape, f32)],
+        compiler_params=params(),
+        cost_estimate=cost(1000, 1000),
+        name="finish",
+    )(*given)
 
 
 def local(
@@ -1213,12 +1271,15 @@
     rows_in = [None] * EXPERTS
     returned = [None] * EXPERTS
     near = GROUPS[0][1:]
-    far = [index for group in GROUPS[1:] for index in group]
     for index in GROUPS[0]:
         rows_in[index] = partner(index, leaving[index])
-    crossing = all_after([leaving[index] for index in far], *[rows_in[index] for index in near])
-    for index, block in zip(far, crossing):
-        rows_in[index] = partner(index, block)
+
+    def cross(group, *others):
+        crossing = all_after([leaving[index] for index in group], *others)
+        for index, block in zip(group, crossing):
+            rows_in[index] = partner(index, block)
+
+    cross(GROUPS[1], *[rows_in[index] for index in near])
 
     sent, scaled, wide, ordered = [], [], [], []
     blocks = weight.shape[0]
@@ -1231,6 +1292,8 @@
         ordered += incoming
         for index, block in zip(group, outs[5:]):
             returned[index] = partner(index, block)
+        if group == GROUPS[0]:
+            cross(GROUPS[2], outs[3], *[rows_in[index] for index in GROUPS[1]])
     group = GROUPS[2]
     incoming = [rows_in[index] for index in group]
     sent[0] = after(sent[0], *[returned[index] for index in near])
@@ -1239,16 +1302,10 @@
     scaled.append(outs[3])
     sent = outs[4]
     ordered += incoming
-    early = 3 * blocks // 8
-    grads_w = [expert_weights(0, early, ordered, scaled, wide, blocks, [])]
-    before = [returned[index] for index in GROUPS[1]] + grads_w
-    for index, block in zip(group, all_after(outs[5:], *before)):
+    grads_w = expert_weights(ordered, scaled, wide, blocks)
+    for index, block in zip(group, outs[5:]):
         returned[index] = partner(index, block)
-    grads_w = expert_weights(
-        early, blocks - early, ordered, scaled, wide, blocks, grads_w
-    )
-    residual_late = after(residual, grads_w)
-    produced = exchange(sent)
+    residual_late = after(residual, grads_w, *[returned[index] for index in GROUPS[1]])
 
     if part < 256:
         grads_w = grads_w.reshape(count // join, 3, width, join, part)
@@ -1271,6 +1328,7 @@
     )
     logit_grad, grad_res, grad_att, delta = outs[:4]
     dealt_out = outs[4:]
+    produced = exchange(after(sent, grad_att))
 
     def flat(block):
         return block.transpose(1, 0, 2).reshape(block.shape[1], -1)
@@ -1297,9 +1355,10 @@
             total += trade(sums[index], "chip", chips, index).astype(f32)
         return total
 
-    def over_planes(total, index):
+    def over_planes(total, index, *beside):
         low = total.astype(bf16)
-        return low.astype(f32) + trade(low, "expert", depth, index).astype(f32)
+        other = trade(low, "expert", depth, index)
+        return after(low, *beside).astype(f32) + other.astype(f32)
 
     def back_through(first, normed):
         return attend_back(
@@ -1323,42 +1382,41 @@
     sums_a = over_cores([dealt_a, dealt_out])
     grads_b, *dealt_b = back_through(count, after(normed_one, sums_a[-1]))
     total_a = over_chips([after(sums_a[0], grads_b), *sums_a[1:]])
-    dealt_b[0] = after(dealt_b[0], produced)
+    dealt_b[1] = after(dealt_b[1], total_a)
     sums_b = over_cores([dealt_b])
-    total_a = after(over_planes(total_a, 1), sums_b[-1])
-    token_grad = tokens_grad([grads_a, grads_b], qkv, tokens, after(grad_res, total_a), small)
-    total_b = over_chips([after(sums_b[0], token_grad), *sums_b[1:]])
-    block_out = output(tcol, gates, small, after(residual, total_b), normed_two, produced)
-    index = 2
-    while index < depth:
-        total_a = over_planes(total_a, index)
-        index *= 2
+    token_grad = tokens_grad([grads_a, grads_b], qkv, tokens, after(grad_res, total_a, sums_b[-1]), small)
+    total_b = over_chips([after(sums_b[0], token_grad, produced), *sums_b[1:]])
+    low_b = total_b.astype(bf16)
+    block_out = output(tcol, gates, small, after(residual, low_b), normed_two, produced)
     index = 1
     while index < depth:
-        total_b = over_planes(total_b, index)
+        total_a = over_planes(total_a, index, token_grad if index == 1 else block_out)
         index *= 2
-    summed = [total_a, total_b]
+    beside = [block_out, total_a]
+    index = 1
+    while index < depth // 2:
+        total_b = over_planes(total_b, index, *beside)
+        beside = []
+        index *= 2
+    low_b = total_b.astype(bf16)
+    high_b = trade(low_b, "expert", depth, index)
 
     if here == 1:
         grads_w = grads_w[0][:, None].astype(f32)
     else:
-        own = grads_w[0]
-        theirs = trade(after(grads_w[1], block_out), "sub", here, 1)
-        pair = jnp.stack([own, theirs], axis=1).astype(f32)
-        swapped = jnp.stack([theirs, own], axis=1).astype(f32)
+        kept = grads_w[0]
+        theirs = trade(after(grads_w[1], low_b), "sub", here, 1)
+        pair = jnp.stack([kept, theirs], axis=1).astype(f32)
+        swapped = jnp.stack([theirs, kept], axis=1).astype(f32)
         grads_w = jnp.where(sub == 0, pair, swapped)
+    grads_w = (grads_w[0], grads_w[1], grads_w[2])
 
     across = 128 * count
-    mixed = summed[0][:, 3 * across :]
-    grad_qkv = jnp.concatenate(
-        [
-            part[:, index * across : (index + 1) * across]
-            for index in range(3)
-            for part in summed
-        ],
-        axis=1,
+    mixed = total_a[:, 3 * across :]
+    grad_qkv, grad_gain = finish(
+        after(low_b, *grads_w), high_b, total_a, mix_qkv, gain_mix.astype(f32)[:, None]
     )
-    grad_gain = jnp.sum(grad_qkv * mix_qkv.astype(f32), axis=1) / gain_mix.astype(f32)
+    grad_gain = grad_gain[:, 0]
     all_ids = EXPERTS + ZEROS
     return (
         block_out,
@@ -1370,9 +1428,7 @@
         mixed[:, width + 15],
         mixed[:, width : width + all_ids],
         mixed[:, width + 12 : width + 14],
-        grads_w[0],
-        grads_w[1],
-        grads_w[2],
+        *grads_w,
     )
 
 

time: 414 us -> 415 us (level)
  starting transfers between devices: 57.3 us -> 72.2 us
  Pallas kernels: 221 us -> 207 us
  waiting for transfers between devices: 69.5 us -> 60.4 us
  other arithmetic: 15.5 us -> 22.7 us
    all_to_all x2, starting transfers between devices: 10.8 us -> 24 us  [exchange(): lax.all_to_all(value, ('expert', 'sub'), split_axis=0, concat_axis=0, til...]
    ppermute x14, waiting for transfers between devices: 36.2 us -> 25.1 us  [partner(): return lax.ppermute(value, ('expert', 'chip', 'sub'), moves)]
    pallas_call x2 -> x1, Pallas kernels: 34.5 us -> 28 us  [expert_weights(): pl.pallas_call(functools.partial(weights_body, tuple((deep // SLOTS for d...]
    all_gather x1, waiting for transfers between devices: 0.01 us -> 5.19 us  [local(): weight = lax.all_gather(mine, 'chip', axis=0, tiled=True)]
    unnamed x81 -> x68, local copies, waits for them, and re-layouts: 13.7 us -> 12.2 us
    pallas_call x3 -> x4, Pallas kernels: 38.4 us -> 39.9 us  [the longest x1 18.5 us: come_back(): pl.pallas_call(return_body, grid=(steps,), in_specs=[SCALAR, rows(ROWS, 8...]
  transfers between devices with their start and end apart: 42 -> 42, of which waited for: 12 -> 13; matrix products, arithmetic and copies ran while one was open for 6% -> 9% of each run, Pallas kernels for 55% -> 50%
where the time goes in v2:
time: 415 us; the launch traced here: 408 us
  Pallas kernels  207 us (50%)
  starting transfers between devices  72.2 us (17%)
  waiting for transfers between devices  60.4 us (15%)
  local copies, waits for them, and re-layouts  30.6 us (7%)
  other arithmetic  22.7 us (5%)
  between operations  14.7 us (4%)
    pallas_call x3, Pallas kernels, expert_rows(): pl.pallas_call(functools.partial(expert_body, group, chained), grid=(bloc...  61.2 us
    pallas_call x2, Pallas kernels, attend_back(): pl.pallas_call(attend_back_body, grid=(count,), in_specs=[SCALAR] + [pair...  33.5 us
    ppermute x24, starting transfers between devices, trade(): return lax.ppermute(value, axis, [(i, i ^ index) for i in range(size)])  31.1 us
    ppermute x24, waiting for transfers between devices, trade(): return lax.ppermute(value, axis, [(i, i ^ index) for i in range(size)])  30.1 us
    pallas_call x1, Pallas kernels, expert_weights(): pl.pallas_call(functools.partial(weights_body, tuple((deep // SLOTS for d...  28 us
    ppermute x14, waiting for transfers between devices, partner(): return lax.ppermute(value, ('expert', 'chip', 'sub'), moves)  25.1 us
    all_to_all x2, starting transfers between devices, exchange(): lax.all_to_all(value, ('expert', 'sub'), split_axis=0, concat_axis=0, til...  24 us
    pallas_call x1, Pallas kernels, come_back(): pl.pallas_call(return_body, grid=(steps,), in_specs=[SCALAR, rows(ROWS, 8...  18.5 us
  transfers between devices with their start and end apart: 42, of which 13 were waited for; matrix products, arithmetic and copies ran while one was open for 9% of the time, Pallas kernels for 50%

profile of v2, /device:TPU:1, one launch (start us, length us, event | category | flops | bytes accessed | tf_op | source)
XLA Modules:
  0.0 408.0 jit_solution(15863739463092719489)
XLA Ops:
  9.3 2.7 collective-permute-done.1
  15.5 2.4 collective-permute-start.2
  21.5 7.7 %place.1 = (s32[8,1024]{1,0:T(8,128)}, s32[1024,8]{1,0:T(8,128)}, bf16[8,224,768]{2,1,0:T(8,128)(2,1)}) custom-call(s32[2,1024]{1,0:T(2,128)} %bitcast.101, s32[2,1024]{1,0:T(2,128)} %bitcast.97, bf16[1024,768]{1,0:T(8,128)(2,1)} %cot_ref.5), custom_call_target="tpu_custom_call" | custom-call | flops 7328287744 | bytes 12268339 | tf_op jit(solution)/shard_map/place/pallas_call | solution.py:166
  29.2 5.9 %all-to-all-start = ((bf16[8,224,768]{2,1,0:T(8,128)(2,1)}), bf16[8,224,768]{2,1,0:T(8,128)(2,1)S(1)}, u32[]{:S(2)}, u32[]{:S(2)}) async-start(bf16[8,224,768]{2,1,0:T(8,128)(2,1)} %get-tuple-element.98), calls=%async_computation | async-start | bytes 5505024 | tf_op jit(solution)/shard_map/all_to_all | solution.py:1209
  42.2 3.4 collective-permute-start.7
  45.6 7.0 %collective-permute-done.3.rest_3_ = bf16[48,3200]{1,0:T(8,128)(2,1)} collective-permute-done((bf16[48,3200]{1,0:T(8,128)(2,1)}, bf16[48,3200]{1,0:T(8,128)(2,1)}, u32[]{:S(2)}, u32[]{:S(2)}) %collective-permute-start.3) | collective-permute-done | bytes 307232 | tf_op jit(solution)/shard_map/ppermute | solution.py:1206
  52.6 3.3 collective-permute-start.8
  55.9 3.7 collective-permute-start.9
  61.2 9.8 %project.1 = (bf16[1024,768]{1,0:T(8,128)(2,1)}, bf16[1024,768]{1,0:T(8,128)(2,1)}, bf16[1024,768]{1,0:T(8,128)(2,1)}, bf16[1024,768]{1,0:T(8,128)(2,1)}, f32[16...) custom-call(s32[10]{0:T(128)} %stack.84.where_ref, bf16[1024,768]{1,0:T(8,128)(2,1)} %tokens_ref.5, ...), custom_call_target="tpu_custom_call" | custom-call | flops 9422084096 | bytes 32715572 | tf_op jit(solution)/shard_map/project/pallas_call | solution.py:285
  70.9 15.0 %attend.1 = (bf16[1024,768]{1,0:T(8,128)(2,1)}, f32[6,2,1024]{2,1,0:T(2,128)}) custom-call(bf16[1024,768]{1,0:T(8,128)(2,1)} %get-tuple-element.79.q_ref, bf16[1024,768]{1,0:T(8,128)(2,1)} %get-tuple-element.80.k_ref, bf16[1024,768]{1,0:T(8,128)(2,1)} %get-tuple-element.81.v_ref), custom_call_target="tpu_custom_call" | custom-call | flops 16750372864 | bytes 16357785 | tf_op jit(solution)/shard_map/attend/pallas_call | solution.py:351
  86.0 12.3 %mix.1 = (bf16[1024,768]{1,0:T(8,128)(2,1)}, bf16[1024,768]{1,0:T(8,128)(2,1)}, f32[8,1024]{1,0:T(8,128)}, f32[16,1024]{1,0:T(8,128)}, bf16[224,768]{1,0:T(8,128...) custom-call(s32[1]{0:T(128)} %bitcast.2.mine_ref, ...), custom_call_target="tpu_custom_call" | custom-call | flops 10468982784 | bytes 36805016 | tf_op jit(solution)/shard_map/mix/pallas_call | solution.py:485
  100.7 8.2 %collective-permute-done.11.refs_3_.refs_2_ = bf16[224,768]{1,0:T(8,128)(2,1)S(1)} collective-permute-done((bf16[224,768]{1,0:T(8,128)(2,1)}, bf16[224,768]{1,0:T(8,128)(2,1)S(1)}, u32[]{:S(2)}, u32[]{:S(2)}) %collective-permute-start.11) | collective-permute-done | bytes 344096 | tf_op jit(solution)/shard_map/ppermute | solution.py:1203
  108.9 7.8 %collective-permute-done.12.refs_4_.refs_3_ = bf16[224,768]{1,0:T(8,128)(2,1)} collective-permute-done((bf16[224,768]{1,0:T(8,128)(2,1)}, bf16[224,768]{1,0:T(8,128)(2,1)}, u32[]{:S(2)}, u32[]{:S(2)}) %collective-permute-start.12) | collective-permute-done | bytes 344096 | tf_op jit(solution)/shard_map/ppermute | solution.py:1203
  119.2 5.2 %all-gather.2.cloned.1.call-done.refs_5_.refs_3_ = bf16[8,3,768,256]{3,2,1,0:T(8,128)(2,1)} async-done(((bf16[2,3,768,256]{3,2,1,0:T(8,128)(2,1)}), bf16[8,3,768,256]{3,2,1,0:T(8,128)(2,1)}) %all-gather.2.cloned.1.call-update) | async-done | bytes 9437200 | tf_op jit(solution)/shard_map/all_gather | solution.py:1238
  124.4 27.4 %expert_rows.3 = (bf16[896,2048]{1,0:T(8,128)(2,1)}, bf16[896,2048]{1,0:T(8,128)(2,1)}, bf16[896,2048]{1,0:T(8,128)(2,1)}, bf16[896,768]{1,0:T(8,128)(2,1)}, bf1...) custom-call(s32[1]{0:T(128)} %bitcast.2.mine_ref, ...), custom_call_target="tpu_custom_call" | custom-call | flops 169114337280 | bytes 204472320 | tf_op jit(solution)/shard_map/expert_rows/pallas_call | solution.py:650
  154.3 3.0 collective-permute-start.15
  157.9 16.9 %expert_rows.4 = (bf16[448,2048]{1,0:T(8,128)(2,1)}, bf16[448,2048]{1,0:T(8,128)(2,1)}, bf16[448,2048]{1,0:T(8,128)(2,1)}, bf16[448,768]{1,0:T(8,128)(2,1)}, bf1...) custom-call(s32[1]{0:T(128)} %bitcast.2.mine_ref, ...), custom_call_target="tpu_custom_call", output_to_operand_aliasing={{4}: (5, {})} | custom-call | flops 84557168640 | bytes 149422080 | tf_op jit(solution)/shard_map/expert_rows/pallas_call | solution.py:650
  179.2 8.0 %collective-permute-done.16.refs_1_.refs_7_ = bf16[224,768]{1,0:T(8,128)(2,1)} collective-permute-done((bf16[224,768]{1,0:T(8,128)(2,1)}, bf16[224,768]{1,0:T(8,128)(2,1)}, u32[]{:S(2)}, u32[]{:S(2)}) %collective-permute-start.16) | collective-permute-done | bytes 344096 | tf_op jit(solution)/shard_map/ppermute | solution.py:1203
  187.2 16.9 %expert_rows.5 = (bf16[448,2048]{1,0:T(8,128)(2,1)}, bf16[448,2048]{1,0:T(8,128)(2,1)}, bf16[448,2048]{1,0:T(8,128)(2,1)}, bf16[448,768]{1,0:T(8,128)(2,1)}, bf1...) custom-call(s32[1]{0:T(128)} %bitcast.2.mine_ref, ...), custom_call_target="tpu_custom_call", output_to_operand_aliasing={{4}: (5, {})} | custom-call | flops 84557168640 | bytes 149422080 | tf_op jit(solution)/shard_map/expert_rows/pallas_call | solution.py:650
  209.2 28.0 %expert_weights.1.refs_1_ = bf16[8,3,768,256]{3,2,1,0:T(8,128)(2,1)} custom-call(bf16[224,768]{1,0:T(8,128)(2,1)} %get-tuple-element.88.refs_0_, bf16[224,768]{1,0:T(8,128)(2,1)} %copy-done.10, bf16[224,768]{1,0:T(8,128)(2,1)} %copy-done.11, bf16[224,768]{1,0:T(8,128)(2,1)} %collective-permute-done.12.refs_4_.refs_3_, ...), custom_call_target="tpu_custom_call" | custom-call | flops 169114336 | bytes 314572 | tf_op jit(solution)/shard_map/expert_weights/pallas_call | solution.py:722
  239.6 18.5 %come_back.1 = (f32[12,1024]{1,0:T(8,128)}, bf16[1024,768]{1,0:T(8,128)(2,1)}, bf16[1024,768]{1,0:T(8,128)(2,1)}, f32[6,2,1024]{2,1,0:T(2,128)}, bf16[4,1,96,896...) custom-call(s32[3]{0:T(128)} %pad_add_fusion.place_ref, s32[1024,8]{1,0:T(8,128)} %get-tuple-element.77.tcol_ref, ...), custom_call_target="tpu_custom_call" | custom-call | flops 157034741760 | bytes 424673280 | tf_op jit(solution)/shard_map/come_back/pallas_call | solution.py:886
  258.1 18.1 %all-to-all-start.1 = ((bf16[8,224,768]{2,1,0:T(8,128)(2,1)}), bf16[8,224,768]{2,1,0:T(8,128)(2,1)S(1)}, u32[]{:S(2)}, u32[]{:S(2)}) async-start(bf16[8,224,768]{2,1,0:T(8,128)(2,1)} %after.24), calls=%async_computation.1 | async-start | bytes 5505024 | tf_op jit(solution)/shard_map/all_to_all | solution.py:1209
  276.3 16.9 %attend_back.2 = (bf16[1024,1152]{1,0:T(8,128)(2,1)}, bf16[4,3,96,384]{3,2,1,0:T(8,128)(2,1)}, bf16[4,3,96,384]{3,2,1,0:T(8,128)(2,1)}) custom-call(s32[3]{0:T(128)} %pad_add_fusion.place_ref, bf16[1024,768]{1,0:T(8,128)(2,1)} %get-tuple-element.79.q_ref, bf16[1024,768]{1,0:T(8,128)(2,1)} %get-tuple-element.80.k_ref, ...), custom_call_target="tpu_custom_call" | custom-call | flops 104689824 | bytes 55050 | tf_op jit(solution)/shard_map/attend_back/pallas_call | solution.py:1030
  301.4 16.7 %attend_back.3 = (bf16[1024,1152]{1,0:T(8,128)(2,1)}, bf16[4,3,96,384]{3,2,1,0:T(8,128)(2,1)}, bf16[4,3,96,384]{3,2,1,0:T(8,128)(2,1)}) custom-call(s32[3]{0:T(128)} %pad_add_fusion.place_ref, bf16[1024,768]{1,0:T(8,128)(2,1)} %get-tuple-element.79.q_ref, bf16[1024,768]{1,0:T(8,128)(2,1)} %get-tuple-element.80.k_ref, ...), custom_call_target="tpu_custom_call" | custom-call | flops 104689824 | bytes 55050 | tf_op jit(solution)/shard_map/attend_back/pallas_call | solution.py:1030
  319.0 7.0 %collective-permute-done.28 = bf16[96,2048]{1,0:T(8,128)(2,1)} collective-permute-done((bf16[96,2048]{1,0:T(8,128)(2,1)}, bf16[96,2048]{1,0:T(8,128)(2,1)}, u32[]{:S(2)}, u32[]{:S(2)}) %collective-permute-start.28) | collective-permute-done | bytes 393248 | tf_op jit(solution)/shard_map/ppermute | solution.py:1206
  326.0 2.6 fusion.13
  331.5 2.3 fusion.8
  339.6 11.0 %tokens_grad.1.refs_1_ = f32[1024,768]{1,0:T(8,128)} custom-call(bf16[1024,1152]{1,0:T(8,128)(2,1)} %get-tuple-element.135.first_ref, bf16[1024,1152]{1,0:T(8,128)(2,1)} %get-tuple-element.134.refs_1_.second_ref, bf16[768,2432]{1,0:T(8,128)(2,1)} %get-tuple-element.136.weight_ref, bf16[1024,768]{1,0:T(8,128)(2,1)} %tokens_ref.5, ...), custom_call_target="tpu_custom_call" | custom-call | flops 36238784 | bytes 125829 | tf_op jit(solution)/shard_map/tokens_grad/pallas_call | solution.py:1082
  361.7 7.9 %output.1.refs_1_ = bf16[1024,768]{1,0:T(8,128)(2,1)} custom-call(s32[1024,8]{1,0:T(8,128)} %get-tuple-element.77.tcol_ref, f32[8,1024]{1,0:T(8,128)} %get-tuple-element.85.gates_ref, f32[16,768]{1,0:T(8,128)} %get-tuple-element.84.small_ref, bf16[1024,768]{1,0:T(8,128)(2,1)} %after.26.residual_ref, bf16[1024,768]{1,0:T(8,128)(2,1)} %get-tuple-element.120.normed_ref, ...), custom_call_target="tpu_custom_call" | custom-call | flops 28185722 | bytes 94371 | tf_op jit(solution)/shard_map/output/pallas_call | solution.py:1119
  375.6 2.8 slice_bitcast_fusion.4
  386.8 9.0 %collective-permute-done.37.high_ref = bf16[96,1152]{1,0:T(8,128)(2,1)S(1)} collective-permute-done((bf16[96,1152]{1,0:T(8,128)(2,1)S(1)}, bf16[96,1152]{1,0:T(8,128)(2,1)S(1)}, u32[]{:S(2)}, u32[]{:S(2)}) %collective-permute-start.37) | collective-permute-done | bytes 221216 | tf_op jit(solution)/shard_map/ppermute | solution.py:1206
  397.1 2.5 finish.1
  (200 shorter events, 83.4 us)
Async XLA Ops:
  7.2 117.2 %all-gather.2.cloned.1.call-start = ((), (), s32[]{:S(2)}) async-start(), calls=%async_computation.3 | async-start | bytes 11796480 | tf_op jit(solution)/shard_map/all_gather | solution.py:1238
  15.5 20.0 %collective-permute-start.2 = (bf16[96,3200]{1,0:T(8,128)(2,1)}, bf16[96,3200]{1,0:T(8,128)(2,1)}, u32[]{:S(2)}, u32[]{:S(2)}) collective-permute-start(bf16[96,3200]{1,0:T(8,128)(2,1)} %fusion.3.rest_0_), channel_id=1, source_target_pairs={{0,4},{2,6},{4,0},{6,2},{1,5},{3,7},{5,1},{7,3},{8,12},{10,14},{12... | collective-permute-start | bytes 1843208 | tf_op jit(solution)/shard_map/ppermute | solution.py:1206
  17.9 20.2 %collective-permute-start = (bf16[96,3200]{1,0:T(8,128)(2,1)}, bf16[96,3200]{1,0:T(8,128)(2,1)S(1)}, u32[]{:S(2)}, u32[]{:S(2)}) collective-permute-start(bf16[96,3200]{1,0:T(8,128)(2,1)} %fusion.3.rest_0_), channel_id=1, source_target_pairs={{0,2},{2,0},{4,6},{6,4},{1,3},{3,1},{5,7},{7,5},{8,10},{10,8},{12,... | collective-permute-start | bytes 1843208 | tf_op jit(solution)/shard_map/ppermute | solution.py:1206
  29.2 90.0 %all-to-all-start = ((bf16[8,224,768]{2,1,0:T(8,128)(2,1)}), bf16[8,224,768]{2,1,0:T(8,128)(2,1)S(1)}, u32[]{:S(2)}, u32[]{:S(2)}) async-start(bf16[8,224,768]{2,1,0:T(8,128)(2,1)} %get-tuple-element.98), calls=%async_computation | async-start | bytes 5505024 | tf_op jit(solution)/shard_map/all_to_all | solution.py:1209
  35.1 340.5 %reduce-scatter.2.cloned.1.call-start = ((), (), s32[]{:S(2)}) async-start(), calls=%async_computation.4 | async-start | bytes 11796480 | tf_op jit(solution)/shard_map/reduce_scatter | solution.py:1313
  35.4 24.9 %collective-permute-start.5 = (bf16[96,3200]{1,0:T(8,128)(2,1)}, bf16[96,3200]{1,0:T(8,128)(2,1)}, u32[]{:S(2)}, u32[]{:S(2)}) collective-permute-start(bf16[96,3200]{1,0:T(8,128)(2,1)} %fusion.3.rest_0_), channel_id=1, source_target_pairs={{0,1},{1,0},{2,3},{3,2},{4,5},{5,4},{6,7},{7,6},{8,9},{9,8},{10,11... | collective-permute-start | bytes 1843208 | tf_op jit(solution)/shard_map/ppermute | solution.py:1206
  37.2 15.4 %collective-permute-start.3 = (bf16[48,3200]{1,0:T(8,128)(2,1)}, bf16[48,3200]{1,0:T(8,128)(2,1)}, u32[]{:S(2)}, u32[]{:S(2)}) collective-permute-start(bf16[48,3200]{1,0:T(8,128)(2,1)} %slice.145), channel_id=1, source_target_pairs={{0,2},{2,0},{4,6},{6,4},{1,3},{3,1},{5,7},{7,5},{8,10},{10,8},{12,... | collective-permute-start | bytes 921608 | tf_op jit(solution)/shard_map/ppermute | solution.py:1206
  39.9 16.0 %collective-permute-start.4 = (bf16[48,3200]{1,0:T(8,128)(2,1)S(1)}, bf16[48,3200]{1,0:T(8,128)(2,1)}, u32[]{:S(2)}, u32[]{:S(2)}) collective-permute-start(bf16[48,3200]{1,0:T(8,128)(2,1)S(1)} %slice.146), channel_id=1, source_target_pairs={{0,4},{2,6},{4,0},{6,2},{1,5},{3,7},{5,1},{7,3},{8,12},{10,14},{12... | collective-permute-start | bytes 921608 | tf_op jit(solution)/shard_map/ppermute | solution.py:1206
  42.2 18.1 %collective-permute-start.7 = (bf16[96,3200]{1,0:T(8,128)(2,1)}, bf16[96,3200]{1,0:T(8,128)(2,1)S(1)}, u32[]{:S(2)}, u32[]{:S(2)}) collective-permute-start(bf16[96,3200]{1,0:T(8,128)(2,1)} %after.17.rest_2_), channel_id=1, source_target_pairs={{0,1},{1,0},{2,3},{3,2},{4,5},{5,4},{6,7},{7,6},{8,9},{9,8},{10,11... | collective-permute-start | bytes 1843208 | tf_op jit(solution)/shard_map/ppermute | solution.py:1206
  45.6 15.6 %collective-permute-start.6 = (bf16[96,3200]{1,0:T(8,128)(2,1)}, bf16[96,3200]{1,0:T(8,128)(2,1)}, u32[]{:S(2)}, u32[]{:S(2)}) collective-permute-start(bf16[96,3200]{1,0:T(8,128)(2,1)} %after.16.rest_1_), channel_id=1, source_target_pairs={{0,1},{1,0},{2,3},{3,2},{4,5},{5,4},{6,7},{7,6},{8,9},{9,8},{10,11... | collective-permute-start | bytes 1843208 | tf_op jit(solution)/shard_map/ppermute | solution.py:1206
  99.9 16.8 %collective-permute-start.12 = (bf16[224,768]{1,0:T(8,128)(2,1)}, bf16[224,768]{1,0:T(8,128)(2,1)}, u32[]{:S(2)}, u32[]{:S(2)}) collective-permute-start(bf16[224,768]{1,0:T(8,128)(2,1)} %get-tuple-element.91), channel_id=1, source_target_pairs={{0,9},{2,11},{4,13},{6,15},{1,8},{3,10},{5,12},{7,14},{8,1},{10,3}... | collective-permute-start | bytes 1032200 | tf_op jit(solution)/shard_map/ppermute | solution.py:1203
  116.7 37.6 %collective-permute-start.13 = (bf16[224,768]{1,0:T(8,128)(2,1)}, bf16[224,768]{1,0:T(8,128)(2,1)}, u32[]{:S(2)}, u32[]{:S(2)}) collective-permute-start(bf16[224,768]{1,0:T(8,128)(2,1)} %get-tuple-element.94), channel_id=1, source_target_pairs={{0,16},{2,18},{4,20},{6,22},{1,17},{3,19},{5,21},{7,23},{8,24},{10... | collective-permute-start | bytes 1032200 | tf_op jit(solution)/shard_map/ppermute | solution.py:1203
  118.9 35.4 %collective-permute-start.14 = (bf16[224,768]{1,0:T(8,128)(2,1)}, bf16[224,768]{1,0:T(8,128)(2,1)}, u32[]{:S(2)}, u32[]{:S(2)}) collective-permute-start(bf16[224,768]{1,0:T(8,128)(2,1)} %get-tuple-element.95), channel_id=1, source_target_pairs={{0,17},{2,19},{4,21},{6,23},{1,16},{3,18},{5,20},{7,22},{8,25},{10... | collective-permute-start | bytes 1032200 | tf_op jit(solution)/shard_map/ppermute | solution.py:1203
  151.8 23.0 %collective-permute-start.17 = (bf16[224,768]{1,0:T(8,128)(2,1)}, bf16[224,768]{1,0:T(8,128)(2,1)S(1)}, u32[]{:S(2)}, u32[]{:S(2)}) collective-permute-start(bf16[224,768]{1,0:T(8,128)(2,1)} %get-tuple-element.105), channel_id=1, source_target_pairs={{0,1},{2,3},{4,5},{6,7},{1,0},{3,2},{5,4},{7,6},{8,9},{10,11},{12,... | collective-permute-start | bytes 1032200 | tf_op jit(solution)/shard_map/ppermute | solution.py:1203
  152.6 22.7 %collective-permute-start.18 = (bf16[224,768]{1,0:T(8,128)(2,1)}, bf16[224,768]{1,0:T(8,128)(2,1)S(1)}, u32[]{:S(2)}, u32[]{:S(2)}) collective-permute-start(bf16[224,768]{1,0:T(8,128)(2,1)} %get-tuple-element.106), channel_id=1, source_target_pairs={{0,8},{2,10},{4,12},{6,14},{1,9},{3,11},{5,13},{7,15},{8,0},{10,2}... | collective-permute-start | bytes 1032200 | tf_op jit(solution)/shard_map/ppermute | solution.py:1203
  153.8 23.7 %collective-permute-start.19 = (bf16[224,768]{1,0:T(8,128)(2,1)}, bf16[224,768]{1,0:T(8,128)(2,1)S(1)}, u32[]{:S(2)}, u32[]{:S(2)}) collective-permute-start(bf16[224,768]{1,0:T(8,128)(2,1)} %get-tuple-element.107), channel_id=1, source_target_pairs={{0,9},{2,11},{4,13},{6,15},{1,8},{3,10},{5,12},{7,14},{8,1},{10,3}... | collective-permute-start | bytes 1032200 | tf_op jit(solution)/shard_map/ppermute | solution.py:1203
  154.3 24.9 %collective-permute-start.15 = (bf16[224,768]{1,0:T(8,128)(2,1)}, bf16[224,768]{1,0:T(8,128)(2,1)}, u32[]{:S(2)}, u32[]{:S(2)}) collective-permute-start(bf16[224,768]{1,0:T(8,128)(2,1)} %get-tuple-element.100), channel_id=1, source_target_pairs={{0,24},{2,26},{4,28},{6,30},{1,25},{3,27},{5,29},{7,31},{8,16},{10... | collective-permute-start | bytes 1032200 | tf_op jit(solution)/shard_map/ppermute | solution.py:1203
  157.4 29.9 %collective-permute-start.16 = (bf16[224,768]{1,0:T(8,128)(2,1)}, bf16[224,768]{1,0:T(8,128)(2,1)}, u32[]{:S(2)}, u32[]{:S(2)}) collective-permute-start(bf16[224,768]{1,0:T(8,128)(2,1)} %get-tuple-element.101), channel_id=1, source_target_pairs={{0,25},{2,27},{4,29},{6,31},{1,24},{3,26},{5,28},{7,30},{8,17},{10... | collective-permute-start | bytes 1032200 | tf_op jit(solution)/shard_map/ppermute | solution.py:1203
  174.9 62.3 %collective-permute-start.20 = (bf16[224,768]{1,0:T(8,128)(2,1)}, bf16[224,768]{1,0:T(8,128)(2,1)S(1)}, u32[]{:S(2)}, u32[]{:S(2)}) collective-permute-start(bf16[224,768]{1,0:T(8,128)(2,1)} %get-tuple-element.118), channel_id=1, source_target_pairs={{0,16},{2,18},{4,20},{6,22},{1,17},{3,19},{5,21},{7,23},{8,24},{10... | collective-permute-start | bytes 1032200 | tf_op jit(solution)/shard_map/ppermute | solution.py:1203
  175.3 62.0 %collective-permute-start.21 = (bf16[224,768]{1,0:T(8,128)(2,1)}, bf16[224,768]{1,0:T(8,128)(2,1)S(1)}, u32[]{:S(2)}, u32[]{:S(2)}) collective-permute-start(bf16[224,768]{1,0:T(8,128)(2,1)} %get-tuple-element.119), channel_id=1, source_target_pairs={{0,17},{2,19},{4,21},{6,23},{1,16},{3,18},{5,20},{7,22},{8,25},{10... | collective-permute-start | bytes 1032200 | tf_op jit(solution)/shard_map/ppermute | solution.py:1203
  204.1 34.6 %collective-permute-start.22 = (bf16[224,768]{1,0:T(8,128)(2,1)}, bf16[224,768]{1,0:T(8,128)(2,1)S(1)}, u32[]{:S(2)}, u32[]{:S(2)}) collective-permute-start(bf16[224,768]{1,0:T(8,128)(2,1)} %get-tuple-element.122), channel_id=1, source_target_pairs={{0,24},{2,26},{4,28},{6,30},{1,25},{3,27},{5,29},{7,31},{8,16},{10... | collective-permute-start | bytes 1032200 | tf_op jit(solution)/shard_map/ppermute | solution.py:1203
  205.3 33.4 %collective-permute-start.23 = (bf16[224,768]{1,0:T(8,128)(2,1)}, bf16[224,768]{1,0:T(8,128)(2,1)S(1)}, u32[]{:S(2)}, u32[]{:S(2)}) collective-permute-start(bf16[224,768]{1,0:T(8,128)(2,1)} %get-tuple-element.123), channel_id=1, source_target_pairs={{0,25},{2,27},{4,29},{6,31},{1,24},{3,26},{5,28},{7,30},{8,17},{10... | collective-permute-start | bytes 1032200 | tf_op jit(solution)/shard_map/ppermute | solution.py:1203
  258.1 97.7 %all-to-all-start.1 = ((bf16[8,224,768]{2,1,0:T(8,128)(2,1)}), bf16[8,224,768]{2,1,0:T(8,128)(2,1)S(1)}, u32[]{:S(2)}, u32[]{:S(2)}) async-start(bf16[8,224,768]{2,1,0:T(8,128)(2,1)} %after.24), calls=%async_computation.1 | async-start | bytes 5505024 | tf_op jit(solution)/shard_map/all_to_all | solution.py:1209
  276.2 17.3 %collective-permute-start.25 = (bf16[4,1,96,896]{3,2,1,0:T(8,128)(2,1)}, bf16[4,1,96,896]{3,2,1,0:T(8,128)(2,1)S(1)}, u32[]{:S(2)}, u32[]{:S(2)}) collective-permute-start(bf16[4,1,96,896]{3,2,1,0:T(8,128)(2,1)} %get-tuple-element.131), channel_id=1, source_target_pairs={{0,1},{1,0},{2,3},{3,2},{4,5},{5,4},{6,7},{7,6},{8,9},{9,8},{10,11... | collective-permute-start | bytes 2064392 | tf_op jit(solution)/shard_map/ppermute | solution.py:1206
  297.0 22.0 %collective-permute-start.26 = (bf16[96,2048]{1,0:T(8,128)(2,1)}, bf16[96,2048]{1,0:T(8,128)(2,1)}, u32[]{:S(2)}, u32[]{:S(2)}) collective-permute-start(bf16[96,2048]{1,0:T(8,128)(2,1)} %pad_maximum_fusion.4), channel_id=1, source_target_pairs={{0,2},{2,0},{4,6},{6,4},{1,3},{3,1},{5,7},{7,5},{8,10},{10,8},{12,... | collective-permute-start | bytes 1179656 | tf_op jit(solution)/shard_map/ppermute | solution.py:1206
  299.0 19.9 %collective-permute-start.27 = (bf16[96,2048]{1,0:T(8,128)(2,1)}, bf16[96,2048]{1,0:T(8,128)(2,1)}, u32[]{:S(2)}, u32[]{:S(2)}) collective-permute-start(bf16[96,2048]{1,0:T(8,128)(2,1)} %pad_maximum_fusion.5), channel_id=1, source_target_pairs={{0,4},{2,6},{4,0},{6,2},{1,5},{3,7},{5,1},{7,3},{8,12},{10,14},{12... | collective-permute-start | bytes 1179656 | tf_op jit(solution)/shard_map/ppermute | solution.py:1206
  299.9 26.2 %collective-permute-start.28 = (bf16[96,2048]{1,0:T(8,128)(2,1)}, bf16[96,2048]{1,0:T(8,128)(2,1)}, u32[]{:S(2)}, u32[]{:S(2)}) collective-permute-start(bf16[96,2048]{1,0:T(8,128)(2,1)} %pad_maximum_fusion.3.refs_1_), channel_id=1, source_target_pairs={{0,6},{2,4},{4,2},{6,0},{1,7},{3,5},{5,3},{7,1},{8,14},{10,12},{12... | collective-permute-start | bytes 1179656 | tf_op jit(solution)/shard_map/ppermute | solution.py:1206
  329.3 21.3 %collective-permute-start.33 = (bf16[96,2048]{1,0:T(8,128)(2,1)S(1)}, bf16[96,2048]{1,0:T(8,128)(2,1)}, u32[]{:S(2)}, u32[]{:S(2)}) collective-permute-start(bf16[96,2048]{1,0:T(8,128)(2,1)S(1)} %get-tuple-element.190.refs_0_), channel_id=1, source_target_pairs={{0,8},{8,0},{16,24},{24,16},{1,9},{9,1},{17,25},{25,17},{2,10},{10... | collective-permute-start | bytes 1179656 | tf_op jit(solution)/shard_map/ppermute | solution.py:1206
  334.6 22.9 %collective-permute-start.32 = (bf16[96,1152]{1,0:T(8,128)(2,1)}, bf16[96,1152]{1,0:T(8,128)(2,1)}, u32[]{:S(2)}, u32[]{:S(2)}) collective-permute-start(bf16[96,1152]{1,0:T(8,128)(2,1)} %bitcast.66.refs_2_), channel_id=1, source_target_pairs={{0,6},{2,4},{4,2},{6,0},{1,7},{3,5},{5,3},{7,1},{8,14},{10,12},{12... | collective-permute-start | bytes 663560 | tf_op jit(solution)/shard_map/ppermute | solution.py:1206
  336.5 21.0 %collective-permute-start.30 = (bf16[96,1152]{1,0:T(8,128)(2,1)}, bf16[96,1152]{1,0:T(8,128)(2,1)}, u32[]{:S(2)}, u32[]{:S(2)}) collective-permute-start(bf16[96,1152]{1,0:T(8,128)(2,1)} %bitcast.68), channel_id=1, source_target_pairs={{0,2},{2,0},{4,6},{6,4},{1,3},{3,1},{5,7},{7,5},{8,10},{10,8},{12,... | collective-permute-start | bytes 663560 | tf_op jit(solution)/shard_map/ppermute | solution.py:1206
  338.4 19.1 %collective-permute-start.31 = (bf16[96,1152]{1,0:T(8,128)(2,1)}, bf16[96,1152]{1,0:T(8,128)(2,1)}, u32[]{:S(2)}, u32[]{:S(2)}) collective-permute-start(bf16[96,1152]{1,0:T(8,128)(2,1)} %bitcast.70), channel_id=1, source_target_pairs={{0,4},{2,6},{4,0},{6,2},{1,5},{3,7},{5,1},{7,3},{8,12},{10,14},{12... | collective-permute-start | bytes 663560 | tf_op jit(solution)/shard_map/ppermute | solution.py:1206
  351.8 19.5 %collective-permute-start.34 = (bf16[96,2048]{1,0:T(8,128)(2,1)S(1)}, bf16[96,2048]{1,0:T(8,128)(2,1)S(1)}, u32[]{:S(2)}, u32[]{:S(2)}) collective-permute-start(bf16[96,2048]{1,0:T(8,128)(2,1)S(1)} %add_convert_fusion.refs_0_), channel_id=1, source_target_pairs={{0,16},{8,24},{16,0},{24,8},{1,17},{9,25},{17,1},{25,9},{2,18},{10... | collective-permute-start | bytes 1179656 | tf_op jit(solution)/shard_map/ppermute | solution.py:1206
  (43 other events, 179.3 us)
Sparse Core Ops, SparseCore 0:
  13.7 110.6 all-gather.1
  237.3 125.0 reduce-scatter.1
